TPU v7x, 128 devices: a whole 4x4x4 slice. The times are simulated.
128 devices in a mesh: pipe: 2 (over core), tensor: 8 (over x_hi, y), dp: 8 (over x_lo, z).
Axes of the slice: x: 4 (x_hi: 2, x_lo: 2; x = x_hi * 2 + x_lo), y: 4, z: 4, core: 2. Of those that a mesh axis runs over, the one named last changes fastest.
Arguments:
- inputs: bfloat16 [6144, 1024], P('dp'), may hold values from -6 to 6
- cotangent: bfloat16 [6144, 1024], P('dp'), may hold values from -6 to 6
- doc_ids: int32 [48, 128], P('dp'), may hold values from 0 to 5, never falling along the last dimension, each value on 1 to 96 neighbouring positions
- qkv_weight: bfloat16 [2, 1024, 3, 1024], P('pipe', None, None, 'tensor'), may hold values from -0.1875 to 0.1875
- qkv_bias: bfloat16 [2, 2, 1024], P('pipe', None, 'tensor'), may hold values from -2 to 2
- out_weight: bfloat16 [2, 1024, 1024], P('pipe', 'tensor'), may hold values from -0.5 to 0.5
- fc1_weight: bfloat16 [2, 1024, 4096], P('pipe', None, 'tensor'), may hold values from -0.1875 to 0.1875
- fc1_bias: bfloat16 [2, 4096], P('pipe', 'tensor'), may hold values from -2 to 2
- fc2_weight: bfloat16 [2, 4096, 1024], P('pipe', 'tensor'), may hold values from -0.09375 to 0.09375
- norm_gains: bfloat16 [2, 2, 1024], P('pipe'), may hold values from 0.5 to 1.5
- shifts: bfloat16 [2, 4, 1024], P('pipe'), may hold values from -2 to 2
Outputs:
- section_outputs: float32 [2, 6144, 1024], P('pipe', 'dp', 'tensor')
- input_grads: float32 [2, 6144, 1024], P('pipe', 'dp', 'tensor')
- grad_qkv: float32 [2, 1024, 3, 1024], P('pipe', 'dp', None, 'tensor')
- grad_qkv_bias: float32 [2, 2, 1024], P('pipe', None, ('tensor', 'dp'))
- grad_out: float32 [2, 1024, 1024], P('pipe', 'tensor', 'dp')
- grad_fc1: float32 [2, 1024, 4096], P('pipe', 'dp', 'tensor')
- grad_fc1_bias: float32 [2, 4096], P('pipe', ('tensor', 'dp'))
- grad_fc2: float32 [2, 4096, 1024], P('pipe', 'tensor', 'dp')
- grad_gains: float32 [2, 2, 1024], P('pipe', None, ('tensor', 'dp'))
- grad_shifts: float32 [2, 4, 1024], P('pipe', None, ('tensor', 'dp'))
Inputs may be any that keep to these rules, and one draw needn't show every extreme that they name: Within each row of doc_ids the numbers never fall; each sequence holds 1 to 96 consecutive tokens, and one of them exactly that many.
All inputs are finite; a program needn't handle non-finite values.
Results may differ from a plain program's by a relative error of at most 0.033.
Values may be sent and summed in bfloat16 or wider, within the bound.
A program may use at most 192 MiB of HBM per device.

v0:
```python
import jax
import jax.numpy as jnp
from jax import lax
from jax.sharding import PartitionSpec as P

HD = 64


EPSILON = 1e-05


def from_behind(array, axis, by):
    devices = lax.axis_size(axis)
    pairs = [(i, i + by) for i in range(devices) if 0 <= i + by < devices]
    return lax.ppermute(array, axis, pairs)


def normalize(hidden, gain_row, offset):
    centre = jnp.mean(hidden, -1, keepdims=True)
    centered = hidden - centre
    variance = jnp.mean(centered * centered, -1, keepdims=True)
    return centered * lax.rsqrt(variance + EPSILON) * gain_row + offset


def gelu_tanh(values):
    return jax.nn.gelu(values, approximate=True)


def visibility(segment):
    positions = jnp.arange(segment.shape[0])
    return (positions[None, :] <= positions[:, None]) & (segment[:, None] == segment[None, :])


def attend(queries, key_rows, values, segment):
    scores = jnp.einsum(
        "qhd,khd->hqk", queries, key_rows, preferred_element_type=jnp.float32
    ) * HD ** (-0.5)
    scores = jnp.where(visibility(segment), scores, -1e30)
    highest = jnp.max(scores, -1, keepdims=True)
    weights = jnp.exp(scores - highest)
    summed = jnp.sum(weights, -1, keepdims=True)
    probability = (weights / summed).astype(jnp.bfloat16)
    mixture = jnp.einsum(
        "hqk,khd->qhd", probability, values, preferred_element_type=jnp.float32
    ).astype(jnp.bfloat16)
    return (mixture, highest + jnp.log(summed))


def attend_back(queries, key_rows, values, segment, log_total, grad_mix):
    scale = HD ** (-0.5)
    scores = (
        jnp.einsum("qhd,khd->hqk", queries, key_rows, preferred_element_type=jnp.float32) * scale
    )
    scores = jnp.where(visibility(segment), scores, -1e30)
    probability = jnp.exp(scores - log_total)
    grad_values = jnp.einsum(
        "hqk,qhd->khd",
        probability.astype(jnp.bfloat16),
        grad_mix,
        preferred_element_type=jnp.float32,
    )
    grad_prob = jnp.einsum("qhd,khd->hqk", grad_mix, values, preferred_element_type=jnp.float32)
    grad_scores = probability * (grad_prob - jnp.sum(probability * grad_prob, -1, keepdims=True))
    grad_scores = grad_scores.astype(jnp.bfloat16)
    grad_queries = (
        jnp.einsum("hqk,khd->qhd", grad_scores, key_rows, preferred_element_type=jnp.float32)
        * scale
    )
    grad_keys = (
        jnp.einsum("hqk,qhd->khd", grad_scores, queries, preferred_element_type=jnp.float32) * scale
    )
    return (grad_queries, grad_keys, grad_values)


def narrow(partial_sum):
    return lax.psum(partial_sum.astype(jnp.bfloat16), "tensor").astype(jnp.float32)


def narrow_grad(partial_sum):
    return lax.psum(partial_sum.astype(jnp.bfloat16), "tensor").astype(jnp.float32)


def split_heads(packed):
    row_count = packed.shape[0]
    local_heads = packed.shape[2] // HD
    return (
        packed[:, 0].reshape(row_count, local_heads, HD),
        packed[:, 1].reshape(row_count, local_heads, HD),
        packed[:, 2].reshape(row_count, local_heads, HD),
    )


def forward_layer(hidden, segment, params):
    (
        qkv_weight,
        qkv_bias,
        out_weight,
        up_projection_weight,
        up_projection_bias,
        down_projection_weight,
        gains,
        shifts,
    ) = params
    head_width = qkv_weight.shape[2]
    normed_all = normalize(hidden, gains[0], shifts[0]).astype(jnp.bfloat16)
    row_count = normed_all.shape[0]
    projected = jnp.einsum(
        "rd,dce->rce", normed_all, qkv_weight, preferred_element_type=jnp.float32
    )
    bias_rows = jnp.stack([qkv_bias[0], jnp.zeros_like(qkv_bias[0]), qkv_bias[1]])
    packed = (projected + bias_rows).astype(jnp.bfloat16)
    queries, key_rows, values = split_heads(packed)
    mixture, log_total = attend(queries, key_rows, values, segment)
    mixture = mixture.reshape(row_count, head_width)
    middle = (
        hidden
        + narrow(jnp.dot(mixture, out_weight, preferred_element_type=jnp.float32))
        + shifts[1]
    )
    wide_two = normalize(middle, gains[1], shifts[2]).astype(jnp.bfloat16)
    input_before_norm = (
        jnp.dot(wide_two, up_projection_weight, preferred_element_type=jnp.float32)
        + up_projection_bias
    )
    activated_hidden = gelu_tanh(input_before_norm).astype(jnp.bfloat16)
    result = (
        middle
        + narrow(
            jnp.dot(activated_hidden, down_projection_weight, preferred_element_type=jnp.float32)
        )
        + shifts[3]
    )
    return (
        result,
        (
            hidden,
            normed_all,
            packed,
            log_total,
            mixture,
            middle,
            wide_two,
            input_before_norm,
            activated_hidden,
        ),
    )


def backward_layer(grad_result, kept, segment, params):
    (
        qkv_weight,
        qkv_bias,
        out_weight,
        up_projection_weight,
        up_projection_bias,
        down_projection_weight,
        gains,
        shifts,
    ) = params
    (
        hidden,
        normed_all,
        packed,
        log_total,
        mixture,
        middle,
        wide_two,
        input_before_norm,
        activated_hidden,
    ) = kept
    row_count = packed.shape[0]
    head_width = packed.shape[2]
    grad_feed = grad_result.astype(jnp.bfloat16)
    grad_down_bias = jnp.sum(grad_feed.astype(jnp.float32), 0)
    grad_down = jnp.einsum(
        "rf,rd->fd", activated_hidden, grad_feed, preferred_element_type=jnp.float32
    )
    grad_active = jnp.einsum(
        "rd,fd->rf", grad_feed, down_projection_weight, preferred_element_type=jnp.float32
    )
    gelu_pull = jax.vjp(gelu_tanh, input_before_norm)[1]
    grad_before = gelu_pull(grad_active)[0].astype(jnp.bfloat16)
    grad_up_bias = jnp.sum(grad_before.astype(jnp.float32), 0)
    grad_up = jnp.einsum("rd,rf->df", wide_two, grad_before, preferred_element_type=jnp.float32)
    grad_normed_two = narrow_grad(
        jnp.einsum(
            "rf,df->rd", grad_before, up_projection_weight, preferred_element_type=jnp.float32
        )
    )
    second_pull = jax.vjp(normalize, middle, gains[1], shifts[2])[1]
    grad_middle_norm, grad_gain_two, grad_shift_two = second_pull(grad_normed_two)
    grad_middle = grad_result + grad_middle_norm
    grad_branch = grad_middle.astype(jnp.bfloat16)
    grad_out_bias = jnp.sum(grad_branch.astype(jnp.float32), 0)
    grad_out_weight = jnp.einsum(
        "rk,rd->kd", mixture, grad_branch, preferred_element_type=jnp.float32
    )
    grad_mixture = jnp.einsum(
        "rd,kd->rk", grad_branch, out_weight, preferred_element_type=jnp.float32
    )
    grad_mixture = grad_mixture.astype(jnp.bfloat16).reshape(row_count, head_width // HD, HD)
    queries, key_rows, values = split_heads(packed)
    grad_queries, grad_keys, grad_values = attend_back(
        queries, key_rows, values, segment, log_total, grad_mixture
    )
    grad_packed = (
        jnp.stack([grad_queries, grad_keys, grad_values], 1)
        .reshape(row_count, 3, head_width)
        .astype(jnp.bfloat16)
    )
    grad_qkv_bias = jnp.sum(grad_packed[:, 0::2].astype(jnp.float32), 0)
    grad_qkv = jnp.einsum(
        "rd,rce->dce", normed_all, grad_packed, preferred_element_type=jnp.float32
    )
    grad_normed = narrow_grad(
        jnp.einsum("rce,dce->rd", grad_packed, qkv_weight, preferred_element_type=jnp.float32)
    )
    first_pull = jax.vjp(normalize, hidden, gains[0], shifts[0])[1]
    grad_hidden_norm, grad_gain_one, grad_shift_one = first_pull(grad_normed)
    grad_hidden = grad_middle + grad_hidden_norm
    grad_gains = jnp.stack([grad_gain_one, grad_gain_two])
    grad_shifts = jnp.stack([grad_shift_one, grad_out_bias, grad_shift_two, grad_down_bias])
    return (
        grad_hidden,
        (
            grad_qkv,
            grad_qkv_bias,
            grad_out_weight,
            grad_up,
            grad_up_bias,
            grad_down,
            grad_gains,
            grad_shifts,
        ),
    )


def shards(
    inputs,
    cotangent,
    doc_ids,
    qkv_weight,
    qkv_bias,
    out_weight,
    fc1_weight,
    fc1_bias,
    fc2_weight,
    norm_gains,
    shifts,
):
    section = lax.axis_index("pipe")
    block_count, row_count = doc_ids.shape
    width = inputs.shape[1]
    layer_params = (
        qkv_weight[0],
        qkv_bias[0].astype(jnp.float32),
        out_weight[0],
        fc1_weight[0],
        fc1_bias[0].astype(jnp.float32),
        fc2_weight[0],
        norm_gains[0].astype(jnp.float32),
        shifts[0].astype(jnp.float32),
    )
    received = jnp.zeros((row_count, width), jnp.float32)
    results = []
    kept_list = []
    for moment in range(block_count + 1):
        first = min(moment, block_count - 1)
        second = max(moment - 1, 0)
        own_rows = inputs[first * row_count : (first + 1) * row_count].astype(jnp.float32)
        entering = jnp.where(section == 0, own_rows, received)
        segment = jnp.where(section == 0, doc_ids[first], doc_ids[second])
        result, kept = forward_layer(entering, segment, layer_params)
        results.append(result)
        kept_list.append((kept, segment))
        if moment < block_count:
            received = from_behind(result.astype(jnp.bfloat16), "pipe", 1).astype(jnp.float32)
    returned = jnp.zeros_like(received)
    totals = None
    input_list = []
    for moment in range(block_count + 1):
        first = min(moment, block_count - 1)
        own_grad = cotangent[first * row_count : (first + 1) * row_count].astype(jnp.float32)
        arriving = jnp.where(section == 1, own_grad, returned)
        chosen = jax.tree.map(
            lambda early, later: jnp.where(section == 0, early, later),
            kept_list[max(moment - 1, 0)],
            kept_list[min(moment + 1, block_count)],
        )
        kept, segment = chosen
        valid = jnp.where(section == 1, moment < block_count, moment >= 1)
        grad_hidden, grads = backward_layer(arriving, kept, segment, layer_params)
        grads = jax.tree.map(lambda value: jnp.where(valid, value, 0.0), grads)
        totals = grads if totals is None else jax.tree.map(jnp.add, totals, grads)
        input_list.append(grad_hidden)
        if moment < block_count:
            returned = from_behind(grad_hidden.astype(jnp.bfloat16), "pipe", -1).astype(jnp.float32)
    section_rows = jnp.stack(
        [
            jnp.where(section == 0, results[position], results[position + 1])
            for position in range(block_count)
        ]
    )
    grad_rows = jnp.stack(
        [
            jnp.where(section == 0, input_list[position + 1], input_list[position])
            for position in range(block_count)
        ]
    )
    grad_qkv, grad_qkv_bias, grad_out, grad_up, grad_up_bias, grad_down, grad_gains, grad_shifts = (
        totals
    )
    share = width // lax.axis_size("tensor")
    start = lax.axis_index("tensor") * share
    section_cols = lax.dynamic_slice_in_dim(section_rows, start, share, 2)
    grad_cols = lax.dynamic_slice_in_dim(grad_rows, start, share, 2)
    grad_gains = lax.dynamic_slice_in_dim(grad_gains, start, share, 1)
    grad_shifts = lax.dynamic_slice_in_dim(grad_shifts, start, share, 1)
    summed = (
        lax.psum_scatter(
            grad_qkv.astype(jnp.bfloat16), "dp", scatter_dimension=0, tiled=True
        ).astype(jnp.float32),
        lax.psum_scatter(
            grad_qkv_bias.astype(jnp.bfloat16), "dp", scatter_dimension=1, tiled=True
        ).astype(jnp.float32),
        lax.psum_scatter(
            grad_out.astype(jnp.bfloat16), "dp", scatter_dimension=1, tiled=True
        ).astype(jnp.float32),
        lax.psum_scatter(
            grad_up.astype(jnp.bfloat16), "dp", scatter_dimension=0, tiled=True
        ).astype(jnp.float32),
        lax.psum_scatter(
            grad_up_bias.astype(jnp.bfloat16), "dp", scatter_dimension=0, tiled=True
        ).astype(jnp.float32),
        lax.psum_scatter(
            grad_down.astype(jnp.bfloat16), "dp", scatter_dimension=1, tiled=True
        ).astype(jnp.float32),
        lax.psum_scatter(
            grad_gains.astype(jnp.bfloat16), "dp", scatter_dimension=1, tiled=True
        ).astype(jnp.float32),
        lax.psum_scatter(
            grad_shifts.astype(jnp.bfloat16), "dp", scatter_dimension=1, tiled=True
        ).astype(jnp.float32),
    )
    section_out = section_cols.reshape(1, -1, section_cols.shape[2])
    grad_in = grad_cols.reshape(1, -1, grad_cols.shape[2])
    return (
        section_out,
        grad_in,
        summed[0][None],
        summed[1][None],
        summed[2][None],
        summed[3][None],
        summed[4][None],
        summed[5][None],
        summed[6][None],
        summed[7][None],
    )


def solution(mesh):
    return jax.shard_map(
        shards,
        mesh=mesh,
        in_specs=(
            P("dp", None),
            P("dp", None),
            P("dp", None),
            P("pipe", None, None, "tensor"),
            P("pipe", None, "tensor"),
            P("pipe", "tensor", None),
            P("pipe", None, "tensor"),
            P("pipe", "tensor"),
            P("pipe", "tensor", None),
            P("pipe", None, None),
            P("pipe", None, None),
        ),
        out_specs=(
            P("pipe", "dp", "tensor"),
            P("pipe", "dp", "tensor"),
            P("pipe", "dp", None, "tensor"),
            P("pipe", None, ("tensor", "dp")),
            P("pipe", "tensor", "dp"),
            P("pipe", "dp", "tensor"),
            P("pipe", ("tensor", "dp")),
            P("pipe", "tensor", "dp"),
            P("pipe", None, ("tensor", "dp")),
            P("pipe", None, ("tensor", "dp")),
        ),
        check_vma=False,
    )
```

profile of v0, /device:TPU:0, one launch (start us, length us, event | category | flops | bytes accessed | tf_op | source)
XLA Modules:
  0.0 2026.9 jit_solution(4716066987465298956)
XLA Ops:
  25.3 80.0 %all-reduce.30.cloned.1.call-done = bf16[128,1024]{1,0:T(8,128)(2,1)} async-done(((bf16[128,1024]{1,0:T(8,128)(2,1)}), bf16[128,1024]{1,0:T(8,128)(2,1)}) %all-reduce.30.cloned.1.call-update) | async-done | bytes 262160 | tf_op jit(solution)/shard_map/psum | solution.py:76
  112.5 81.2 %all-reduce.32.cloned.1.call-done = bf16[128,1024]{1,0:T(8,128)(2,1)} async-done(((bf16[128,1024]{1,0:T(8,128)(2,1)}), bf16[128,1024]{1,0:T(8,128)(2,1)}) %all-reduce.32.cloned.1.call-update) | async-done | bytes 262160 | tf_op jit(solution)/shard_map/psum | solution.py:76
  200.8 2.5 fusion.557
  208.6 80.8 %all-reduce.34.cloned.1.call-done = bf16[128,1024]{1,0:T(8,128)(2,1)} async-done(((bf16[128,1024]{1,0:T(8,128)(2,1)}), bf16[128,1024]{1,0:T(8,128)(2,1)}) %all-reduce.34.cloned.1.call-update) | async-done | bytes 262160 | tf_op jit(solution)/shard_map/psum | solution.py:76
  289.4 2.1 fusion.560
  293.3 2.1 convert_reduce_fusion.34
  295.4 2.9 fusion.346
  300.9 3.0 fusion.309
  303.9 80.6 %all-reduce.62.cloned.1.call-done = (bf16[128,1024]{1,0:T(8,128)(2,1)}, bf16[128,1024]{1,0:T(8,128)(2,1)}) async-done(((bf16[128,1024]{1,0:T(8,128)(2,1)}, bf16[128,1024]{1,0:T(8,128)(2,1)}), (bf16[128,1024]{1,0:T(8,128)(2,1)}, bf16[128,1024]{1,0:T(8,128)(2,1)})) %all-reduce.62.cloned.1.call-update) | async-done | bytes 524304 | tf_op jit(solution)/shard_map/psum | solution.py:76
  401.7 2.2 fusion.1
  410.7 2.6 fusion.282
  413.3 78.1 %all-reduce.60.cloned.1.call-done = (bf16[128,1024]{1,0:T(8,128)(2,1)}, bf16[128,1024]{1,0:T(8,128)(2,1)}) async-done(((bf16[128,1024]{1,0:T(8,128)(2,1)}, bf16[128,1024]{1,0:T(8,128)(2,1)}), (bf16[128,1024]{1,0:T(8,128)(2,1)}, bf16[128,1024]{1,0:T(8,128)(2,1)})) %all-reduce.60.cloned.1.call-update) | async-done | bytes 524304 | tf_op jit(solution)/shard_map/psum | solution.py:76
  493.2 2.1 fusion.129
  495.6 2.1 fusion.556
  507.7 3.0 fusion.363
  510.8 3.0 fusion.307
  513.7 77.9 %all-reduce.58.cloned.1.call-done = (bf16[128,1024]{1,0:T(8,128)(2,1)}, bf16[128,1024]{1,0:T(8,128)(2,1)}) async-done(((bf16[128,1024]{1,0:T(8,128)(2,1)}, bf16[128,1024]{1,0:T(8,128)(2,1)}), (bf16[128,1024]{1,0:T(8,128)(2,1)}, bf16[128,1024]{1,0:T(8,128)(2,1)})) %all-reduce.58.cloned.1.call-update) | async-done | bytes 524304 | tf_op jit(solution)/shard_map/psum | solution.py:76
  603.4 2.3 fusion.2
  605.7 2.7 fusion.280
  622.1 79.9 %all-reduce.56.cloned.1.call-done = (bf16[128,1024]{1,0:T(8,128)(2,1)}, bf16[128,1024]{1,0:T(8,128)(2,1)}) async-done(((bf16[128,1024]{1,0:T(8,128)(2,1)}, bf16[128,1024]{1,0:T(8,128)(2,1)}), (bf16[128,1024]{1,0:T(8,128)(2,1)}, bf16[128,1024]{1,0:T(8,128)(2,1)})) %all-reduce.56.cloned.1.call-update) | async-done | bytes 524304 | tf_op jit(solution)/shard_map/psum | solution.py:76
  711.6 2.2 bitcast_dynamic-update-slice_fusion.5
  723.3 3.1 fusion.361
  728.3 78.5 %all-reduce.54.cloned.1.call-done = (bf16[128,1024]{1,0:T(8,128)(2,1)}, bf16[128,1024]{1,0:T(8,128)(2,1)}) async-done(((bf16[128,1024]{1,0:T(8,128)(2,1)}, bf16[128,1024]{1,0:T(8,128)(2,1)}), (bf16[128,1024]{1,0:T(8,128)(2,1)}, bf16[128,1024]{1,0:T(8,128)(2,1)})) %all-reduce.54.cloned.1.call-update) | async-done | bytes 524304 | tf_op jit(solution)/shard_map/psum | solution.py:76
  821.8 2.3 fusion.3
  824.1 2.6 fusion.278
  841.1 79.8 %all-reduce.52.cloned.1.call-done = (bf16[128,1024]{1,0:T(8,128)(2,1)}, bf16[128,1024]{1,0:T(8,128)(2,1)}) async-done(((bf16[128,1024]{1,0:T(8,128)(2,1)}, bf16[128,1024]{1,0:T(8,128)(2,1)}), (bf16[128,1024]{1,0:T(8,128)(2,1)}, bf16[128,1024]{1,0:T(8,128)(2,1)})) %all-reduce.52.cloned.1.call-update) | async-done | bytes 524304 | tf_op jit(solution)/shard_map/psum | solution.py:76
  920.9 2.1 multiply_reduce_fusion.8
  925.0 2.3 bitcast_dynamic-update-slice_fusion.4
  929.5 2.6 fusion.547
  947.2 80.8 %all-reduce.50.cloned.1.call-done = (bf16[128,1024]{1,0:T(8,128)(2,1)}, bf16[128,1024]{1,0:T(8,128)(2,1)}) async-done(((bf16[128,1024]{1,0:T(8,128)(2,1)}, bf16[128,1024]{1,0:T(8,128)(2,1)}), (bf16[128,1024]{1,0:T(8,128)(2,1)}, bf16[128,1024]{1,0:T(8,128)(2,1)})) %all-reduce.50.cloned.1.call-update) | async-done | bytes 524304 | tf_op jit(solution)/shard_map/psum | solution.py:76
  1043.8 2.3 fusion.4
  1047.6 2.2 convolution_add_fusion.2
  1056.3 2.6 fusion.276
  1059.5 78.8 %all-reduce.48.cloned.1.call-done = (bf16[128,1024]{1,0:T(8,128)(2,1)}, bf16[128,1024]{1,0:T(8,128)(2,1)}) async-done(((bf16[128,1024]{1,0:T(8,128)(2,1)}, bf16[128,1024]{1,0:T(8,128)(2,1)}), (bf16[128,1024]{1,0:T(8,128)(2,1)}, bf16[128,1024]{1,0:T(8,128)(2,1)})) %all-reduce.48.cloned.1.call-update) | async-done | bytes 524304 | tf_op jit(solution)/shard_map/psum | solution.py:76
  1138.3 2.1 multiply_reduce_fusion.6
  1142.5 2.3 bitcast_dynamic-update-slice_fusion.3
  1146.9 2.1 fusion.543
  1159.9 83.8 %all-reduce.46.cloned.1.call-done = (bf16[128,1024]{1,0:T(8,128)(2,1)}, bf16[128,1024]{1,0:T(8,128)(2,1)}) async-done(((bf16[128,1024]{1,0:T(8,128)(2,1)}, bf16[128,1024]{1,0:T(8,128)(2,1)}), (bf16[128,1024]{1,0:T(8,128)(2,1)}, bf16[128,1024]{1,0:T(8,128)(2,1)})) %all-reduce.46.cloned.1.call-update) | async-done | bytes 524304 | tf_op jit(solution)/shard_map/psum | solution.py:76
  1262.7 2.2 fusion.5
  1274.9 2.5 fusion.274
  1277.5 78.3 %all-reduce.44.cloned.1.call-done = (bf16[128,1024]{1,0:T(8,128)(2,1)}, bf16[128,1024]{1,0:T(8,128)(2,1)}) async-done(((bf16[128,1024]{1,0:T(8,128)(2,1)}, bf16[128,1024]{1,0:T(8,128)(2,1)}), (bf16[128,1024]{1,0:T(8,128)(2,1)}, bf16[128,1024]{1,0:T(8,128)(2,1)})) %all-reduce.44.cloned.1.call-update) | async-done | bytes 524304 | tf_op jit(solution)/shard_map/psum | solution.py:76
  1355.8 2.1 multiply_reduce_fusion.4
  1360.0 2.3 bitcast_dynamic-update-slice_fusion.2
  1364.4 2.1 fusion.535
  1378.6 81.9 %all-reduce.36.cloned.1.call-done = bf16[128,1024]{1,0:T(8,128)(2,1)} async-done(((bf16[128,1024]{1,0:T(8,128)(2,1)}), bf16[128,1024]{1,0:T(8,128)(2,1)}) %all-reduce.36.cloned.1.call-update) | async-done | bytes 262160 | tf_op jit(solution)/shard_map/psum | solution.py:80
  1470.9 2.2 fusion.6
  1474.7 81.2 %all-reduce.38.cloned.1.call-done = bf16[128,1024]{1,0:T(8,128)(2,1)} async-done(((bf16[128,1024]{1,0:T(8,128)(2,1)}), bf16[128,1024]{1,0:T(8,128)(2,1)}) %all-reduce.38.cloned.1.call-update) | async-done | bytes 262160 | tf_op jit(solution)/shard_map/psum | solution.py:80
  1555.9 2.1 multiply_reduce_fusion.2
  1560.1 2.6 bitcast_dynamic-update-slice_fusion.1
  1571.6 2.1 convolution_add_fusion
  1573.7 79.1 %all-reduce.40.cloned.1.call-done = bf16[128,1024]{1,0:T(8,128)(2,1)} async-done(((bf16[128,1024]{1,0:T(8,128)(2,1)}), bf16[128,1024]{1,0:T(8,128)(2,1)}) %all-reduce.40.cloned.1.call-update) | async-done | bytes 262160 | tf_op jit(solution)/shard_map/psum | solution.py:80
  1664.8 79.6 %all-reduce.42.cloned.1.call-done = (bf16[128,1024]{1,0:T(8,128)(2,1)}, bf16[128,1024]{1,0:T(8,128)(2,1)}) async-done(((bf16[128,1024]{1,0:T(8,128)(2,1)}, bf16[128,1024]{1,0:T(8,128)(2,1)}), (bf16[128,1024]{1,0:T(8,128)(2,1)}, bf16[128,1024]{1,0:T(8,128)(2,1)})) %all-reduce.42.cloned.1.call-update) | async-done | bytes 524304 | tf_op jit(solution)/shard_map/psum | solution.py:76
  1751.0 4.9 add_convert_fusion.2
  1763.6 2.3 copy.193
  1767.0 2.9 fusion.301
  1772.9 18.9 all-reduce
  1792.4 6.0 add_convert_fusion.1
  1799.8 21.1 %reduce-scatter.24.cloned.1.call-done = bf16[128,128]{1,0:T(8,128)(2,1)} async-done(((bf16[1024,128]{1,0:T(8,128)(2,1)}), bf16[128,128]{1,0:T(8,128)(2,1)}) %reduce-scatter.24.cloned.1.call-update) | async-done | bytes 32784
  1821.9 2.3 bitcast_dynamic-update-slice_fusion
  1829.3 30.2 %reduce-scatter.28.cloned.1.call-done = bf16[16,2]{1,0:T(8,128)(2,1)} async-done(((bf16[128,2]{1,0:T(8,128)(2,1)}), bf16[16,2]{1,0:T(8,128)(2,1)}) %reduce-scatter.28.cloned.1.call-update) | async-done | bytes 80
  1860.9 36.7 %reduce-scatter.30.cloned.1.call-done = bf16[16,4]{1,0:T(8,128)(2,1)} async-done(((bf16[128,4]{1,0:T(8,128)(2,1)}), bf16[16,4]{1,0:T(8,128)(2,1)}) %reduce-scatter.30.cloned.1.call-update) | async-done | bytes 144
  1899.0 38.4 %reduce-scatter.18.cloned.1.call-done = bf16[128,3,128]{2,0,1:T(8,128)(2,1)} async-done(((bf16[1024,3,128]{2,0,1:T(8,128)(2,1)}), bf16[128,3,128]{2,0,1:T(8,128)(2,1)}) %reduce-scatter.18.cloned.1.call-update) | async-done | bytes 98320 | tf_op jit(solution)/shard_map/reduce_scatter | solution.py:320
  1939.0 38.8 %reduce-scatter.26.cloned.1.call-done = bf16[128,512]{1,0:T(8,128)(2,1)} async-done(((bf16[1024,512]{1,0:T(8,128)(2,1)}), bf16[128,512]{1,0:T(8,128)(2,1)}) %reduce-scatter.26.cloned.1.call-update) | async-done | bytes 131088
  1979.5 38.5 %reduce-scatter.20.cloned.1.call-done = bf16[128,512]{1,0:T(8,128)(2,1)} async-done(((bf16[1024,512]{1,0:T(8,128)(2,1)}), bf16[128,512]{1,0:T(8,128)(2,1)}) %reduce-scatter.20.cloned.1.call-update) | async-done | bytes 131088 | tf_op jit(solution)/shard_map/reduce_scatter | solution.py:329
  (1213 shorter events, 322.1 us)
Async XLA Ops:
  7.2 102.8 %copy-start = (bf16[1,512,1024]{2,1,0:T(8,128)(2,1)S(1)}, bf16[1,512,1024]{2,1,0:T(8,128)(2,1)}, u32[]{:S(2)}) copy-start(bf16[1,512,1024]{2,1,0:T(8,128)(2,1)} %param.19) | copy-start | bytes 3145732
  7.2 98.1 %all-reduce.30.cloned.1.call-start = ((), (), s32[]{:S(2)}) async-start(), calls=%async_computation.7 | async-start | bytes 524288 | tf_op jit(solution)/shard_map/psum | solution.py:76
  14.9 189.5 %copy-start.16 = (bf16[1024,3,128]{0,2,1:T(8,128)(2,1)}, bf16[1024,3,128]{0,2,1:T(8,128)(2,1)S(1)}, u32[]{:S(2)}) copy-start(bf16[1024,3,128]{0,2,1:T(8,128)(2,1)S(1)} %copy.84) | copy-start | bytes 2359300
  16.6 91.1 %copy-start.142 = (f32[128,384]{0,1}, f32[128,384]{0,1:S(1)}, u32[]{:S(2)}) copy-start(f32[128,384]{0,1:S(1)} %fusion.518) | copy-start | bytes 589828
  16.8 91.0 %copy-start.1 = (bf16[1,1024,512]{2,1,0:T(8,128)(2,1)S(1)}, bf16[1,1024,512]{2,1,0:T(8,128)(2,1)}, u32[]{:S(2)}) copy-start(bf16[1,1024,512]{2,1,0:T(8,128)(2,1)} %param.17) | copy-start | bytes 3145732
  17.0 92.3 %copy-start.273 = (f32[2,128]{1,0:T(2,128)}, f32[2,128]{1,0:T(2,128)S(1)}, u32[]{:S(2)}) copy-start(f32[2,128]{1,0:T(2,128)S(1)} %get-tuple-element.293) | copy-start | bytes 3076
  17.3 90.6 %copy-start.192 = (bf16[2,64,128]{2,1,0:T(8,128)(2,1)}, bf16[2,64,128]{2,1,0:T(8,128)(2,1)S(1)}, u32[]{:S(2)}) copy-start(bf16[2,64,128]{2,1,0:T(8,128)(2,1)S(1)} %convolution_convert_fusion.34) | copy-start | bytes 98308
  18.3 175.5 %all-reduce.32.cloned.1.call-start = ((), (), s32[]{:S(2)}) async-start(), calls=%async_computation.8 | async-start | bytes 524288 | tf_op jit(solution)/shard_map/psum | solution.py:76
  107.8 85.9 %copy-start.23 = (bf16[128,1024]{1,0:T(8,128)(2,1)S(1)}, bf16[128,1024]{1,0:T(8,128)(2,1)}, u32[]{:S(2)}) copy-start(bf16[128,1024]{1,0:T(8,128)(2,1)} %all-reduce.30.cloned.1.call-done) | copy-start | bytes 786436
  110.0 86.9 %copy-start.352 = (s32[128]{0:T(128)S(1)}, s32[128]{0:T(128)}, u32[]{:S(2)}) copy-start(s32[128]{0:T(128)} %get-tuple-element.260) | copy-start | bytes 1540
  110.0 87.6 %copy-start.364 = (u32[128]{0:T(128)S(1)}, u32[128]{0:T(128)}, u32[]{:S(2)}) copy-start(u32[128]{0:T(128)} %constant.151) | copy-start | bytes 1540
  111.1 178.3 %all-reduce.34.cloned.1.call-start = ((), (), s32[]{:S(2)}) async-start(), calls=%async_computation.9 | async-start | bytes 524288 | tf_op jit(solution)/shard_map/psum | solution.py:76
  195.6 4.0 collective-permute-start
  206.7 177.8 %all-reduce.62.cloned.1.call-start = ((), (), s32[]{:S(2)}) async-start(), calls=%async_computation.30 | async-start | bytes 1048576 | tf_op jit(solution)/shard_map/psum | solution.py:76
  291.5 318.5 %copy-start.12 = (f32[128,1024]{1,0:T(8,128)}, f32[128,1024]{1,0:T(8,128)S(1)}, u32[]{:S(2)}) copy-start(f32[128,1024]{1,0:T(8,128)S(1)} %get-tuple-element.195) | copy-start | bytes 1572868
  300.8 190.5 %all-reduce.60.cloned.1.call-start = ((), (), s32[]{:S(2)}) async-start(), calls=%async_computation.29 | async-start | bytes 1048576 | tf_op jit(solution)/shard_map/psum | solution.py:76
  391.3 2.6 collective-permute-start.1
  407.6 184.1 %all-reduce.58.cloned.1.call-start = ((), (), s32[]{:S(2)}) async-start(), calls=%async_computation.28 | async-start | bytes 1048576 | tf_op jit(solution)/shard_map/psum | solution.py:76
  498.8 3.4 collective-permute-start.6
  507.6 194.4 %all-reduce.56.cloned.1.call-start = ((), (), s32[]{:S(2)}) async-start(), calls=%async_computation.27 | async-start | bytes 1048576 | tf_op jit(solution)/shard_map/psum | solution.py:76
  608.5 4.1 collective-permute-start.2
  614.8 87.2 %copy-start.32 = (f32[128,1024]{1,0:T(8,128)S(1)}, f32[128,1024]{1,0:T(8,128)}, u32[]{:S(2)}) copy-start(f32[128,1024]{1,0:T(8,128)} %get-tuple-element.177) | copy-start | bytes 1572868
  618.3 188.6 %all-reduce.54.cloned.1.call-start = ((), (), s32[]{:S(2)}) async-start(), calls=%async_computation.26 | async-start | bytes 1048576 | tf_op jit(solution)/shard_map/psum | solution.py:76
  713.8 3.6 collective-permute-start.7
  722.8 198.1 %all-reduce.52.cloned.1.call-start = ((), (), s32[]{:S(2)}) async-start(), calls=%async_computation.25 | async-start | bytes 1048576 | tf_op jit(solution)/shard_map/psum | solution.py:76
  826.8 4.0 collective-permute-start.3
  837.2 190.9 %all-reduce.50.cloned.1.call-start = ((), (), s32[]{:S(2)}) async-start(), calls=%async_computation.24 | async-start | bytes 1048576 | tf_op jit(solution)/shard_map/psum | solution.py:76
  928.2 10.0 collective-permute-start.8
  942.9 195.4 %all-reduce.48.cloned.1.call-start = ((), (), s32[]{:S(2)}) async-start(), calls=%async_computation.23 | async-start | bytes 1048576 | tf_op jit(solution)/shard_map/psum | solution.py:76
  1042.4 7.4 collective-permute-start.4
  1054.6 189.1 %all-reduce.46.cloned.1.call-start = ((), (), s32[]{:S(2)}) async-start(), calls=%async_computation.22 | async-start | bytes 1048576 | tf_op jit(solution)/shard_map/psum | solution.py:76
  1145.6 8.3 collective-permute-start.9
  1158.6 197.2 %all-reduce.44.cloned.1.call-start = ((), (), s32[]{:S(2)}) async-start(), calls=%async_computation.21 | async-start | bytes 1048576 | tf_op jit(solution)/shard_map/psum | solution.py:76
  1249.6 2.6 collective-permute-start.5
  1272.0 188.4 %all-reduce.36.cloned.1.call-start = ((), (), s32[]{:S(2)}) async-start(), calls=%async_computation.10 | async-start | bytes 524288 | tf_op jit(solution)/shard_map/psum | solution.py:80
  1274.9 85.0 %copy-start.346 = (f32[128]{0:T(128)S(1)}, f32[128]{0:T(128)}, u32[]{:S(2)}) copy-start(f32[128]{0:T(128)} %copy-done.345) | copy-start | bytes 1540
  1363.1 8.6 collective-permute-start.10
  1376.5 179.4 %all-reduce.38.cloned.1.call-start = ((), (), s32[]{:S(2)}) async-start(), calls=%async_computation.11 | async-start | bytes 524288 | tf_op jit(solution)/shard_map/psum | solution.py:80
  1470.9 89.1 %copy-start.310 = (f32[128]{0:T(128)S(1)}, f32[128]{0:T(128)}, u32[]{:S(2)}) copy-start(f32[128]{0:T(128)} %broadcast_multiply_fusion.2) | copy-start | bytes 1540
  1470.9 89.1 %copy-start.351 = (f32[128]{0:T(128)S(1)}, f32[128]{0:T(128)}, u32[]{:S(2)}) copy-start(f32[128]{0:T(128)} %copy-done.350) | copy-start | bytes 1540
  1473.2 179.6 %all-reduce.40.cloned.1.call-start = ((), (), s32[]{:S(2)}) async-start(), calls=%async_computation.12 | async-start | bytes 524288 | tf_op jit(solution)/shard_map/psum | solution.py:80
  1562.7 3.6 collective-permute-start.11
  1570.0 84.6 %copy-start.361 = (f32[128]{0:T(128)S(1)}, f32[128]{0:T(128)}, u32[]{:S(2)}) copy-start(f32[128]{0:T(128)} %multiply_reduce_fusion.1) | copy-start | bytes 1540
  1570.0 174.4 %all-reduce.42.cloned.1.call-start = ((), (), s32[]{:S(2)}) async-start(), calls=%async_computation.20 | async-start | bytes 1048576 | tf_op jit(solution)/shard_map/psum | solution.py:76
  1660.8 137.7 %reduce-scatter.22.cloned.1.call-start = ((), (), s32[]{:S(2)}) async-start(), calls=%async_computation.15 | async-start | bytes 36864
  1662.4 158.5 %reduce-scatter.24.cloned.1.call-start = ((), (), s32[]{:S(2)}) async-start(), calls=%async_computation.16 | async-start | bytes 294912
  1663.7 85.4 %copy-start.236 = (f32[1024]{0:T(1024)S(1)}, f32[1024]{0:T(1024)}, u32[]{:S(2)}) copy-start(f32[1024]{0:T(1024)} %get-tuple-element.96) | copy-start | bytes 12292
  1663.7 85.4 %copy-start.237 = (f32[1024]{0:T(1024)S(1)}, f32[1024]{0:T(1024)}, u32[]{:S(2)}) copy-start(f32[1024]{0:T(1024)} %get-tuple-element.100) | copy-start | bytes 12292
  1663.7 85.4 %copy-start.238 = (f32[1024]{0:T(1024)S(1)}, f32[1024]{0:T(1024)}, u32[]{:S(2)}) copy-start(f32[1024]{0:T(1024)} %get-tuple-element.62) | copy-start | bytes 12292
  1663.8 85.4 %copy-start.239 = (f32[1024]{0:T(1024)S(1)}, f32[1024]{0:T(1024)}, u32[]{:S(2)}) copy-start(f32[1024]{0:T(1024)} %get-tuple-element.98) | copy-start | bytes 12292
  1663.8 85.4 %copy-start.240 = (f32[1024]{0:T(1024)S(1)}, f32[1024]{0:T(1024)}, u32[]{:S(2)}) copy-start(f32[1024]{0:T(1024)} %get-tuple-element.55) | copy-start | bytes 12292
  1663.8 85.4 %copy-start.241 = (f32[1024]{0:T(1024)S(1)}, f32[1024]{0:T(1024)}, u32[]{:S(2)}) copy-start(f32[1024]{0:T(1024)} %get-tuple-element.104) | copy-start | bytes 12292
  1663.8 85.4 %copy-start.242 = (f32[1024]{0:T(1024)S(1)}, f32[1024]{0:T(1024)}, u32[]{:S(2)}) copy-start(f32[1024]{0:T(1024)} %get-tuple-element.63) | copy-start | bytes 12292
  1663.8 85.4 %copy-start.243 = (f32[1024]{0:T(1024)S(1)}, f32[1024]{0:T(1024)}, u32[]{:S(2)}) copy-start(f32[1024]{0:T(1024)} %get-tuple-element.102) | copy-start | bytes 12292
  1663.8 87.1 %copy-start.90 = (bf16[128,1024]{1,0:T(8,128)(2,1)S(1)}, bf16[128,1024]{1,0:T(8,128)(2,1)}, u32[]{:S(2)}) copy-start(bf16[128,1024]{1,0:T(8,128)(2,1)} %copy-done.89) | copy-start | bytes 786436
  1663.8 87.1 %copy-start.96 = (bf16[128,1024]{1,0:T(8,128)(2,1)S(1)}, bf16[128,1024]{1,0:T(8,128)(2,1)}, u32[]{:S(2)}) copy-start(bf16[128,1024]{1,0:T(8,128)(2,1)} %copy-done.94) | copy-start | bytes 786436
  1664.7 84.5 %copy-start.245 = (f32[1024]{0:T(1024)S(1)}, f32[1024]{0:T(1024)}, u32[]{:S(2)}) copy-start(f32[1024]{0:T(1024)} %get-tuple-element.56) | copy-start | bytes 12292
  1664.7 84.5 %copy-start.247 = (f32[1024]{0:T(1024)S(1)}, f32[1024]{0:T(1024)}, u32[]{:S(2)}) copy-start(f32[1024]{0:T(1024)} %get-tuple-element.108) | copy-start | bytes 12292
  1664.7 84.5 %copy-start.248 = (f32[1024]{0:T(1024)S(1)}, f32[1024]{0:T(1024)}, u32[]{:S(2)}) copy-start(f32[1024]{0:T(1024)} %get-tuple-element.64) | copy-start | bytes 12292
  1664.8 194.8 %reduce-scatter.28.cloned.1.call-start = ((), (), s32[]{:S(2)}) async-start(), calls=%async_computation.18 | async-start | bytes 36864
  1749.1 148.5 %reduce-scatter.30.cloned.1.call-start = ((), (), s32[]{:S(2)}) async-start(), calls=%async_computation.19 | async-start | bytes 36864
  1750.9 186.5 %reduce-scatter.18.cloned.1.call-start = ((), (), s32[]{:S(2)}) async-start(), calls=%async_computation.13 | async-start | bytes 884736 | tf_op jit(solution)/shard_map/reduce_scatter | solution.py:320
  1755.9 221.8 %reduce-scatter.26.cloned.1.call-start = ((), (), s32[]{:S(2)}) async-start(), calls=%async_computation.17 | async-start | bytes 1179648
  1766.0 252.1 %reduce-scatter.20.cloned.1.call-start = ((), (), s32[]{:S(2)}) async-start(), calls=%async_computation.14 | async-start | bytes 1179648 | tf_op jit(solution)/shard_map/reduce_scatter | solution.py:329
  (337 other events, 2509.0 us)
Sparse Core Ops, SparseCore 0:
  18.4 86.8 all-reduce.29
  111.2 82.4 all-reduce.31
  206.9 82.4 all-reduce.33
  300.9 83.5 all-reduce.61
  407.7 83.5 all-reduce.59
  507.7 83.8 all-reduce.57
  618.4 83.5 all-reduce.55
  722.9 83.8 all-reduce.53
  837.3 83.5 all-reduce.51
  943.0 84.9 all-reduce.49
  1054.7 83.5 all-reduce.47
  1158.7 84.9 all-reduce.45
  1272.1 83.5 all-reduce.43
  1376.6 83.7 all-reduce.35
  1473.3 82.5 all-reduce.37
  1570.2 82.6 all-reduce.39
  1660.9 83.5 all-reduce.41
  1747.4 35.0 reduce-scatter.21
  1784.8 36.0 reduce-scatter.23
  1823.8 35.7 reduce-scatter.27
  1861.9 35.6 reduce-scatter.29
  1900.2 37.1 reduce-scatter.17
  1939.8 37.9 reduce-scatter.25
  1980.0 37.9 reduce-scatter.19
where the time goes:
time: 2040 us; the launch traced here: 2030 us
  waiting for transfers between devices  1570 us (77%)
  other arithmetic  202 us (10%)
  matrix products  140 us (7%)
  local copies, waits for them, and re-layouts  62.9 us (3%)
    psum x14, waiting for transfers between devices, narrow(): lax.psum(partial_sum.astype(jnp.bfloat16), 'tensor').astype(jnp.float32)  1120 us
    psum x3, waiting for transfers between devices, narrow_grad(): lax.psum(partial_sum.astype(jnp.bfloat16), 'tensor').astype(jnp.float32)  242 us
    unnamed x29, waiting for transfers between devices  127 us
  transfers between devices with their start and end apart: 36, of which 26 were waited for; matrix products, arithmetic and copies ran while one was open for 8% of the time, Pallas kernels for 0%

commit v1 on v0

v1 whole, which is shorter than its diff:
```python
import functools

import jax
import jax.numpy as jnp
from jax import lax
from jax.experimental import pallas as pl
from jax.experimental.pallas import tpu as pltpu
from jax.sharding import PartitionSpec as P

MESH = pl.DeviceIdType.MESH
F32 = jnp.float32
BF16 = jnp.bfloat16
EPSILON = 1e-05
HD = 64
SCALE = HD**-0.5
D = 1024
ROWS = 128
T = 8
OWN = ROWS // T
GELU_C = 0.7978845608028654
GELU_A = 0.044715


def mm(a, b):
    return lax.dot_general(a, b, (((1,), (0,)), ((), ())), preferred_element_type=F32)


def mm_nt(a, b):
    return lax.dot_general(a, b, (((1,), (1,)), ((), ())), preferred_element_type=F32)


def mm_tn(a, b):
    return lax.dot_general(a, b, (((0,), (0,)), ((), ())), preferred_element_type=F32)


def standardize(rows):
    centered = rows - jnp.mean(rows, -1, keepdims=True)
    variance = jnp.mean(centered * centered, -1, keepdims=True)
    root = lax.rsqrt(variance + EPSILON)
    return centered * root, root


def norm_back(rows, gain, grad):
    unit, root = standardize(rows)
    e = grad * gain
    slope = root * (
        e - jnp.mean(e, -1, keepdims=True) - unit * jnp.mean(e * unit, -1, keepdims=True)
    )
    return slope, jnp.sum(grad * unit, 0, keepdims=True), jnp.sum(grad, 0, keepdims=True)


def kernel(
    chunks,
    x_ref,
    ct_ref,
    mask_ref,
    wqkv_in,
    wout_in,
    w1_in,
    w2_in,
    vec_in,
    sec_ref,
    ing_ref,
    gqkv_ref,
    gout_ref,
    g1_ref,
    g2_ref,
    gsmall_ref,
    gbias_ref,
    wqkv,
    wout,
    w1,
    w2,
    vec,
    n1,
    n2,
    dmr,
    dyr,
    qkv,
    mix,
    prob,
    up,
    act,
    dup,
    dqkv,
    hrow,
    mrow,
    part,
    rs,
    ostage,
    obuf,
    wsem,
    wsend,
    rsem,
    rsend,
    gsem,
    gsend,
    osem,
    osend,
):
    c = lax.axis_index("pipe")
    t = lax.axis_index("tensor")
    d = lax.axis_index("dp")

    barrier = pltpu.get_barrier_semaphore()
    for j in range(T):
        other = lax.rem(t + j, T)
        if j:
            pl.semaphore_signal(barrier, inc=1, device_id=(c, other, d), device_id_type=MESH)
        pl.semaphore_signal(barrier, inc=1, device_id=(1 - c, other, d), device_id_type=MESH)
    pl.semaphore_wait(barrier, 2 * T - 1)

    weights = ((vec_in, vec), (wqkv_in, wqkv), (wout_in, wout), (w1_in, w1), (w2_in, w2))
    for i, (own, both) in enumerate(weights):
        pltpu.make_async_copy(own, both.at[c], wsem.at[i, c]).start()
        pltpu.make_async_remote_copy(
            src_ref=own,
            dst_ref=both.at[c],
            send_sem=wsend.at[i],
            recv_sem=wsem.at[i, c],
            device_id=(1 - c, t, d),
            device_id_type=MESH,
        ).start()

    def need(i, layer):
        both = weights[i][1]
        pltpu.make_async_copy(both.at[layer], both.at[layer], wsem.at[i, layer]).wait()

    def span(k):
        return pl.ds(pl.multiple_of(k * ROWS, ROWS), ROWS)

    def mine(k, who):
        return pl.ds(pl.multiple_of(k * ROWS + who * OWN, OWN), OWN)

    def scatter_start(ph, k):
        for j in range(1, T):
            other = lax.rem(t + j, T)
            pltpu.make_async_remote_copy(
                src_ref=part.at[ph, mine(k, other)],
                dst_ref=rs.at[ph, k, j - 1],
                send_sem=rsend.at[ph],
                recv_sem=rsem.at[ph, k],
                device_id=(c, other, d),
                device_id_type=MESH,
            ).start()

    def scatter_finish(ph, k):
        pltpu.make_async_copy(rs.at[ph, k], rs.at[ph, k], rsem.at[ph, k]).wait()
        total = part[ph, mine(k, t)].astype(F32)
        for j in range(T - 1):
            total = total + rs[ph, k, j].astype(F32)
        return total

    def gather_start(which, buf, layer, k):
        for j in range(1, T):
            other = lax.rem(t + j, T)
            pltpu.make_async_remote_copy(
                src_ref=buf.at[layer, mine(k, t)],
                dst_ref=buf.at[layer, mine(k, t)],
                send_sem=gsend.at[which, layer],
                recv_sem=gsem.at[which, layer, k],
                device_id=(c, other, d),
                device_id_type=MESH,
            ).start()

    def gather_wait(which, buf, layer, k):
        view = buf.at[layer, pl.ds(0, (T - 1) * OWN)]
        pltpu.make_async_copy(view, view, gsem.at[which, layer, k]).wait()

    def emit(kind, layer, k, rows):
        low = rows.astype(BF16)
        for j in range(T):
            ostage[kind, layer, k, j] = low[:, j * 128 : (j + 1) * 128]
        target = pl.ds(pl.multiple_of(c * (chunks * ROWS) + k * ROWS + t * OWN, OWN), OWN)

        def remote(j):
            other = lax.rem(t + j, T)
            pltpu.make_async_remote_copy(
                src_ref=ostage.at[kind, layer, k, other],
                dst_ref=obuf.at[kind, target],
                send_sem=osend.at[kind, layer],
                recv_sem=osem.at[kind],
                device_id=(layer, other, d),
                device_id_type=MESH,
            ).start()

        for j in range(1, T):
            remote(j)

        @pl.when(c == layer)
        def _():
            pltpu.make_async_copy(
                ostage.at[kind, layer, k, t], obuf.at[kind, target], osem.at[kind]
            ).start()

        @pl.when(c != layer)
        def _():
            remote(0)

    left_half = lax.broadcasted_iota(jnp.int32, (ROWS, 128), 1) < HD

    def heads(value):
        zero = jnp.zeros_like(value)
        return jnp.where(left_half, value, zero), jnp.where(left_half, zero, value)

    def each(count, body):
        def step(i, carry):
            body(i)
            return carry

        lax.fori_loop(0, count, step, 0)

    def forward(layer):
        ph = layer * 2

        @pl.when(layer == 0)
        def _():
            need(0, 0)
            need(1, 0)
            gain = vec[0, 0:1]
            offset = vec[0, 2:3]

            def start(k):
                unit, _ = standardize(x_ref[span(k)].astype(F32))
                n1[0, span(k)] = (unit * gain + offset).astype(BF16)
                hrow[0, k] = x_ref[mine(k, t)].astype(F32)

            each(chunks, start)
            need(2, 0)

        @pl.when(layer == 1)
        def _():
            need(2, 1)

        def attention(k):
            @pl.when(layer == 1)
            def _():
                gather_wait(0, n1, 1, k)

            packed = mm(n1[layer, span(k)], wqkv[layer]) + vec[layer, 6:7, 0:384]
            packed = packed.astype(BF16)
            qkv[layer, span(k)] = packed
            queries, keys, values = packed[:, 0:128], packed[:, 128:256], packed[:, 256:384]
            visible = mask_ref[span(k)] > 0
            parts = []
            for head, query in enumerate(heads(queries)):
                scores = jnp.where(visible, mm_nt(query, keys) * SCALE, -1e30)
                weights_ = jnp.exp(scores - jnp.max(scores, -1, keepdims=True))
                p = weights_ / jnp.sum(weights_, -1, keepdims=True)
                prob[layer, k, head] = p
                parts.append(mm(p.astype(BF16), values))
            mixture = jnp.where(left_half, parts[0], parts[1]).astype(BF16)
            mix[layer, span(k)] = mixture
            part[ph, span(k)] = mm(mixture, wout[layer]).astype(BF16)
            scatter_start(ph, k)

        each(chunks, attention)

        def second_norm(k):
            rows = hrow[layer, k] + scatter_finish(ph, k) + vec[layer, 3:4]
            mrow[layer, k] = rows
            unit, _ = standardize(rows)
            n2[layer, mine(k, t)] = (unit * vec[layer, 1:2] + vec[layer, 4:5]).astype(BF16)
            gather_start(1, n2, layer, k)

        each(chunks, second_norm)
        need(3, layer)
        need(4, layer)

        def feed(k):
            gather_wait(1, n2, layer, k)
            u = mm(n2[layer, span(k)], w1[layer]) + vec[layer, 7:8, 0:512]
            up[layer, span(k)] = u
            g = 0.5 * u * (1.0 + jnp.tanh(GELU_C * (u + GELU_A * (u * u * u))))
            g = g.astype(BF16)
            act[layer, span(k)] = g
            part[ph + 1, span(k)] = mm(g, w2[layer]).astype(BF16)
            scatter_start(ph + 1, k)

        each(chunks, feed)

        @pl.when(layer == 0)
        def _():
            need(0, 1)
            need(1, 1)

        def finish(k):
            rows = mrow[layer, k] + scatter_finish(ph + 1, k) + vec[layer, 5:6]

            @pl.when(layer == 0)
            def _():
                entering = rows.astype(BF16).astype(F32)
                hrow[1, k] = entering
                unit, _ = standardize(entering)
                n1[1, mine(k, t)] = (unit * vec[1, 0:1] + vec[1, 2:3]).astype(BF16)
                gather_start(0, n1, 1, k)

            emit(0, layer, k, rows)

        each(chunks, finish)

    each(2, forward)

    def copy_ct(k):
        dyr[1, span(k)] = ct_ref[span(k)]

    each(chunks, copy_ct)
    gsmall_ref[...] = jnp.zeros_like(gsmall_ref)
    gbias_ref[...] = jnp.zeros_like(gbias_ref)

    def backward(i):
        layer = 1 - i
        ph = 4 + layer * 2

        def feed_back(k):
            @pl.when(layer == 0)
            def _():
                gather_wait(3, dyr, 0, k)

            grad = mm_nt(dyr[layer, span(k)], w2[layer])
            u = up[layer, span(k)]
            bend = jnp.tanh(GELU_C * (u + GELU_A * (u * u * u)))
            slope = 0.5 * (1.0 + bend) + (0.5 * u) * (1.0 - bend * bend) * (
                GELU_C * (1.0 + (3.0 * GELU_A) * (u * u))
            )
            du = (grad * slope).astype(BF16)
            dup[span(k)] = du
            part[ph, span(k)] = mm_nt(du, w1[layer]).astype(BF16)
            scatter_start(ph, k)
            gbias_ref[layer, 0:1, 384:896] += jnp.sum(du.astype(F32), 0, keepdims=True)

        each(chunks, feed_back)

        def grad_down(b):
            cols = pl.ds(pl.multiple_of(b * 128, 128), 128)
            g2_ref[layer, cols] = mm_tn(act[layer, :, cols], dyr[layer]).astype(BF16)

        each(4, grad_down)

        def grad_up(b):
            cols = pl.ds(pl.multiple_of(b * 256, 256), 256)
            g1_ref[layer, cols] = mm_tn(n2[layer, :, cols], dup[...]).astype(BF16)

        each(4, grad_up)

        def middle(k):
            grad = dyr[layer, mine(k, t)].astype(F32)
            slope, gain_grad, shift_grad = norm_back(
                mrow[layer, k], vec[layer, 1:2], scatter_finish(ph, k)
            )
            dm = grad + slope
            mrow[layer, k] = dm
            low = dm.astype(BF16)
            dmr[layer, mine(k, t)] = low
            gather_start(2, dmr, layer, k)
            gsmall_ref[layer, 1:2] += gain_grad
            gsmall_ref[layer, 3:4] += jnp.sum(low.astype(F32), 0, keepdims=True)
            gsmall_ref[layer, 4:5] += shift_grad
            gsmall_ref[layer, 5:6] += jnp.sum(grad, 0, keepdims=True)

        each(chunks, middle)

        def attention_back(k):
            gather_wait(2, dmr, layer, k)
            da = mm_nt(dmr[layer, span(k)], wout[layer]).astype(BF16)
            packed = qkv[layer, span(k)]
            queries, keys, values = packed[:, 0:128], packed[:, 128:256], packed[:, 256:384]
            dqs, dks, dvs = [], [], []
            for head, grad in enumerate(heads(da)):
                p = prob[layer, k, head]
                dvs.append(mm_tn(p.astype(BF16), da))
                dp = mm_nt(grad, values)
                ds = p * (dp - jnp.sum(p * dp, -1, keepdims=True))
                ds = ds.astype(BF16)
                dqs.append(mm(ds, keys))
                dks.append(mm_tn(ds, queries))
            grads = jnp.concatenate(
                [
                    jnp.where(left_half, dqs[0], dqs[1]) * SCALE,
                    jnp.where(left_half, dks[0], dks[1]) * SCALE,
                    jnp.where(left_half, dvs[0], dvs[1]),
                ],
                1,
            ).astype(BF16)
            dqkv[span(k)] = grads
            part[ph + 1, span(k)] = mm_nt(grads, wqkv[layer]).astype(BF16)
            scatter_start(ph + 1, k)
            gbias_ref[layer, 0:1, 0:384] += jnp.sum(grads.astype(F32), 0, keepdims=True)

        each(chunks, attention_back)

        gout_ref[layer] = mm_tn(mix[layer], dmr[layer]).astype(BF16)

        def grad_qkv(b):
            cols = pl.ds(pl.multiple_of(b * 256, 256), 256)
            gqkv_ref[layer, cols] = mm_tn(n1[layer, :, cols], dqkv[...]).astype(BF16)

        each(4, grad_qkv)

        def finish(k):
            slope, gain_grad, shift_grad = norm_back(
                hrow[layer, k], vec[layer, 0:1], scatter_finish(ph + 1, k)
            )
            rows = mrow[layer, k] + slope

            @pl.when(layer == 1)
            def _():
                dyr[0, mine(k, t)] = rows.astype(BF16)
                gather_start(3, dyr, 0, k)

            emit(1, layer, k, rows)
            gsmall_ref[layer, 0:1] += gain_grad
            gsmall_ref[layer, 2:3] += shift_grad

        each(chunks, finish)

    each(2, backward)

    for i, (own, both) in enumerate(weights):
        pltpu.make_async_copy(both.at[0], both.at[0], wsend.at[i]).wait()
    for ph in range(8):
        pltpu.make_async_copy(rs.at[ph], rs.at[ph], rsend.at[ph]).wait()
    for which, buf, layer in (
        (0, n1, 1),
        (1, n2, 0),
        (1, n2, 1),
        (2, dmr, 0),
        (2, dmr, 1),
        (3, dyr, 0),
    ):
        view = rs.at[0]
        pltpu.make_async_copy(view, view, gsend.at[which, layer]).wait()
    for kind in range(2):
        for layer in range(2):

            @pl.when(c == layer)
            def _():
                view = ostage.at[kind, layer, :, pl.ds(0, T - 1)]
                pltpu.make_async_copy(view, view, osend.at[kind, layer]).wait()

            @pl.when(c != layer)
            def _():
                view = ostage.at[kind, layer]
                pltpu.make_async_copy(view, view, osend.at[kind, layer]).wait()

    for kind, out in enumerate((sec_ref, ing_ref)):
        pltpu.make_async_copy(obuf.at[kind], obuf.at[kind], osem.at[kind]).wait()
        out[...] = obuf[kind].astype(F32)


def core(chunks, x, ct, mask, wqkv, wout, w1, w2, vec):
    n = chunks * ROWS
    vm = pl.BlockSpec(memory_space=pltpu.VMEM)
    hbm = pl.BlockSpec(memory_space=pl.ANY)
    out_shape = (
        jax.ShapeDtypeStruct((2 * n, 128), F32),
        jax.ShapeDtypeStruct((2 * n, 128), F32),
        jax.ShapeDtypeStruct((2, D, 384), BF16),
        jax.ShapeDtypeStruct((2, 128, D), BF16),
        jax.ShapeDtypeStruct((2, D, 512), BF16),
        jax.ShapeDtypeStruct((2, 512, D), BF16),
        jax.ShapeDtypeStruct((2, 8, D), F32),
        jax.ShapeDtypeStruct((2, 1, 896), F32),
    )
    dma = pltpu.SemaphoreType.DMA
    scratch = [
        pltpu.VMEM((2, D, 384), BF16),
        pltpu.VMEM((2, 128, D), BF16),
        pltpu.VMEM((2, D, 512), BF16),
        pltpu.VMEM((2, 512, D), BF16),
        pltpu.VMEM((2, 8, D), F32),
        pltpu.VMEM((2, n, D), BF16),
        pltpu.VMEM((2, n, D), BF16),
        pltpu.VMEM((2, n, D), BF16),
        pltpu.VMEM((2, n, D), BF16),
        pltpu.VMEM((2, n, 384), BF16),
        pltpu.VMEM((2, n, 128), BF16),
        pltpu.VMEM((2, chunks, 2, ROWS, ROWS), F32),
        pltpu.VMEM((2, n, 512), F32),
        pltpu.VMEM((2, n, 512), BF16),
        pltpu.VMEM((n, 512), BF16),
        pltpu.VMEM((n, 384), BF16),
        pltpu.VMEM((2, chunks, OWN, D), F32),
        pltpu.VMEM((2, chunks, OWN, D), F32),
        pltpu.VMEM((8, n, D), BF16),
        pltpu.VMEM((8, chunks, T - 1, OWN, D), BF16),
        pltpu.VMEM((2, 2, chunks, T, OWN, 128), BF16),
        pltpu.VMEM((2, 2 * n, 128), BF16),
        dma((5, 2)),
        dma((5,)),
        dma((8, chunks)),
        dma((8,)),
        dma((4, 2, chunks)),
        dma((4, 2)),
        dma((2,)),
        dma((2, 2)),
    ]
    return pl.pallas_call(
        functools.partial(kernel, chunks),
        out_shape=out_shape,
        in_specs=[vm, vm, vm, hbm, hbm, hbm, hbm, hbm],
        out_specs=[vm] * 8,
        scratch_shapes=scratch,
        compiler_params=pltpu.CompilerParams(
            collective_id=0, has_side_effects=True, vmem_limit_bytes=62 * 2**20
        ),
        name="layers",
    )(x, ct, mask, wqkv, wout, w1, w2, vec)


def shards(
    inputs,
    cotangent,
    doc_ids,
    qkv_weight,
    qkv_bias,
    out_weight,
    fc1_weight,
    fc1_bias,
    fc2_weight,
    norm_gains,
    shifts,
):
    c = lax.axis_index("pipe")
    t = lax.axis_index("tensor")
    n_dp = lax.axis_size("dp")
    chunks = doc_ids.shape[0] // 2
    n = chunks * ROWS
    x = lax.dynamic_slice_in_dim(inputs, c * n, n, 0)
    ct = lax.dynamic_slice_in_dim(cotangent, c * n, n, 0)
    docs = lax.dynamic_slice_in_dim(doc_ids, c * chunks, chunks, 0)
    place = jnp.arange(ROWS)
    visible = (place[None, :] <= place[:, None])[None] & (docs[:, :, None] == docs[:, None, :])
    mask = visible.astype(F32).reshape(n, ROWS)
    bias = jnp.concatenate([qkv_bias[0, 0], jnp.zeros_like(qkv_bias[0, 0]), qkv_bias[0, 1]])
    vec = jnp.concatenate(
        [
            norm_gains[0],
            shifts[0],
            jnp.pad(bias, (0, D - 384))[None],
            jnp.pad(fc1_bias[0], (0, D - 512))[None],
        ],
        0,
    ).astype(F32)
    sec, ing, gqkv, gout, g1, g2, gsmall, gbias = core(
        chunks,
        x,
        ct,
        mask,
        qkv_weight[0].reshape(D, 384),
        out_weight[0],
        fc1_weight[0],
        fc2_weight[0],
        vec,
    )
    m = n_dp
    packed = jnp.concatenate(
        [
            gqkv.reshape(2, m, -1),
            gout.reshape(2, 128, m, D // m).transpose(0, 2, 1, 3).reshape(2, m, -1),
            g1.reshape(2, m, -1),
            g2.reshape(2, 512, m, D // m).transpose(0, 2, 1, 3).reshape(2, m, -1),
        ],
        2,
    )
    own = lax.dynamic_index_in_dim(packed, c, 0, False)
    away = lax.dynamic_index_in_dim(packed, 1 - c, 0, False)
    came = lax.ppermute(away, "pipe", [(0, 1), (1, 0)])
    total = (own.astype(F32) + came.astype(F32)).astype(BF16)
    total = lax.psum_scatter(total, "dp", scatter_dimension=0, tiled=True).astype(F32)[0]
    sizes = [D * 384 // m, 128 * D // m, D * 512 // m, 512 * D // m]
    edges = [0]
    for size in sizes:
        edges.append(edges[-1] + size)
    pieces = [total[a:b] for a, b in zip(edges[:-1], edges[1:])]
    wide = jnp.zeros((2, T, 896), F32)
    wide = lax.dynamic_update_slice(wide, gbias.reshape(2, 1, 896), (0, t, 0))
    tiny = jnp.concatenate([gsmall[:, :6].reshape(2, -1), wide.reshape(2, -1)], 1)
    tiny = lax.psum(tiny, ("pipe", "tensor", "dp"))
    tiny = lax.dynamic_index_in_dim(tiny, c, 0, False)
    small = tiny[: 6 * D].reshape(6, D)
    share = D // (T * m)
    place = (t * m + lax.axis_index("dp")) * share
    small = lax.dynamic_slice_in_dim(small, place, share, 1)
    wide = tiny[6 * D :].reshape(T, 896)
    wide = lax.dynamic_index_in_dim(wide, t, 0, False)
    step = lax.axis_index("dp")
    qb = jnp.stack([wide[0:128], wide[256:384]])
    qb = lax.dynamic_slice_in_dim(qb, step * (128 // m), 128 // m, 1)
    ub = lax.dynamic_slice_in_dim(wide[384:896], step * (512 // m), 512 // m, 0)
    return (
        sec[None],
        ing[None],
        pieces[0].reshape(1, D // m, 3, 128),
        qb[None],
        pieces[1].reshape(1, 128, D // m),
        pieces[2].reshape(1, D // m, 512),
        ub[None],
        pieces[3].reshape(1, 512, D // m),
        small[None, 0:2],
        small[None, 2:6],
    )


def solution(mesh):
    return jax.shard_map(
        shards,
        mesh=mesh,
        in_specs=(
            P("dp", None),
            P("dp", None),
            P("dp", None),
            P("pipe", None, None, "tensor"),
            P("pipe", None, "tensor"),
            P("pipe", "tensor", None),
            P("pipe", None, "tensor"),
            P("pipe", "tensor"),
            P("pipe", "tensor", None),
            P("pipe", None, None),
            P("pipe", None, None),
        ),
        out_specs=(
            P("pipe", "dp", "tensor"),
            P("pipe", "dp", "tensor"),
            P("pipe", "dp", None, "tensor"),
            P("pipe", None, ("tensor", "dp")),
            P("pipe", "tensor", "dp"),
            P("pipe", "dp", "tensor"),
            P("pipe", ("tensor", "dp")),
            P("pipe", "tensor", "dp"),
            P("pipe", None, ("tensor", "dp")),
            P("pipe", None, ("tensor", "dp")),
        ),
        check_vma=False,
    )
```

time: 2040 us -> 435 us (0.21)
  waiting for transfers between devices: 1570 us -> 220 us
  other arithmetic: 202 us -> 24.8 us
  Pallas kernels: 0 us -> 147 us
  matrix products: 140 us -> 0 us
  local copies, waits for them, and re-layouts: 62.9 us -> 29 us
    psum x17 -> x1, waiting for transfers between devices: 1360 us -> 127 us  [shards(): tiny = lax.psum(tiny, ('pipe', 'tensor', 'dp'))]
    pallas_call x0 -> x1, Pallas kernels: none -> 147 us  [core(): pl.pallas_call(functools.partial(kernel, chunks), out_shape=out_shape, in...]
    dot_general x126 -> x0, matrix products: 136 us -> none  [the longest x7 20.6 us: backward_layer(): jnp.einsum('rd,rf->df', wide_two, grad_before, preferred_element_type=jnp...]
    reduce_sum x96 -> x0, other arithmetic: 122 us -> none  [the longest x25 29.6 us: normalize(): centre = jnp.mean(hidden, -1, keepdims=True)]
    reduce_scatter x2 -> x0, waiting for transfers between devices: 76.9 us -> none  [the longest x1 38.5 us: shards(): lax.psum_scatter(grad_up.astype(jnp.bfloat16), 'dp', scatter_dimension=0,...]
    unnamed x29 -> x3, waiting for transfers between devices: 127 us -> 87.7 us
  transfers between devices with their start and end apart: 36 -> 3, of which waited for: 26 -> 3; matrix products, arithmetic and copies ran while one was open for 8% -> 2% of each run, Pallas kernels for 0% -> 0%
where the time goes in v1:
time: 435 us
  waiting for transfers between devices  220 us (51%)
  Pallas kernels  147 us (34%)
  local copies, waits for them, and re-layouts  29 us (7%)
  other arithmetic  24.8 us (6%)
  between operations  14.4 us (3%)
    pallas_call x1, Pallas kernels, core(): pl.pallas_call(functools.partial(kernel, chunks), out_shape=out_shape, in...  147 us
    psum x1, waiting for transfers between devices, shards(): tiny = lax.psum(tiny, ('pipe', 'tensor', 'dp'))  127 us
    unnamed x3, waiting for transfers between devices  87.7 us
    concatenate x1, other arithmetic, shards(): jnp.concatenate([gqkv.reshape(2, m, -1), gout.reshape(2, 128, m, D // m)....  14.7 us
    unnamed x32, local copies, waits for them, and re-layouts  11.6 us
  transfers between devices with their start and end apart: 3, of which 3 were waited for; matrix products, arithmetic and copies ran while one was open for 2% of the time, Pallas kernels for 0%

profile of v1, /device:TPU:0, one launch (start us, length us, event | category | flops | bytes accessed | tf_op | source)
XLA Modules:
  0.0 434.6 jit_solution(4440858364591372553)
XLA Ops:
  7.2 0.0 copy-start
  7.2 0.0 copy-start.5
  7.2 0.0 all-reduce.6.cloned.1.call-start
  7.3 0.6 copy-done
  7.9 0.7 slice_bitcast_fusion.4
  8.6 0.7 reduce
  9.4 0.0 copy-start.7
  9.4 0.0 copy-start.9
  9.4 1.4 copy.25
  10.9 1.2 copy.26.wqkv_in
  12.0 0.8 fusion.2.mask_ref
  12.8 0.0 copy-done.5
  12.8 2.5 constant_dynamic-slice_fusion.4
  15.3 0.0 copy-done.7
  15.3 0.0 copy-done.9
  15.3 0.6 maximum_convert_fusion.vec_in
  16.0 146.8 %layers.1 = (f32[768,128]{1,0:T(8,128)}, f32[768,128]{1,0:T(8,128)}, bf16[2,1024,384]{2,1,0:T(8,128)(2,1)}, bf16[2,128,1024]{2,1,0:T(8,128)(2,1)}, bf16[2,1024,5...) custom-call(bf16[384,1024]{1,0:T(8,128)(2,1)} %get-tuple-element.53.x_ref, ...), custom_call_target="tpu_custom_call" | custom-call | tf_op jit(solution)/shard_map/layers/pallas_call | solution.py:498
  162.8 0.0 copy-start.2
  162.8 1.3 copy.28
  164.1 0.3 copy-done.2
  164.4 1.7 reshape.102
  166.0 2.2 reshape.105
  168.2 2.2 copy.29
  170.5 1.5 bitcast_bitcast_fusion
  171.9 14.7 %pad_maximum_fusion = bf16[2,8,196608]{2,1,0:T(8,128)(2,1)S(1)} fusion(bf16[2,8,65536]{2,1,0:T(8,128)(2,1)} %bitcast_bitcast_fusion, bf16[2,8,65536]{2,1,0:T(8,128)(2,1)S(1)} %reshape.105, bf16[2,8,16384]{2,1,0:T(8,128)(2,1)S(1)} %bitcast_bitcast_fusion.1, bf16[2,8,49152]{2,1,0:T(8,128)(2,1)} %reshape.102), kind=kLoop, calls=%fused_computation | loop fusion | flops 25165824 | bytes 12582912 | tf_op jit(solution)/shard_map/concatenate | solution.py:557
  186.7 0.0 copy-start.1
  186.7 0.0 copy-start.8
  186.7 0.0 copy-start.6
  186.7 0.3 dynamic-slice_bitcast_fusion
  187.0 2.3 copy-done.1
  189.3 0.0 collective-permute-start
  189.4 0.0 copy-done.8
  189.4 0.1 dynamic_update_slice.3
  189.5 0.0 copy-done.6
  189.6 0.7 pad_maximum_fusion.1
  190.3 0.0 all-reduce.6.cloned.1.call-update
  190.3 0.0 all-reduce.8.cloned.1.call-start
  190.4 4.8 %collective-permute-done = bf16[8,196608]{1,0:T(8,128)(2,1)} collective-permute-done((bf16[8,196608]{1,0:T(8,128)(2,1)S(1)}, bf16[8,196608]{1,0:T(8,128)(2,1)}, u32[]{:S(2)}, u32[]{:S(2)}) %collective-permute-start) | collective-permute-done | bytes 3145760 | tf_op jit(solution)/shard_map/ppermute | solution.py:568
  195.1 4.3 fusion
  199.5 0.0 all-reduce.8.cloned.1.call-update
  199.5 0.0 copy-start.4
  199.5 0.0 copy-start.3
  199.5 0.6 copy-done.10
  200.1 0.6 dynamic-slice.1
  200.7 127.0 %all-reduce.6.cloned.1.call-done = f32[2,13312]{1,0:T(2,128)} async-done(((f32[2,13312]{1,0:T(2,128)}), f32[2,13312]{1,0:T(2,128)}) %all-reduce.6.cloned.1.call-update) | async-done | bytes 106512 | tf_op jit(solution)/shard_map/psum | solution.py:579
  327.7 1.0 dynamic-slice_reduce_fusion
  328.7 0.9 dynamic-slice_reduce_fusion.1
  329.6 0.6 dynamic-slice.7
  330.2 0.1 constant_dynamic-slice_fusion
  330.3 0.6 fusion.8
  330.9 0.1 constant_dynamic-slice_fusion.1
  331.0 0.6 slice_bitcast_fusion.2
  331.6 0.6 slice_bitcast_fusion.1
  332.1 87.7 %all-reduce.8.cloned.1.call-done = bf16[8,196608]{1,0:T(8,128)(2,1)} async-done(((bf16[8,196608]{1,0:T(8,128)(2,1)}), bf16[8,196608]{1,0:T(8,128)(2,1)}) %all-reduce.8.cloned.1.call-update) | async-done | bytes 3145744
  419.8 2.9 dynamic-slice_convert_fusion
  422.7 0.6 slice.66
  423.3 0.5 slice_reduce_fusion.1
  423.8 0.9 fusion.9
  424.7 0.1 reshape.108
  424.8 0.7 copy.27
  425.5 0.7 reshape.113
  426.3 0.0 copy-done.4
  426.3 0.7 copy.37
  427.0 0.7 copy.38
  (18 shorter events, 0.2 us)
Async XLA Ops:
  7.2 0.7 copy-start
  7.2 5.6 %copy-start.5 = (bf16[768,1024]{1,0:T(8,128)(2,1)S(1)}, bf16[768,1024]{1,0:T(8,128)(2,1)}, u32[]{:S(2)}) copy-start(bf16[768,1024]{1,0:T(8,128)(2,1)} %param.12) | copy-start | bytes 4718596
  7.2 320.5 %all-reduce.6.cloned.1.call-start = ((), (), s32[]{:S(2)}) async-start(), calls=%async_computation | async-start | bytes 212992 | tf_op jit(solution)/shard_map/psum | solution.py:579
  9.4 5.9 %copy-start.7 = (bf16[1,4,1024]{2,1,0:T(4,128)(2,1)S(1)}, bf16[1,4,1024]{2,1,0:T(4,128)(2,1)}, u32[]{:S(2)}) copy-start(bf16[1,4,1024]{2,1,0:T(4,128)(2,1)} %param.21) | copy-start | bytes 24580
  9.4 5.9 %copy-start.9 = (bf16[1,2,1024]{2,1,0:T(2,128)(2,1)S(1)}, bf16[1,2,1024]{2,1,0:T(2,128)(2,1)}, u32[]{:S(2)}) copy-start(bf16[1,2,1024]{2,1,0:T(2,128)(2,1)} %param.20) | copy-start | bytes 12292
  162.8 1.6 copy-start.2
  186.7 2.6 copy-start.1
  186.7 2.6 copy-start.8
  186.7 2.8 copy-start.6
  189.3 5.8 %collective-permute-start = (bf16[8,196608]{1,0:T(8,128)(2,1)S(1)}, bf16[8,196608]{1,0:T(8,128)(2,1)}, u32[]{:S(2)}, u32[]{:S(2)}) collective-permute-start(bf16[8,196608]{1,0:T(8,128)(2,1)S(1)} %dynamic-slice_bitcast_fusion), channel_id=1, source_target_pairs={{0,64},{64,0},{1,65},{65,1},{2,66},{66,2},{3,67},{67,3},{4,68},{68... | collective-permute-start | bytes 9437192 | tf_op jit(solution)/shard_map/ppermute | solution.py:568
  190.3 229.5 %all-reduce.8.cloned.1.call-start = ((), (), s32[]{:S(2)}) async-start(), calls=%async_computation.1 | async-start | bytes 6291456
  199.5 0.7 copy-start.10
  199.5 226.8 %copy-start.4 = (f32[768,128]{1,0:T(8,128)S(1)}, f32[768,128]{1,0:T(8,128)}, u32[]{:S(2)}) copy-start(f32[768,128]{1,0:T(8,128)} %get-tuple-element.18) | copy-start | bytes 1179652
  199.5 227.5 %copy-start.3 = (f32[768,128]{1,0:T(8,128)S(1)}, f32[768,128]{1,0:T(8,128)}, u32[]{:S(2)}) copy-start(f32[768,128]{1,0:T(8,128)} %get-tuple-element.19) | copy-start | bytes 1179652
Sparse Core Ops, SparseCore 0:
  190.4 137.2 all-reduce.5
  330.4 89.3 all-reduce.7

commit v2 on v1

v2 whole, which is shorter than its diff:
```python
import functools

import jax
import jax.numpy as jnp
from jax import lax
from jax.experimental import pallas as pl
from jax.experimental.pallas import tpu as pltpu
from jax.sharding import PartitionSpec as P

MESH = pl.DeviceIdType.MESH
F32 = jnp.float32
BF16 = jnp.bfloat16
EPSILON = 1e-05
HD = 64
SCALE = HD**-0.5
D = 1024
ROWS = 128
T = 8
Y = 4
OWN = ROWS // T
GELU_C = 0.7978845608028654
GELU_A = 0.044715


def mm(a, b):
    return lax.dot_general(a, b, (((1,), (0,)), ((), ())), preferred_element_type=F32)


def mm_nt(a, b):
    return lax.dot_general(a, b, (((1,), (1,)), ((), ())), preferred_element_type=F32)


def mm_tn(a, b):
    return lax.dot_general(a, b, (((0,), (0,)), ((), ())), preferred_element_type=F32)


def standardize(rows):
    centered = rows - jnp.mean(rows, -1, keepdims=True)
    variance = jnp.mean(centered * centered, -1, keepdims=True)
    root = lax.rsqrt(variance + EPSILON)
    return centered * root, root


def norm_back(rows, gain, grad):
    unit, root = standardize(rows)
    e = grad * gain
    slope = root * (
        e - jnp.mean(e, -1, keepdims=True) - unit * jnp.mean(e * unit, -1, keepdims=True)
    )
    return slope, jnp.sum(grad * unit, 0, keepdims=True), jnp.sum(grad, 0, keepdims=True)


def kernel(
    chunks,
    nz,
    x_ref,
    ct_ref,
    mask_ref,
    wqkv_in,
    wout_in,
    w1_in,
    w2_in,
    vec_in,
    sec_ref,
    ing_ref,
    gqkv_ref,
    gout_ref,
    g1_ref,
    g2_ref,
    gsmall_ref,
    gbias_ref,
    wqkv,
    wout,
    w1,
    w2,
    vec,
    n1,
    n2,
    dmr,
    dyr,
    qkv,
    mix,
    prob,
    up,
    act,
    dup,
    dqkv,
    hrow,
    mrow,
    part,
    cbuf,
    psum,
    rs,
    ostage,
    obuf,
    gbufs,
    zrs,
    zsums,
    xrs,
    gpack,
    tsum,
    tr,
    wsem,
    wsend,
    wrelay,
    vsem,
    vsend,
    csem,
    csend,
    rsem,
    rsend,
    gsem,
    gsend,
    hsem,
    hsend,
    osem,
    osend,
    zsem,
    zsend,
    xsem,
    xsend,
    tsem,
    tsend,
):
    c = lax.axis_index("pipe")
    t = lax.axis_index("tensor")
    d = lax.axis_index("dp")
    xh = t // Y
    y = lax.rem(t, Y)
    xl = d // nz
    z = lax.rem(d, nz)
    sib = (1 - c, t, d)

    barrier = pltpu.get_barrier_semaphore()

    def greet(device):
        pl.semaphore_signal(barrier, inc=1, device_id=device, device_id_type=MESH)

    for j in range(T):
        other = lax.rem(t + j, T)
        if j:
            greet((c, other, d))
        greet((1 - c, other, d))
    far = (1 - xl) * nz + z
    for core_ in range(2):
        for j in range(2):
            greet((core_, j * Y + y, far))
    for j in range(1, nz):
        greet((c, t, xl * nz + lax.rem(z + j, nz)))
    pl.semaphore_wait(barrier, 2 * T - 1 + 4 + nz - 1)

    def remote(src, dst, send, recv, device):
        pltpu.make_async_remote_copy(
            src_ref=src,
            dst_ref=dst,
            send_sem=send,
            recv_sem=recv,
            device_id=device,
            device_id_type=MESH,
        ).start()

    def await_bytes(view, sem):
        pltpu.make_async_copy(view, view, sem).wait()

    weights = ((wqkv_in, wqkv), (wout_in, wout), (w1_in, w1), (w2_in, w2))
    native = c == xh
    partner = (xh, (1 - xh) * Y + y, far)
    home = (xh, t, d)

    def half(i, which):
        size = weights[i][1].shape[1] // 2
        return pl.ds(pl.multiple_of(which * size, size), size)

    def send_weight(i, whole):
        own, both = weights[i]

        @pl.when(native)
        def _():
            for h in range(2):
                pltpu.make_async_copy(
                    own.at[half(i, h)], both.at[c, half(i, h)], wsem.at[i, c, h]
                ).start()

        @pl.when(jnp.logical_not(native))
        def _():
            for h in range(2):
                remote(
                    own.at[half(i, h)],
                    both.at[c, half(i, h)],
                    wsend.at[i],
                    wsem.at[i, c, h],
                    home,
                )

        for h in (0, 1) if whole else (xl,):
            remote(
                own.at[half(i, h)],
                both.at[c, half(i, h)],
                wsend.at[i],
                wsem.at[i, c, h],
                partner,
            )

    def await_half(i, layer, h):
        await_bytes(weights[i][1].at[layer, half(i, h)], wsem.at[i, layer, h])

    def relay(i, layer):
        both = weights[i][1]

        @pl.when(jnp.logical_not(native))
        def _():
            await_half(i, layer, 1 - xl)
            piece = both.at[layer, half(i, 1 - xl)]
            remote(piece, piece, wrelay.at[i, layer], wsem.at[i, layer, 1 - xl], (c, t, far))

    def need(i, layer, whole=False):
        if whole:
            await_half(i, layer, 0)
            await_half(i, layer, 1)
        else:

            @pl.when(native)
            def _():
                await_half(i, layer, 1 - xl)

            await_half(i, layer, xl)

    def span(k):
        return pl.ds(pl.multiple_of(k * ROWS, ROWS), ROWS)

    def side(k, who):
        return pl.ds(pl.multiple_of(k * ROWS + who * (ROWS // 2), ROWS // 2), ROWS // 2)

    own_start = (c * Y + y) * OWN

    def mine(k):
        return pl.ds(pl.multiple_of(k * ROWS + own_start, OWN), OWN)

    def y_peer(j):
        return (c, xh * Y + lax.rem(y + j, Y), d)

    def reduce_start(ph, k):
        remote(
            part.at[ph, side(k, 1 - c)], cbuf.at[ph, k], csend.at[ph], csem.at[ph, k], sib
        )

    def reduce_middle(ph, k):
        await_bytes(cbuf.at[ph, k], csem.at[ph, k])
        psum[ph, k] = (part[ph, side(k, c)].astype(F32) + cbuf[ph, k].astype(F32)).astype(BF16)
        for j in range(1, Y):
            rows = pl.ds(pl.multiple_of(lax.rem(y + j, Y) * OWN, OWN), OWN)
            remote(
                psum.at[ph, k, rows], rs.at[ph, k, j - 1], rsend.at[ph], rsem.at[ph, k], y_peer(j)
            )

    def reduce_finish(ph, k):
        await_bytes(rs.at[ph, k], rsem.at[ph, k])
        rows = pl.ds(pl.multiple_of(y * OWN, OWN), OWN)
        total = psum[ph, k, rows].astype(F32)
        for j in range(Y - 1):
            total = total + rs[ph, k, j].astype(F32)
        return total

    def gather_start(which, buf, layer, k):
        for j in range(1, Y):
            view = buf.at[layer, mine(k)]
            remote(view, view, gsend.at[which, layer], gsem.at[which, layer, k], y_peer(j))

    def gather_middle(which, buf, layer, k):
        await_bytes(buf.at[layer, pl.ds(0, (Y - 1) * OWN)], gsem.at[which, layer, k])
        view = buf.at[layer, side(k, c)]
        remote(view, view, hsend.at[which, layer], hsem.at[which, layer, k], sib)

    def gather_finish(which, buf, layer, k):
        await_bytes(buf.at[layer, side(k, 1 - c)], hsem.at[which, layer, k])

    def emit(kind, layer, k, rows):
        low = rows.astype(BF16)
        for j in range(T):
            ostage[kind, layer, k, j] = low[:, j * 128 : (j + 1) * 128]
        first = xh * (chunks * ROWS) + k * ROWS + own_start
        target = pl.ds(pl.multiple_of(first, OWN), OWN)

        def away(j):
            other = lax.rem(t + j, T)
            remote(
                ostage.at[kind, layer, k, other],
                obuf.at[kind, target],
                osend.at[kind, layer],
                osem.at[kind],
                (layer, other, d),
            )

        for j in range(1, T):
            away(j)

        @pl.when(c == layer)
        def _():
            pltpu.make_async_copy(
                ostage.at[kind, layer, k, t], obuf.at[kind, target], osem.at[kind]
            ).start()

        @pl.when(c != layer)
        def _():
            away(0)

    slot = xh * 2 + xl

    def x_send(m, layer, source):
        for to in range(2):
            self_ = jnp.logical_and(jnp.logical_and(c == layer, native), xl == to)
            src, dst = source(to), xrs[m].at[slot]

            @pl.when(self_)
            def _():
                pltpu.make_async_copy(src, dst, xsem.at[m]).start()

            @pl.when(jnp.logical_not(self_))
            def _():
                remote(
                    src, dst, xsend.at[m, layer], xsem.at[m], (layer, c * Y + y, to * nz + z)
                )

    def z_peer(j):
        return (c, t, xl * nz + lax.rem(z + j, nz))

    def z_first_start(m, layer):
        for j in range(1, nz):
            for to in range(2):
                remote(
                    gbufs[m].at[layer, to * nz + lax.rem(z + j, nz)],
                    zrs[m].at[layer, j - 1, to],
                    zsend.at[m, layer],
                    zsem.at[m, layer],
                    z_peer(j),
                )

    def z_first_middle(m, layer):
        if nz > 1:
            await_bytes(zrs[m].at[layer], zsem.at[m, layer])
        for to in range(2):
            total = gbufs[m][layer, to * nz + z].astype(F32)
            for j in range(nz - 1):
                total = total + zrs[m][layer, j, to].astype(F32)
            zsums[m][layer, to] = total.astype(BF16)
        x_send(m, layer, lambda to: zsums[m].at[layer, to])

    def z_first_finish(m):
        await_bytes(xrs[m], xsem.at[m])
        return sum4(m)

    def sum4(m):
        total = xrs[m][0].astype(F32)
        for j in range(1, 4):
            total = total + xrs[m][j].astype(F32)
        return total

    def x_first_start(m, layer):
        x_send(m, layer, lambda to: gbufs[m].at[layer, pl.ds(to * nz, nz)])

    def x_first_middle(m):
        await_bytes(xrs[m], xsem.at[m])
        zsums[m][...] = sum4(m).astype(BF16)
        for j in range(1, nz):
            remote(
                zsums[m].at[lax.rem(z + j, nz)],
                zrs[m].at[j - 1],
                zsend.at[m, 0],
                zsem.at[m, 0],
                z_peer(j),
            )

    def x_first_finish(m):
        total = zsums[m][z].astype(F32)
        if nz > 1:
            await_bytes(zrs[m], zsem.at[m, 0])
        for j in range(nz - 1):
            total = total + zrs[m][j].astype(F32)
        return total

    left_half = lax.broadcasted_iota(jnp.int32, (ROWS, 128), 1) < HD

    def heads(value):
        zero = jnp.zeros_like(value)
        return jnp.where(left_half, value, zero), jnp.where(left_half, zero, value)

    def each(count, body):
        def step(i, carry):
            body(i)
            return carry

        lax.fori_loop(0, count, step, 0)

    def flow(before, work, after):
        def step(s):
            @pl.when(s < chunks)
            def _():
                before(s)

            @pl.when(jnp.logical_and(s >= 1, s < chunks + 1))
            def _():
                work(s - 1)

            @pl.when(s >= 2)
            def _():
                after(s - 2)

        each(chunks + 2, step)

    @pl.when(native)
    def _():
        pltpu.make_async_copy(vec_in, vec.at[c], vsem.at[c]).start()

    @pl.when(jnp.logical_not(native))
    def _():
        remote(vec_in, vec.at[c], vsend.at[0], vsem.at[c], home)

    remote(vec_in, vec.at[c], vsend.at[0], vsem.at[c], partner)

    @pl.when(c == 0)
    def _():
        send_weight(0, True)
        send_weight(1, True)

    await_bytes(vec.at[0], vsem.at[0])
    await_bytes(vec.at[1], vsem.at[1])
    gpack[...] = jnp.zeros_like(gpack)

    def start(k):
        unit, _ = standardize(x_ref[span(k)].astype(F32))
        n1[0, span(k)] = (unit * vec[0, 0:1] + vec[0, 2:3]).astype(BF16)
        hrow[0, k] = x_ref[mine(k)].astype(F32)
        dyr[1, span(k)] = ct_ref[span(k)]

    each(chunks, start)

    def forward(layer):
        ph = layer * 2

        @pl.when(layer == 0)
        def _():
            need(0, 0, True)

            @pl.when(c == 0)
            def _():
                send_weight(2, False)
                send_weight(3, False)

            need(1, 0, True)

        @pl.when(layer == 1)
        def _():
            need(0, 1)
            need(1, 1)

        def arrive(k):
            @pl.when(layer == 1)
            def _():
                gather_middle(0, n1, 1, k)

        def attention(k):
            @pl.when(layer == 1)
            def _():
                gather_finish(0, n1, 1, k)

            packed = mm(n1[layer, span(k)], wqkv[layer]) + vec[layer, 6:7, 0:384]
            packed = packed.astype(BF16)
            qkv[layer, span(k)] = packed
            queries, keys, values = packed[:, 0:128], packed[:, 128:256], packed[:, 256:384]
            visible = mask_ref[span(k)] > 0
            parts = []
            for head, query in enumerate(heads(queries)):
                scores = jnp.where(visible, mm_nt(query, keys) * SCALE, -1e30)
                weights_ = jnp.exp(scores - jnp.max(scores, -1, keepdims=True))
                p = weights_ / jnp.sum(weights_, -1, keepdims=True)
                prob[layer, k, head] = p
                parts.append(mm(p.astype(BF16), values))
            mixture = jnp.where(left_half, parts[0], parts[1]).astype(BF16)
            mix[layer, span(k)] = mixture
            part[ph, span(k)] = mm(mixture, wout[layer]).astype(BF16)
            reduce_start(ph, k)

        flow(arrive, attention, lambda k: reduce_middle(ph, k))

        relay(2, layer)

        def second_norm(k):
            rows = hrow[layer, k] + reduce_finish(ph, k) + vec[layer, 3:4]
            mrow[layer, k] = rows
            unit, _ = standardize(rows)
            n2[layer, mine(k)] = (unit * vec[layer, 1:2] + vec[layer, 4:5]).astype(BF16)
            gather_start(1, n2, layer, k)

        each(chunks, second_norm)
        relay(3, layer)
        need(2, layer)
        need(3, layer)

        def feed(k):
            gather_finish(1, n2, layer, k)
            u = mm(n2[layer, span(k)], w1[layer]) + vec[layer, 7:8, 0:512]
            up[layer, span(k)] = u
            g = 0.5 * u * (1.0 + jnp.tanh(GELU_C * (u + GELU_A * (u * u * u))))
            g = g.astype(BF16)
            act[layer, span(k)] = g
            part[ph + 1, span(k)] = mm(g, w2[layer]).astype(BF16)
            reduce_start(ph + 1, k)

        flow(
            lambda k: gather_middle(1, n2, layer, k),
            feed,
            lambda k: reduce_middle(ph + 1, k),
        )

        @pl.when(jnp.logical_and(layer == 0, c == 1))
        def _():
            send_weight(0, False)
            send_weight(1, False)

        def finish(k):
            rows = mrow[layer, k] + reduce_finish(ph + 1, k) + vec[layer, 5:6]

            @pl.when(layer == 0)
            def _():
                entering = rows.astype(BF16).astype(F32)
                hrow[1, k] = entering
                unit, _ = standardize(entering)
                n1[1, mine(k)] = (unit * vec[1, 0:1] + vec[1, 2:3]).astype(BF16)
                gather_start(0, n1, 1, k)

            emit(0, layer, k, rows)

        each(chunks, finish)

        @pl.when(layer == 0)
        def _():
            @pl.when(c == 1)
            def _():
                send_weight(2, False)
                send_weight(3, False)

            relay(0, 1)
            relay(1, 1)

    each(2, forward)

    def backward(i):
        layer = 1 - i
        ph = 4 + layer * 2

        def arrive(k):
            @pl.when(layer == 0)
            def _():
                gather_middle(3, dyr, 0, k)

        def feed_back(k):
            @pl.when(layer == 0)
            def _():
                gather_finish(3, dyr, 0, k)

            grad = mm_nt(dyr[layer, span(k)], w2[layer])
            u = up[layer, span(k)]
            bend = jnp.tanh(GELU_C * (u + GELU_A * (u * u * u)))
            slope = 0.5 * (1.0 + bend) + (0.5 * u) * (1.0 - bend * bend) * (
                GELU_C * (1.0 + (3.0 * GELU_A) * (u * u))
            )
            du = (grad * slope).astype(BF16)
            dup[span(k)] = du
            part[ph, span(k)] = mm_nt(du, w1[layer]).astype(BF16)
            reduce_start(ph, k)
            gpack[layer, 6:7, 384:896] += jnp.sum(du.astype(F32), 0, keepdims=True)

        flow(arrive, feed_back, lambda k: reduce_middle(ph, k))

        pieces = 2 * nz
        wide = D // pieces

        def grad_down(b):
            cols = pl.ds(pl.multiple_of(b * 128, 128), 128)
            block = mm_tn(act[layer, :, cols], dyr[layer]).astype(BF16)
            for q in range(pieces):
                gbufs[0][layer, q, cols] = block[:, q * wide : (q + 1) * wide]

        each(4, grad_down)
        z_first_start(0, layer)

        def middle(k):
            grad = dyr[layer, mine(k)].astype(F32)
            slope, gain_grad, shift_grad = norm_back(
                mrow[layer, k], vec[layer, 1:2], reduce_finish(ph, k)
            )
            dm = grad + slope
            mrow[layer, k] = dm
            low = dm.astype(BF16)
            dmr[layer, mine(k)] = low
            gather_start(2, dmr, layer, k)
            gpack[layer, 1:2] += gain_grad
            gpack[layer, 3:4] += jnp.sum(low.astype(F32), 0, keepdims=True)
            gpack[layer, 4:5] += shift_grad
            gpack[layer, 5:6] += jnp.sum(grad, 0, keepdims=True)

        each(chunks, middle)

        def grad_up(b):
            cols = pl.ds(pl.multiple_of(b * wide, wide), wide)
            gbufs[1][layer, b] = mm_tn(n2[layer, :, cols], dup[...]).astype(BF16)

        each(pieces, grad_up)
        x_first_start(1, layer)

        @pl.when(layer == 0)
        def _():
            collect_attention(1)

        def attention_back(k):
            gather_finish(2, dmr, layer, k)
            da = mm_nt(dmr[layer, span(k)], wout[layer]).astype(BF16)
            packed = qkv[layer, span(k)]
            queries, keys, values = packed[:, 0:128], packed[:, 128:256], packed[:, 256:384]
            dqs, dks, dvs = [], [], []
            for head, grad in enumerate(heads(da)):
                p = prob[layer, k, head]
                dvs.append(mm_tn(p.astype(BF16), da))
                dp = mm_nt(grad, values)
                ds = p * (dp - jnp.sum(p * dp, -1, keepdims=True))
                ds = ds.astype(BF16)
                dqs.append(mm(ds, keys))
                dks.append(mm_tn(ds, queries))
            grads = jnp.concatenate(
                [
                    jnp.where(left_half, dqs[0], dqs[1]) * SCALE,
                    jnp.where(left_half, dks[0], dks[1]) * SCALE,
                    jnp.where(left_half, dvs[0], dvs[1]),
                ],
                1,
            ).astype(BF16)
            dqkv[span(k)] = grads
            part[ph + 1, span(k)] = mm_nt(grads, wqkv[layer]).astype(BF16)
            reduce_start(ph + 1, k)
            gpack[layer, 6:7, 0:384] += jnp.sum(grads.astype(F32), 0, keepdims=True)

        flow(
            lambda k: gather_middle(2, dmr, layer, k),
            attention_back,
            lambda k: reduce_middle(ph + 1, k),
        )

        block = mm_tn(mix[layer], dmr[layer]).astype(BF16)
        for q in range(pieces):
            gbufs[4][layer, q] = block[:, q * wide : (q + 1) * wide]
        x_first_start(4, layer)

        def grad_qkv(b):
            cols = pl.ds(pl.multiple_of(b * wide, wide), wide)
            block = mm_tn(n1[layer, :, cols], dqkv[...]).astype(BF16)
            gbufs[2][layer, b] = block[:, 0:256]
            gbufs[3][layer, b] = block[:, 256:384]

        each(pieces, grad_qkv)
        z_first_start(2, layer)
        x_first_start(3, layer)

        def finish(k):
            slope, gain_grad, shift_grad = norm_back(
                hrow[layer, k], vec[layer, 0:1], reduce_finish(ph + 1, k)
            )
            rows = mrow[layer, k] + slope

            @pl.when(layer == 1)
            def _():
                dyr[0, mine(k)] = rows.astype(BF16)
                gather_start(3, dyr, 0, k)

            emit(1, layer, k, rows)
            gpack[layer, 0:1] += gain_grad
            gpack[layer, 2:3] += shift_grad

        each(chunks, finish)
        x_send(5, layer, lambda to: gpack.at[layer])
        z_first_middle(0, layer)

        @pl.when(c == layer)
        def _():
            x_first_middle(1)

    def collect_attention(layer):
        @pl.when(c == layer)
        def _():
            x_first_middle(4)
            x_first_middle(3)

        z_first_middle(2, layer)

        @pl.when(c == layer)
        def _():
            await_bytes(xrs[5], xsem.at[5])
            zsums[5][...] = sum4(5)
            for j in range(1, nz):
                remote(zsums[5], zrs[5].at[j - 1], zsend.at[5, 0], zsem.at[5, 0], z_peer(j))

    each(2, backward)
    collect_attention(0)

    total = zsums[5][...]
    if nz > 1:
        await_bytes(zrs[5], zsem.at[5, 0])
    for j in range(nz - 1):
        total = total + zrs[5][j]
    for j in range(T):
        tsum[j] = total[:, j * 128 : (j + 1) * 128]
    gbias_ref[...] = total
    for j in range(1, T):
        other = lax.rem(t + j, T)
        remote(tsum.at[other], tr.at[j - 1], tsend.at[0], tsem.at[0], (c, other, d))

    g1_ref[...] = x_first_finish(1)
    gout_ref[...] = x_first_finish(4)
    gqkv_ref[:, 256:384] = x_first_finish(3)
    g2_ref[...] = z_first_finish(0)
    gqkv_ref[:, 0:256] = z_first_finish(2)
    await_bytes(tr, tsem.at[0])
    small = tsum[t]
    for j in range(T - 1):
        small = small + tr[j]
    gsmall_ref[...] = small
    for kind, out in enumerate((sec_ref, ing_ref)):
        await_bytes(obuf.at[kind], osem.at[kind])
        out[...] = obuf[kind].astype(F32)

    for i in range(4):
        both = weights[i][1]
        early = i < 2

        @pl.when(jnp.logical_not(native))
        def _():
            await_bytes(both.at[0], wsend.at[i])
            for layer in range(2):
                if layer or not early:
                    await_bytes(both.at[0, half(i, 0)], wrelay.at[i, layer])

        await_bytes(both.at[0, half(i, 0)], wsend.at[i])
        if early:

            @pl.when(c == 0)
            def _():
                await_bytes(both.at[0, half(i, 0)], wsend.at[i])

    @pl.when(jnp.logical_not(native))
    def _():
        await_bytes(vec.at[0], vsend.at[0])

    await_bytes(vec.at[0], vsend.at[0])
    for ph in range(8):
        await_bytes(cbuf.at[ph], csend.at[ph])
        await_bytes(rs.at[ph], rsend.at[ph])
    for which, layer in ((0, 1), (1, 0), (1, 1), (2, 0), (2, 1), (3, 0)):
        await_bytes(rs.at[0], gsend.at[which, layer])
        await_bytes(cbuf.at[0], hsend.at[which, layer])
    for layer in range(2):
        for kind in range(2):

            @pl.when(c == layer)
            def _():
                view = ostage.at[kind, layer, :, pl.ds(0, T - 1)]
                await_bytes(view, osend.at[kind, layer])

            @pl.when(c != layer)
            def _():
                await_bytes(ostage.at[kind, layer], osend.at[kind, layer])

        self_ = jnp.logical_and(c == layer, native)
        for m in range(6):
            if nz > 1 and m in (0, 2):
                await_bytes(zrs[m].at[layer], zsend.at[m, layer])
            await_bytes(xrs[m].at[0], xsend.at[m, layer])

            @pl.when(jnp.logical_not(self_))
            def _():
                await_bytes(xrs[m].at[0], xsend.at[m, layer])

    if nz > 1:
        for m in (1, 3, 4, 5):
            await_bytes(zrs[m], zsend.at[m, 0])
    await_bytes(tr, tsend.at[0])


def core(chunks, nz, x, ct, mask, wqkv, wout, w1, w2, vec):
    n = chunks * ROWS
    vm = pl.BlockSpec(memory_space=pltpu.VMEM)
    hbm = pl.BlockSpec(memory_space=pl.ANY)
    pieces = 2 * nz
    wide = D // pieces
    out_shape = (
        jax.ShapeDtypeStruct((2 * n, 128), F32),
        jax.ShapeDtypeStruct((2 * n, 128), F32),
        jax.ShapeDtypeStruct((wide, 384), F32),
        jax.ShapeDtypeStruct((128, wide), F32),
        jax.ShapeDtypeStruct((wide, 512), F32),
        jax.ShapeDtypeStruct((512, wide), F32),
        jax.ShapeDtypeStruct((8, 128), F32),
        jax.ShapeDtypeStruct((8, D), F32),
    )
    dma = pltpu.SemaphoreType.DMA
    shape = ((512, wide), (wide, 512), (wide, 256), (wide, 128), (128, wide))
    back = max(nz - 1, 1)
    gbufs = [pltpu.VMEM((2, pieces) + s, BF16) for s in shape]
    zrs, zsums, xrs = [], [], []
    for m, s in enumerate(shape):
        if m in (0, 2):
            zrs.append(pltpu.VMEM((2, back, 2) + s, BF16))
            zsums.append(pltpu.VMEM((2, 2) + s, BF16))
            xrs.append(pltpu.VMEM((4,) + s, BF16))
        else:
            zrs.append(pltpu.VMEM((back,) + s, BF16))
            zsums.append(pltpu.VMEM((nz,) + s, BF16))
            xrs.append(pltpu.VMEM((4, nz) + s, BF16))
    zrs.append(pltpu.VMEM((back, 8, D), F32))
    zsums.append(pltpu.VMEM((8, D), F32))
    xrs.append(pltpu.VMEM((4, 8, D), F32))
    scratch = [
        pltpu.VMEM((2, D, 384), BF16),
        pltpu.VMEM((2, 128, D), BF16),
        pltpu.VMEM((2, D, 512), BF16),
        pltpu.VMEM((2, 512, D), BF16),
        pltpu.VMEM((2, 8, D), F32),
        pltpu.VMEM((2, n, D), BF16),
        pltpu.VMEM((2, n, D), BF16),
        pltpu.VMEM((2, n, D), BF16),
        pltpu.VMEM((2, n, D), BF16),
        pltpu.VMEM((2, n, 384), BF16),
        pltpu.VMEM((2, n, 128), BF16),
        pltpu.VMEM((2, chunks, 2, ROWS, ROWS), F32),
        pltpu.VMEM((2, n, 512), F32),
        pltpu.VMEM((2, n, 512), BF16),
        pltpu.VMEM((n, 512), BF16),
        pltpu.VMEM((n, 384), BF16),
        pltpu.VMEM((2, chunks, OWN, D), F32),
        pltpu.VMEM((2, chunks, OWN, D), F32),
        pltpu.VMEM((8, n, D), BF16),
        pltpu.VMEM((8, chunks, ROWS // 2, D), BF16),
        pltpu.VMEM((8, chunks, ROWS // 2, D), BF16),
        pltpu.VMEM((8, chunks, Y - 1, OWN, D), BF16),
        pltpu.VMEM((2, 2, chunks, T, OWN, 128), BF16),
        pltpu.VMEM((2, 2 * n, 128), BF16),
        gbufs,
        zrs,
        zsums,
        xrs,
        pltpu.VMEM((2, 8, D), F32),
        pltpu.VMEM((T, 8, 128), F32),
        pltpu.VMEM((T - 1, 8, 128), F32),
        dma((4, 2, 2)),
        dma((4,)),
        dma((4, 2)),
        dma((2,)),
        dma((1,)),
        dma((8, chunks)),
        dma((8,)),
        dma((8, chunks)),
        dma((8,)),
        dma((4, 2, chunks)),
        dma((4, 2)),
        dma((4, 2, chunks)),
        dma((4, 2)),
        dma((2,)),
        dma((2, 2)),
        dma((6, 2)),
        dma((6, 2)),
        dma((6,)),
        dma((6, 2)),
        dma((1,)),
        dma((1,)),
    ]
    return pl.pallas_call(
        functools.partial(kernel, chunks, nz),
        out_shape=out_shape,
        in_specs=[vm, vm, vm, hbm, hbm, hbm, hbm, hbm],
        out_specs=[vm] * 8,
        scratch_shapes=scratch,
        compiler_params=pltpu.CompilerParams(
            collective_id=0, has_side_effects=True, vmem_limit_bytes=62 * 2**20
        ),
        name="layers",
    )(x, ct, mask, wqkv, wout, w1, w2, vec)


def shards(
    inputs,
    cotangent,
    doc_ids,
    qkv_weight,
    qkv_bias,
    out_weight,
    fc1_weight,
    fc1_bias,
    fc2_weight,
    norm_gains,
    shifts,
):
    t = lax.axis_index("tensor")
    step = lax.axis_index("dp")
    m = lax.axis_size("dp")
    chunks = doc_ids.shape[0] // 2
    n = chunks * ROWS
    xh = t // Y
    x = lax.dynamic_slice_in_dim(inputs, xh * n, n, 0)
    ct = lax.dynamic_slice_in_dim(cotangent, xh * n, n, 0)
    docs = lax.dynamic_slice_in_dim(doc_ids, xh * chunks, chunks, 0)
    place = jnp.arange(ROWS)
    visible = (place[None, :] <= place[:, None])[None] & (docs[:, :, None] == docs[:, None, :])
    mask = visible.astype(F32).reshape(n, ROWS)
    bias = jnp.concatenate([qkv_bias[0, 0], jnp.zeros_like(qkv_bias[0, 0]), qkv_bias[0, 1]])
    vec = jnp.concatenate(
        [
            norm_gains[0],
            shifts[0],
            jnp.pad(bias, (0, D - 384))[None],
            jnp.pad(fc1_bias[0], (0, D - 512))[None],
        ],
        0,
    ).astype(F32)
    sec, ing, gqkv, gout, g1, g2, gsmall, gbias = core(
        chunks,
        m // 2,
        x,
        ct,
        mask,
        qkv_weight[0].reshape(D, 384),
        out_weight[0],
        fc1_weight[0],
        fc2_weight[0],
        vec,
    )
    share = D // (T * m)
    small = lax.dynamic_slice_in_dim(gsmall, step * share, share, 1)
    bias_row = gbias[6]
    qb = jnp.stack([bias_row[0:128], bias_row[256:384]])
    qb = lax.dynamic_slice_in_dim(qb, step * (128 // m), 128 // m, 1)
    ub = lax.dynamic_slice_in_dim(bias_row[384:896], step * (512 // m), 512 // m, 0)
    return (
        sec[None],
        ing[None],
        gqkv.reshape(1, D // m, 3, 128),
        qb[None],
        gout[None],
        g1[None],
        ub[None],
        g2[None],
        small[None, 0:2],
        small[None, 2:6],
    )


def solution(mesh):
    return jax.shard_map(
        shards,
        mesh=mesh,
        in_specs=(
            P("dp", None),
            P("dp", None),
            P("dp", None),
            P("pipe", None, None, "tensor"),
            P("pipe", None, "tensor"),
            P("pipe", "tensor", None),
            P("pipe", None, "tensor"),
            P("pipe", "tensor"),
            P("pipe", "tensor", None),
            P("pipe", None, None),
            P("pipe", None, None),
        ),
        out_specs=(
            P("pipe", "dp", "tensor"),
            P("pipe", "dp", "tensor"),
            P("pipe", "dp", None, "tensor"),
            P("pipe", None, ("tensor", "dp")),
            P("pipe", "tensor", "dp"),
            P("pipe", "dp", "tensor"),
            P("pipe", ("tensor", "dp")),
            P("pipe", "tensor", "dp"),
            P("pipe", None, ("tensor", "dp")),
            P("pipe", None, ("tensor", "dp")),
        ),
        check_vma=False,
    )
```

time: 435 us -> 183 us (0.42)
  waiting for transfers between devices: 220 us -> 0 us
  other arithmetic: 24.8 us -> 1.49 us
  Pallas kernels: 147 us -> 165 us
  local copies, waits for them, and re-layouts: 29 us -> 15.3 us
  between operations: 14.4 us -> 0.85 us
    psum x1 -> x0, waiting for transfers between devices: 127 us -> none  [shards(): tiny = lax.psum(tiny, ('pipe', 'tensor', 'dp'))]
    unnamed x3 -> x0, waiting for transfers between devices: 87.7 us -> none
    pallas_call x1, Pallas kernels: 147 us -> 165 us  [core(): pl.pallas_call(functools.partial(kernel, chunks, nz), out_shape=out_shape...]
    concatenate x2 -> x0, other arithmetic: 15.4 us -> none  [the longest x1 14.7 us: shards(): jnp.concatenate([gqkv.reshape(2, m, -1), gout.reshape(2, 128, m, D // m)....]
    convert_element_type x2 -> x0, other arithmetic: 7.18 us -> none  [the longest x1 4.33 us: shards(): total = (own.astype(F32) + came.astype(F32)).astype(BF16)]
    reshape x8 -> x0, local copies, waits for them, and re-layouts: 6.21 us -> none  [the longest x1 2.21 us: shards(): g1.reshape(2, m, -1)]
    unnamed x32 -> x27, local copies, waits for them, and re-layouts: 11.6 us -> 5.71 us
    ppermute x1 -> x0, waiting for transfers between devices: 4.78 us -> none  [shards(): came = lax.ppermute(away, 'pipe', [(0, 1), (1, 0)])]
  transfers between devices with their start and end apart: 3 -> 0, of which waited for: 3 -> 0; matrix products, arithmetic and copies ran while one was open for 2% -> 0% of each run, Pallas kernels for 0% -> 0%
where the time goes in v2:
time: 183 us
  Pallas kernels  165 us (90%)
  local copies, waits for them, and re-layouts  15.3 us (8%)
    pallas_call x1, Pallas kernels, core(): pl.pallas_call(functools.partial(kernel, chunks, nz), out_shape=out_shape...  165 us
    unnamed x27, local copies, waits for them, and re-layouts  5.71 us

profile of v2, /device:TPU:0, one launch (start us, length us, event | category | flops | bytes accessed | tf_op | source)
XLA Modules:
  0.0 183.0 jit_solution(7158087272401518868)
XLA Ops:
  0.6 0.0 copy-start
  0.7 0.0 copy-start.9
  0.7 0.0 copy-start.8
  0.7 0.0 copy-start.6
  0.7 0.0 copy-start.7
  0.7 0.0 copy-start.1
  0.7 2.7 %constant_dynamic-slice_fusion.4 = (bf16[384,1024]{1,0:T(8,128)(2,1)}, bf16[384,1024]{1,0:T(8,128)(2,1)}) fusion(bf16[768,1024]{1,0:T(8,128)(2,1)} %param.12, s32[]{:T(128)S(6)} %select_n.20, bf16[768,1024]{1,0:T(8,128)(2,1)} %param.11), kind=kLoop, calls=%fused_computation.16 | loop fusion | bytes 3145732 | tf_op jit(solution)/shard_map/dynamic_slice | solution.py:907
  3.5 0.0 copy-done
  3.5 0.8 fusion.1.mask_ref
  4.3 0.0 copy-done.9
  4.3 0.0 copy-done.8
  4.4 0.0 copy-done.6
  4.4 0.0 copy-done.7
  4.4 0.6 maximum_convert_fusion.vec_in
  5.1 0.0 copy-done.1
  5.1 0.3 copy.23
  5.4 1.1 copy.24.wqkv_in
  6.5 165.4 %layers.1 = (f32[768,128]{1,0:T(8,128)}, f32[768,128]{1,0:T(8,128)}, f32[128,384]{1,0:T(8,128)}, f32[128,128]{1,0:T(8,128)}, f32[128,512]{1,0:T(8,128)}, /*index...) custom-call(bf16[384,1024]{1,0:T(8,128)(2,1)} %get-tuple-element.51.x_ref, ...), custom_call_target="tpu_custom_call" | custom-call | tf_op jit(solution)/shard_map/layers/pallas_call | solution.py:874
  171.9 0.0 copy-start.2
  171.9 0.0 copy-start.5
  171.9 0.0 copy-start.4
  171.9 0.0 copy-start.3
  171.9 0.8 fusion.8
  172.7 0.6 fusion.7
  173.4 1.1 copy.25
  174.4 0.8 copy.26
  175.2 0.7 constant_dynamic-slice_fusion
  176.0 0.6 slice_bitcast_fusion
  176.6 0.6 slice_bitcast_fusion.1
  177.1 0.7 slice.32
  177.8 0.6 constant_dynamic-slice_fusion.1
  178.4 1.8 copy.32
  180.2 0.0 copy-done.2
  180.2 0.7 copy.33
  180.9 0.0 copy-done.5
  180.9 0.6 copy.34
  181.6 0.0 copy-done.4
  181.6 0.7 copy.35
  182.3 0.0 copy-done.3
  182.3 0.7 copy.36
  (11 shorter events, 0.1 us)
Async XLA Ops:
  0.6 2.8 %copy-start = (s32[6,128]{1,0:T(8,128)S(1)}, s32[6,128]{1,0:T(8,128)}, u32[]{:S(2)}) copy-start(s32[6,128]{1,0:T(8,128)} %param.13) | copy-start | bytes 9220
  0.7 3.6 %copy-start.9 = (bf16[1,2,128]{2,1,0:T(2,128)(2,1)S(1)}, bf16[1,2,128]{2,1,0:T(2,128)(2,1)}, u32[]{:S(2)}) copy-start(bf16[1,2,128]{2,1,0:T(2,128)(2,1)} %param.15) | copy-start | bytes 1540
  0.7 3.7 %copy-start.8 = (bf16[1,512]{1,0:T(2,128)(2,1)S(1)}, bf16[1,512]{1,0:T(2,128)(2,1)}, u32[]{:S(2)}) copy-start(bf16[1,512]{1,0:T(2,128)(2,1)} %param.18) | copy-start | bytes 3076
  0.7 3.7 %copy-start.6 = (bf16[1,4,1024]{2,1,0:T(4,128)(2,1)S(1)}, bf16[1,4,1024]{2,1,0:T(4,128)(2,1)}, u32[]{:S(2)}) copy-start(bf16[1,4,1024]{2,1,0:T(4,128)(2,1)} %param.21) | copy-start | bytes 24580
  0.7 3.7 %copy-start.7 = (bf16[1,2,1024]{2,1,0:T(2,128)(2,1)S(1)}, bf16[1,2,1024]{2,1,0:T(2,128)(2,1)}, u32[]{:S(2)}) copy-start(bf16[1,2,1024]{2,1,0:T(2,128)(2,1)} %param.20) | copy-start | bytes 12292
  0.7 4.3 %copy-start.1 = (bf16[1,1024,3,128]{3,1,2,0:T(8,128)(2,1)S(1)}, bf16[1,1024,3,128]{3,1,2,0:T(8,128)(2,1)}, u32[]{:S(2)}) copy-start(bf16[1,1024,3,128]{3,1,2,0:T(8,128)(2,1)} %param.14) | copy-start | bytes 2359300
  171.9 8.3 %copy-start.2 = (f32[768,128]{1,0:T(8,128)S(1)}, f32[768,128]{1,0:T(8,128)}, u32[]{:S(2)}) copy-start(f32[768,128]{1,0:T(8,128)} %get-tuple-element.19) | copy-start | bytes 1179652
  171.9 9.0 %copy-start.5 = (f32[128,128]{1,0:T(8,128)S(1)}, f32[128,128]{1,0:T(8,128)}, u32[]{:S(2)}) copy-start(f32[128,128]{1,0:T(8,128)} %get-tuple-element.22) | copy-start | bytes 196612
  171.9 9.6 %copy-start.4 = (f32[128,512]{1,0:T(8,128)S(1)}, f32[128,512]{1,0:T(8,128)}, u32[]{:S(2)}) copy-start(f32[128,512]{1,0:T(8,128)} %get-tuple-element.23) | copy-start | bytes 786436
  171.9 10.3 %copy-start.3 = (f32[512,128]{1,0:T(8,128)S(1)}, f32[512,128]{1,0:T(8,128)}, u32[]{:S(2)}) copy-start(f32[512,128]{1,0:T(8,128)} %get-tuple-element.24) | copy-start | bytes 786436

commit v3 on v2

--- a/solution.py
+++ b/solution.py
@@ -53,22 +53,27 @@
 def kernel(
     chunks,
     nz,
-    x_ref,
-    ct_ref,
-    mask_ref,
+    x_in,
+    ct_in,
+    docs_ref,
     wqkv_in,
     wout_in,
     w1_in,
     w2_in,
-    vec_in,
-    sec_ref,
-    ing_ref,
+    qb_in,
+    b1_in,
+    gains_in,
+    shifts_in,
+    rows_ref,
     gqkv_ref,
     gout_ref,
     g1_ref,
     g2_ref,
     gsmall_ref,
     gbias_ref,
+    x_ref,
+    mask_ref,
+    vec_in,
     wqkv,
     wout,
     w1,
@@ -100,8 +105,10 @@
     gpack,
     tsum,
     tr,
+    insem,
     wsem,
     wsend,
+    whome,
     wrelay,
     vsem,
     vsend,
@@ -131,6 +138,12 @@
     z = lax.rem(d, nz)
     sib = (1 - c, t, d)
 
+    first_row = pl.ds(pl.multiple_of(xh * (chunks * ROWS), ROWS), chunks * ROWS)
+    x_copy = pltpu.make_async_copy(x_in.at[first_row], x_ref, insem.at[0])
+    ct_copy = pltpu.make_async_copy(ct_in.at[first_row], dyr.at[1], insem.at[1])
+    x_copy.start()
+    ct_copy.start()
+
     barrier = pltpu.get_barrier_semaphore()
 
     def greet(device):
@@ -147,6 +160,12 @@
             greet((core_, j * Y + y, far))
     for j in range(1, nz):
         greet((c, t, xl * nz + lax.rem(z + j, nz)))
+    vec_in[...] = jnp.zeros_like(vec_in)
+    vec_in[0:2] = gains_in[0].astype(F32)
+    vec_in[2:6] = shifts_in[0].astype(F32)
+    vec_in[6:7, 0:128] = qb_in[0, 0:1].astype(F32)
+    vec_in[6:7, 256:384] = qb_in[0, 1:2].astype(F32)
+    vec_in[7:8, 0:512] = b1_in[...].astype(F32)
     pl.semaphore_wait(barrier, 2 * T - 1 + 4 + nz - 1)
 
     def remote(src, dst, send, recv, device):
@@ -171,7 +190,7 @@
         size = weights[i][1].shape[1] // 2
         return pl.ds(pl.multiple_of(which * size, size), size)
 
-    def send_weight(i, whole):
+    def send_weight(i):
         own, both = weights[i]
 
         @pl.when(native)
@@ -187,19 +206,21 @@
                 remote(
                     own.at[half(i, h)],
                     both.at[c, half(i, h)],
-                    wsend.at[i],
+                    whome.at[i],
                     wsem.at[i, c, h],
                     home,
                 )
 
-        for h in (0, 1) if whole else (xl,):
-            remote(
-                own.at[half(i, h)],
-                both.at[c, half(i, h)],
-                wsend.at[i],
-                wsem.at[i, c, h],
-                partner,
-            )
+        remote(
+            own.at[half(i, xl)],
+            both.at[c, half(i, xl)],
+            wsend.at[i],
+            wsem.at[i, c, xl],
+            partner,
+        )
+
+    def weight_left(i):
+        await_bytes(weights[i][1].at[0, half(i, 0)], wsend.at[i])
 
     def await_half(i, layer, h):
         await_bytes(weights[i][1].at[layer, half(i, h)], wsem.at[i, layer, h])
@@ -213,17 +234,12 @@
             piece = both.at[layer, half(i, 1 - xl)]
             remote(piece, piece, wrelay.at[i, layer], wsem.at[i, layer, 1 - xl], (c, t, far))
 
-    def need(i, layer, whole=False):
-        if whole:
-            await_half(i, layer, 0)
-            await_half(i, layer, 1)
-        else:
-
-            @pl.when(native)
-            def _():
-                await_half(i, layer, 1 - xl)
-
-            await_half(i, layer, xl)
+    def need(i, layer):
+        @pl.when(native)
+        def _():
+            await_half(i, layer, 1 - xl)
+
+        await_half(i, layer, xl)
 
     def span(k):
         return pl.ds(pl.multiple_of(k * ROWS, ROWS), ROWS)
@@ -419,18 +435,25 @@
 
     @pl.when(c == 0)
     def _():
-        send_weight(0, True)
-        send_weight(1, True)
-
+        send_weight(0)
+        send_weight(1)
+
+    gpack[...] = jnp.zeros_like(gpack)
+    x_copy.wait()
+    ct_copy.wait()
     await_bytes(vec.at[0], vsem.at[0])
     await_bytes(vec.at[1], vsem.at[1])
-    gpack[...] = jnp.zeros_like(gpack)
+    lanes = lax.broadcasted_iota(jnp.int32, (ROWS, ROWS), 1)
+    places = lax.broadcasted_iota(jnp.int32, (ROWS, ROWS), 0)
 
     def start(k):
         unit, _ = standardize(x_ref[span(k)].astype(F32))
         n1[0, span(k)] = (unit * vec[0, 0:1] + vec[0, 2:3]).astype(BF16)
         hrow[0, k] = x_ref[mine(k)].astype(F32)
-        dyr[1, span(k)] = ct_ref[span(k)]
+        segment = docs_ref[pl.ds(xh * chunks + k, 1)].astype(F32)
+        segment = jnp.broadcast_to(segment, (ROWS, ROWS))
+        visible = jnp.logical_and(lanes <= places, segment == segment.T)
+        mask_ref[span(k)] = jnp.where(visible, 1.0, 0.0)
 
     each(chunks, start)
 
@@ -439,19 +462,16 @@
 
         @pl.when(layer == 0)
         def _():
-            need(0, 0, True)
+            relay(0, 0)
+            relay(1, 0)
 
             @pl.when(c == 0)
             def _():
-                send_weight(2, False)
-                send_weight(3, False)
-
-            need(1, 0, True)
-
-        @pl.when(layer == 1)
-        def _():
-            need(0, 1)
-            need(1, 1)
+                weight_left(0)
+                send_weight(2)
+
+        need(0, layer)
+        need(1, layer)
 
         def arrive(k):
             @pl.when(layer == 1)
@@ -482,7 +502,17 @@
 
         flow(arrive, attention, lambda k: reduce_middle(ph, k))
 
-        relay(2, layer)
+        @pl.when(jnp.logical_and(layer == 0, c == 0))
+        def _():
+            send_weight(3)
+
+        @pl.when(layer == 0)
+        def _():
+            relay(2, 0)
+
+        @pl.when(layer == 1)
+        def _():
+            relay(3, 1)
 
         def second_norm(k):
             rows = hrow[layer, k] + reduce_finish(ph, k) + vec[layer, 3:4]
@@ -492,7 +522,16 @@
             gather_start(1, n2, layer, k)
 
         each(chunks, second_norm)
-        relay(3, layer)
+
+        @pl.when(layer == 0)
+        def _():
+            relay(3, 0)
+
+            @pl.when(c == 1)
+            def _():
+                send_weight(0)
+                send_weight(1)
+
         need(2, layer)
         need(3, layer)
 
@@ -512,10 +551,14 @@
             lambda k: reduce_middle(ph + 1, k),
         )
 
-        @pl.when(jnp.logical_and(layer == 0, c == 1))
-        def _():
-            send_weight(0, False)
-            send_weight(1, False)
+        @pl.when(layer == 0)
+        def _():
+            @pl.when(c == 1)
+            def _():
+                send_weight(2)
+
+            relay(0, 1)
+            relay(1, 1)
 
         def finish(k):
             rows = mrow[layer, k] + reduce_finish(ph + 1, k) + vec[layer, 5:6]
@@ -536,11 +579,9 @@
         def _():
             @pl.when(c == 1)
             def _():
-                send_weight(2, False)
-                send_weight(3, False)
-
-            relay(0, 1)
-            relay(1, 1)
+                send_weight(3)
+
+            relay(2, 1)
 
     each(2, forward)
 
@@ -723,27 +764,25 @@
     for j in range(T - 1):
         small = small + tr[j]
     gsmall_ref[...] = small
-    for kind, out in enumerate((sec_ref, ing_ref)):
+    for kind in range(2):
         await_bytes(obuf.at[kind], osem.at[kind])
-        out[...] = obuf[kind].astype(F32)
+    rows_ref[...] = obuf[...]
 
     for i in range(4):
         both = weights[i][1]
-        early = i < 2
 
         @pl.when(jnp.logical_not(native))
         def _():
-            await_bytes(both.at[0], wsend.at[i])
+            await_bytes(both.at[0], whome.at[i])
             for layer in range(2):
-                if layer or not early:
-                    await_bytes(both.at[0, half(i, 0)], wrelay.at[i, layer])
-
-        await_bytes(both.at[0, half(i, 0)], wsend.at[i])
-        if early:
-
-            @pl.when(c == 0)
-            def _():
-                await_bytes(both.at[0, half(i, 0)], wsend.at[i])
+                await_bytes(both.at[0, half(i, 0)], wrelay.at[i, layer])
+
+        if i:
+            weight_left(i)
+
+    @pl.when(c == 1)
+    def _():
+        weight_left(0)
 
     @pl.when(jnp.logical_not(native))
     def _():
@@ -784,15 +823,14 @@
     await_bytes(tr, tsend.at[0])
 
 
-def core(chunks, nz, x, ct, mask, wqkv, wout, w1, w2, vec):
+def core(chunks, nz, x, ct, docs, wqkv, wout, w1, w2, qb, b1, gains, shifts):
     n = chunks * ROWS
     vm = pl.BlockSpec(memory_space=pltpu.VMEM)
     hbm = pl.BlockSpec(memory_space=pl.ANY)
     pieces = 2 * nz
     wide = D // pieces
     out_shape = (
-        jax.ShapeDtypeStruct((2 * n, 128), F32),
-        jax.ShapeDtypeStruct((2 * n, 128), F32),
+        jax.ShapeDtypeStruct((2, 2 * n, 128), BF16),
         jax.ShapeDtypeStruct((wide, 384), F32),
         jax.ShapeDtypeStruct((128, wide), F32),
         jax.ShapeDtypeStruct((wide, 512), F32),
@@ -818,6 +856,9 @@
     zsums.append(pltpu.VMEM((8, D), F32))
     xrs.append(pltpu.VMEM((4, 8, D), F32))
     scratch = [
+        pltpu.VMEM((n, D), BF16),
+        pltpu.VMEM((n, ROWS), F32),
+        pltpu.VMEM((8, D), F32),
         pltpu.VMEM((2, D, 384), BF16),
         pltpu.VMEM((2, 128, D), BF16),
         pltpu.VMEM((2, D, 512), BF16),
@@ -849,7 +890,9 @@
         pltpu.VMEM((2, 8, D), F32),
         pltpu.VMEM((T, 8, 128), F32),
         pltpu.VMEM((T - 1, 8, 128), F32),
+        dma((2,)),
         dma((4, 2, 2)),
+        dma((4,)),
         dma((4,)),
         dma((4, 2)),
         dma((2,)),
@@ -874,14 +917,60 @@
     return pl.pallas_call(
         functools.partial(kernel, chunks, nz),
         out_shape=out_shape,
-        in_specs=[vm, vm, vm, hbm, hbm, hbm, hbm, hbm],
-        out_specs=[vm] * 8,
+        in_specs=[hbm, hbm, vm, hbm, hbm, hbm, hbm, vm, vm, vm, vm],
+        out_specs=[vm] * 7,
         scratch_shapes=scratch,
         compiler_params=pltpu.CompilerParams(
             collective_id=0, has_side_effects=True, vmem_limit_bytes=62 * 2**20
         ),
         name="layers",
-    )(x, ct, mask, wqkv, wout, w1, w2, vec)
+    )(x, ct, docs, wqkv, wout, w1, w2, qb, b1, gains, shifts)
+
+
+def closing(
+    m,
+    rows,
+    gqkv,
+    gout,
+    g1,
+    g2,
+    small,
+    bias,
+    sec_out,
+    ing_out,
+    gqkv_out,
+    qb_out,
+    gout_out,
+    g1_out,
+    b1_out,
+    g2_out,
+    gains_out,
+    shifts_out,
+):
+    d = lax.axis_index("dp")
+    sec_out[0] = rows[0].astype(F32)
+    ing_out[0] = rows[1].astype(F32)
+    for j in range(3):
+        gqkv_out[0, :, j, :] = gqkv[:, j * 128 : (j + 1) * 128]
+    gout_out[0] = gout[...]
+    g1_out[0] = g1[...]
+    g2_out[0] = g2[...]
+    share = 128 // m
+    shift = lax.rem(128 - d * share, 128)
+    rolled = pltpu.roll(small[...], shift, 1)
+    gains_out[0] = rolled[0:2, 0:share]
+    shifts_out[0] = rolled[2:6, 0:share]
+    for j in range(2):
+        rolled = pltpu.roll(bias[:, j * 256 : j * 256 + 128], shift, 1)
+        qb_out[0, j : j + 1] = rolled[6:7, 0:share]
+    wide = 512 // m
+    if wide >= 128:
+        b1_out[...] = bias[6:7, pl.ds(pl.multiple_of(384 + d * wide, 128), wide)]
+    else:
+        per = 128 // wide
+        block = bias[:, pl.ds(pl.multiple_of(384 + d // per * 128, 128), 128)]
+        rolled = pltpu.roll(block, lax.rem(128 - lax.rem(d, per) * wide, 128), 1)
+        b1_out[...] = rolled[6:7, 0:wide]
 
 
 def shards(
@@ -897,58 +986,45 @@
     norm_gains,
     shifts,
 ):
-    t = lax.axis_index("tensor")
-    step = lax.axis_index("dp")
     m = lax.axis_size("dp")
     chunks = doc_ids.shape[0] // 2
     n = chunks * ROWS
-    xh = t // Y
-    x = lax.dynamic_slice_in_dim(inputs, xh * n, n, 0)
-    ct = lax.dynamic_slice_in_dim(cotangent, xh * n, n, 0)
-    docs = lax.dynamic_slice_in_dim(doc_ids, xh * chunks, chunks, 0)
-    place = jnp.arange(ROWS)
-    visible = (place[None, :] <= place[:, None])[None] & (docs[:, :, None] == docs[:, None, :])
-    mask = visible.astype(F32).reshape(n, ROWS)
-    bias = jnp.concatenate([qkv_bias[0, 0], jnp.zeros_like(qkv_bias[0, 0]), qkv_bias[0, 1]])
-    vec = jnp.concatenate(
-        [
-            norm_gains[0],
-            shifts[0],
-            jnp.pad(bias, (0, D - 384))[None],
-            jnp.pad(fc1_bias[0], (0, D - 512))[None],
-        ],
-        0,
-    ).astype(F32)
-    sec, ing, gqkv, gout, g1, g2, gsmall, gbias = core(
+    results = core(
         chunks,
         m // 2,
-        x,
-        ct,
-        mask,
+        inputs,
+        cotangent,
+        doc_ids,
         qkv_weight[0].reshape(D, 384),
         out_weight[0],
         fc1_weight[0],
         fc2_weight[0],
-        vec,
+        qkv_bias,
+        fc1_bias,
+        norm_gains,
+        shifts,
     )
-    share = D // (T * m)
-    small = lax.dynamic_slice_in_dim(gsmall, step * share, share, 1)
-    bias_row = gbias[6]
-    qb = jnp.stack([bias_row[0:128], bias_row[256:384]])
-    qb = lax.dynamic_slice_in_dim(qb, step * (128 // m), 128 // m, 1)
-    ub = lax.dynamic_slice_in_dim(bias_row[384:896], step * (512 // m), 512 // m, 0)
-    return (
-        sec[None],
-        ing[None],
-        gqkv.reshape(1, D // m, 3, 128),
-        qb[None],
-        gout[None],
-        g1[None],
-        ub[None],
-        g2[None],
-        small[None, 0:2],
-        small[None, 2:6],
+    vm = pl.BlockSpec(memory_space=pltpu.VMEM)
+    shapes = (
+        (1, 2 * n, 128),
+        (1, 2 * n, 128),
+        (1, D // m, 3, 128),
+        (1, 2, 128 // m),
+        (1, 128, D // m),
+        (1, D // m, 512),
+        (1, 512 // m),
+        (1, 512, D // m),
+        (1, 2, 128 // m),
+        (1, 4, 128 // m),
     )
+    return pl.pallas_call(
+        functools.partial(closing, m),
+        out_shape=[jax.ShapeDtypeStruct(shape, F32) for shape in shapes],
+        in_specs=[vm] * 7,
+        out_specs=[vm] * 10,
+        compiler_params=pltpu.CompilerParams(vmem_limit_bytes=48 * 2**20),
+        name="closing",
+    )(*results)
 
 
 def solution(mesh):

time: 183 us -> 168 us (0.918)
  Pallas kernels: 165 us -> 158 us
  local copies, waits for them, and re-layouts: 15.3 us -> 9.34 us
    pallas_call x1, Pallas kernels: 165 us -> 157 us  [core(): pl.pallas_call(functools.partial(kernel, chunks, nz), out_shape=out_shape...]
    dynamic_slice x4 -> x0, local copies, waits for them, and re-layouts: 4.05 us -> none  [the longest x1 2.72 us: shards(): ct = lax.dynamic_slice_in_dim(cotangent, xh * n, n, 0)]
    unnamed x27 -> x15, local copies, waits for them, and re-layouts: 5.71 us -> 7.49 us
where the time goes in v3:
time: 168 us
  Pallas kernels  158 us (94%)
  local copies, waits for them, and re-layouts  9.34 us (6%)
    pallas_call x1, Pallas kernels, core(): pl.pallas_call(functools.partial(kernel, chunks, nz), out_shape=out_shape...  157 us
    unnamed x15, local copies, waits for them, and re-layouts  7.49 us

profile of v3, /device:TPU:0, one launch (start us, length us, event | category | flops | bytes accessed | tf_op | source)
XLA Modules:
  0.0 167.8 jit_solution(9840514797640119381)
XLA Ops:
  0.6 1.4 copy.23
  2.1 1.2 copy.24.wqkv_in
  3.2 156.7 %layers.1 = (bf16[2,768,128]{2,1,0:T(8,128)(2,1)}, f32[128,384]{1,0:T(8,128)}, f32[128,128]{1,0:T(8,128)}, f32[128,512]{1,0:T(8,128)}, f32[512,128]{1,0:T(8,128)}, /*index=5*/f32[8,128]{1,0:T(8,128)}, f32[8,1024]{1,0:T(8,128)}) custom-call(bf16[768,1024]{1,0:T(8,128)(2,1)} %x_in.1, bf16[768,1024]{1,0:T(8,128)(2,1)} %ct_in.1, s32[6,128]{1,0:T(8,128)} %docs_ref.1, ...), custom_call_target="tpu_custom_call" | custom-call | tf_op jit(solution)/shard_map/layers/pallas_call | solution.py:917
  159.9 0.0 copy-start
  159.9 1.0 copy-done
  160.9 0.0 copy-start.1
  160.9 0.9 copy-done.1
  161.9 0.0 copy-start.2
  161.9 0.9 copy-done.2
  162.8 0.0 copy-start.3
  162.8 0.9 copy-done.3
  163.7 0.0 copy-start.4
  163.7 0.8 copy-done.4
  164.6 0.0 copy-start.5
  164.6 0.8 copy-done.5
  165.3 0.0 copy-start.6
  165.3 0.7 copy-done.6
  166.0 1.1 closing.1
  167.1 0.7 copy.25
Async XLA Ops:
  159.9 1.0 copy-start
  160.9 0.9 copy-start.1
  161.9 0.9 copy-start.2
  162.8 0.9 copy-start.3
  163.7 0.8 copy-start.4
  164.6 0.8 copy-start.5
  165.3 0.7 copy-start.6

commit v4 on v3

v4 whole, which is shorter than its diff:
```python
import functools

import jax
import jax.numpy as jnp
from jax import lax
from jax.experimental import pallas as pl
from jax.experimental.pallas import tpu as pltpu
from jax.sharding import PartitionSpec as P

MESH = pl.DeviceIdType.MESH
F32 = jnp.float32
BF16 = jnp.bfloat16
EPSILON = 1e-05
HD = 64
SCALE = HD**-0.5
D = 1024
ROWS = 128
T = 8
Y = 4
PARTS = 2
OWN = ROWS // T
GELU_C = 0.7978845608028654
GELU_A = 0.044715


def mm(a, b):
    return lax.dot_general(a, b, (((1,), (0,)), ((), ())), preferred_element_type=F32)


def mm_nt(a, b):
    return lax.dot_general(a, b, (((1,), (1,)), ((), ())), preferred_element_type=F32)


def mm_tn(a, b):
    return lax.dot_general(a, b, (((0,), (0,)), ((), ())), preferred_element_type=F32)


def standardize(rows):
    centered = rows - jnp.mean(rows, -1, keepdims=True)
    variance = jnp.mean(centered * centered, -1, keepdims=True)
    root = lax.rsqrt(variance + EPSILON)
    return centered * root, root


def norm_back(rows, gain, grad):
    unit, root = standardize(rows)
    e = grad * gain
    slope = root * (
        e - jnp.mean(e, -1, keepdims=True) - unit * jnp.mean(e * unit, -1, keepdims=True)
    )
    return slope, jnp.sum(grad * unit, 0, keepdims=True), jnp.sum(grad, 0, keepdims=True)


def kernel(
    chunks,
    nz,
    x_in,
    ct_in,
    docs_ref,
    wqkv_in,
    wout_in,
    w1_in,
    w2_in,
    qb_in,
    b1_in,
    gains_in,
    shifts_in,
    rows_ref,
    grads_ref,
    x_ref,
    mask_ref,
    vec_in,
    wqkv,
    wout,
    w1,
    w2,
    vec,
    n1,
    n2,
    dmr,
    dyr,
    qkv,
    mix,
    prob,
    up,
    act,
    dup,
    dqkv,
    hrow,
    mrow,
    part,
    cbuf,
    psum,
    rs,
    ostage,
    obuf,
    gbufs,
    zrs,
    zsums,
    xrs,
    gpack,
    sstage,
    sbias,
    sgot,
    ssum,
    sall,
    insem,
    wsem,
    wsend,
    whome,
    wrelay,
    vsem,
    vsend,
    csem,
    csend,
    rsem,
    rsend,
    gsem,
    gsend,
    hsem,
    hsend,
    osem,
    osend,
    zsem,
    zsend,
    xsem,
    xsend,
    ssem,
    ssend,
):
    c = lax.axis_index("pipe")
    t = lax.axis_index("tensor")
    d = lax.axis_index("dp")
    xh = t // Y
    y = lax.rem(t, Y)
    xl = d // nz
    z = lax.rem(d, nz)
    sib = (1 - c, t, d)

    first_row = pl.ds(pl.multiple_of(xh * (chunks * ROWS), ROWS), chunks * ROWS)
    x_copy = pltpu.make_async_copy(x_in.at[first_row], x_ref, insem.at[0])
    ct_copy = pltpu.make_async_copy(ct_in.at[first_row], dyr.at[1], insem.at[1])
    x_copy.start()
    ct_copy.start()

    barrier = pltpu.get_barrier_semaphore()

    def greet(device):
        pl.semaphore_signal(barrier, inc=1, device_id=device, device_id_type=MESH)

    for j in range(T):
        other = lax.rem(t + j, T)
        if j:
            greet((c, other, d))
        greet((1 - c, other, d))
    far = (1 - xl) * nz + z
    for core_ in range(2):
        for j in range(2):
            greet((core_, j * Y + y, far))
    for j in range(1, nz):
        greet((c, t, xl * nz + lax.rem(z + j, nz)))
        greet((c, t, (1 - xl) * nz + lax.rem(z + j, nz)))
    vec_in[...] = jnp.zeros_like(vec_in)
    vec_in[0:2] = gains_in[0].astype(F32)
    vec_in[2:6] = shifts_in[0].astype(F32)
    vec_in[6:7, 0:128] = qb_in[0, 0:1].astype(F32)
    vec_in[6:7, 256:384] = qb_in[0, 1:2].astype(F32)
    vec_in[7:8, 0:512] = b1_in[...].astype(F32)
    pl.semaphore_wait(barrier, 2 * T - 1 + 4 + 2 * (nz - 1))

    def remote(src, dst, send, recv, device):
        pltpu.make_async_remote_copy(
            src_ref=src,
            dst_ref=dst,
            send_sem=send,
            recv_sem=recv,
            device_id=device,
            device_id_type=MESH,
        ).start()

    def await_bytes(view, sem):
        pltpu.make_async_copy(view, view, sem).wait()

    weights = ((wqkv_in, wqkv), (wout_in, wout), (w1_in, w1), (w2_in, w2))
    native = c == xh
    partner = (xh, (1 - xh) * Y + y, far)
    home = (xh, t, d)

    def half(i, which, q):
        size = weights[i][1].shape[1] // (2 * PARTS)
        return pl.ds(pl.multiple_of((which * PARTS + q) * size, size), size)

    def send_weight(i):
        own, both = weights[i]
        for q in range(PARTS):
            piece = half(i, xl, q)
            remote(
                own.at[piece], both.at[c, piece], wsend.at[i], wsem.at[i, c, xl, q], partner
            )
        for h in range(2):
            for q in range(PARTS):
                src, dst = own.at[half(i, h, q)], both.at[c, half(i, h, q)]

                @pl.when(native)
                def _():
                    pltpu.make_async_copy(src, dst, wsem.at[i, c, h, q]).start()

                @pl.when(jnp.logical_not(native))
                def _():
                    remote(src, dst, whome.at[i], wsem.at[i, c, h, q], home)

    def whole_half(i):
        return weights[i][1].at[0, pl.ds(0, weights[i][1].shape[1] // 2)]

    def weight_left(i):
        await_bytes(whole_half(i), wsend.at[i])

    def await_half(i, layer, h, q):
        await_bytes(weights[i][1].at[layer, half(i, h, q)], wsem.at[i, layer, h, q])

    def relay(i, layer):
        both = weights[i][1]

        @pl.when(jnp.logical_not(native))
        def _():
            for q in range(PARTS):
                await_half(i, layer, 1 - xl, q)
                piece = both.at[layer, half(i, 1 - xl, q)]
                remote(
                    piece, piece, wrelay.at[i, layer], wsem.at[i, layer, 1 - xl, q], (c, t, far)
                )

    def need(i, layer):
        for q in range(PARTS):

            @pl.when(native)
            def _():
                await_half(i, layer, 1 - xl, q)

            await_half(i, layer, xl, q)

    def span(k):
        return pl.ds(pl.multiple_of(k * ROWS, ROWS), ROWS)

    def side(k, who):
        return pl.ds(pl.multiple_of(k * ROWS + who * (ROWS // 2), ROWS // 2), ROWS // 2)

    own_start = (c * Y + y) * OWN

    def mine(k):
        return pl.ds(pl.multiple_of(k * ROWS + own_start, OWN), OWN)

    def y_peer(j):
        return (c, xh * Y + lax.rem(y + j, Y), d)

    def reduce_start(ph, k):
        remote(
            part.at[ph, side(k, 1 - c)], cbuf.at[ph, k], csend.at[ph], csem.at[ph, k], sib
        )

    def reduce_middle(ph, k):
        await_bytes(cbuf.at[ph, k], csem.at[ph, k])
        psum[ph, k] = (part[ph, side(k, c)].astype(F32) + cbuf[ph, k].astype(F32)).astype(BF16)
        for j in range(1, Y):
            rows = pl.ds(pl.multiple_of(lax.rem(y + j, Y) * OWN, OWN), OWN)
            remote(
                psum.at[ph, k, rows], rs.at[ph, k, j - 1], rsend.at[ph], rsem.at[ph, k], y_peer(j)
            )

    def reduce_finish(ph, k):
        await_bytes(rs.at[ph, k], rsem.at[ph, k])
        rows = pl.ds(pl.multiple_of(y * OWN, OWN), OWN)
        total = psum[ph, k, rows].astype(F32)
        for j in range(Y - 1):
            total = total + rs[ph, k, j].astype(F32)
        return total

    def gather_start(which, buf, layer, k):
        for j in range(1, Y):
            view = buf.at[layer, mine(k)]
            remote(view, view, gsend.at[which, layer], gsem.at[which, layer, k], y_peer(j))

    def gather_middle(which, buf, layer, k):
        await_bytes(buf.at[layer, pl.ds(0, (Y - 1) * OWN)], gsem.at[which, layer, k])
        view = buf.at[layer, side(k, c)]
        remote(view, view, hsend.at[which, layer], hsem.at[which, layer, k], sib)

    def gather_finish(which, buf, layer, k):
        await_bytes(buf.at[layer, side(k, 1 - c)], hsem.at[which, layer, k])

    def emit(kind, layer, k, rows):
        low = rows.astype(BF16)
        for j in range(T):
            ostage[kind, layer, k, j] = low[:, j * 128 : (j + 1) * 128]
        first = xh * (chunks * ROWS) + k * ROWS + own_start
        target = pl.ds(pl.multiple_of(first, OWN), OWN)

        def away(j):
            other = lax.rem(t + j, T)
            remote(
                ostage.at[kind, layer, k, other],
                obuf.at[kind, target],
                osend.at[kind, layer],
                osem.at[kind],
                (layer, other, d),
            )

        for j in range(1, T):
            away(j)

        @pl.when(c == layer)
        def _():
            pltpu.make_async_copy(
                ostage.at[kind, layer, k, t], obuf.at[kind, target], osem.at[kind]
            ).start()

        @pl.when(c != layer)
        def _():
            away(0)

    slot = xh * 2 + xl

    def x_send(m, layer, source):
        for to in range(2):
            self_ = jnp.logical_and(jnp.logical_and(c == layer, native), xl == to)
            src, dst = source(to), xrs[m].at[slot]

            @pl.when(self_)
            def _():
                pltpu.make_async_copy(src, dst, xsem.at[m]).start()

            @pl.when(jnp.logical_not(self_))
            def _():
                remote(
                    src, dst, xsend.at[m, layer], xsem.at[m], (layer, c * Y + y, to * nz + z)
                )

    def z_peer(j):
        return (c, t, xl * nz + lax.rem(z + j, nz))

    def z_first_start(m, layer):
        for j in range(1, nz):
            for to in range(2):
                remote(
                    gbufs[m].at[layer, to * nz + lax.rem(z + j, nz)],
                    zrs[m].at[layer, j - 1, to],
                    zsend.at[m, layer],
                    zsem.at[m, layer],
                    z_peer(j),
                )

    def z_first_middle(m, layer):
        if nz > 1:
            await_bytes(zrs[m].at[layer], zsem.at[m, layer])
        for to in range(2):
            total = gbufs[m][layer, to * nz + z].astype(F32)
            for j in range(nz - 1):
                total = total + zrs[m][layer, j, to].astype(F32)
            zsums[m][layer, to] = total.astype(BF16)
        x_send(m, layer, lambda to: zsums[m].at[layer, to])

    def z_first_finish(m):
        await_bytes(xrs[m], xsem.at[m])
        return sum4(m)

    def sum4(m):
        total = xrs[m][0].astype(F32)
        for j in range(1, 4):
            total = total + xrs[m][j].astype(F32)
        return total

    def x_first_start(m, layer):
        x_send(m, layer, lambda to: gbufs[m].at[layer, pl.ds(to * nz, nz)])

    def x_first_middle(m):
        await_bytes(xrs[m], xsem.at[m])
        zsums[m][...] = sum4(m).astype(BF16)
        for j in range(1, nz):
            remote(
                zsums[m].at[lax.rem(z + j, nz)],
                zrs[m].at[j - 1],
                zsend.at[m, 0],
                zsem.at[m, 0],
                z_peer(j),
            )

    def x_first_finish(m):
        total = zsums[m][z].astype(F32)
        if nz > 1:
            await_bytes(zrs[m], zsem.at[m, 0])
        for j in range(nz - 1):
            total = total + zrs[m][j].astype(F32)
        return total

    left_half = lax.broadcasted_iota(jnp.int32, (ROWS, 128), 1) < HD

    def heads(value):
        zero = jnp.zeros_like(value)
        return jnp.where(left_half, value, zero), jnp.where(left_half, zero, value)

    def each(count, body):
        def step(i, carry):
            body(i)
            return carry

        lax.fori_loop(0, count, step, 0)

    @pl.when(native)
    def _():
        pltpu.make_async_copy(vec_in, vec.at[c], vsem.at[c]).start()

    @pl.when(jnp.logical_not(native))
    def _():
        remote(vec_in, vec.at[c], vsend.at[0], vsem.at[c], home)

    remote(vec_in, vec.at[c], vsend.at[0], vsem.at[c], partner)

    @pl.when(c == 0)
    def _():
        send_weight(0)
        send_weight(1)

    gpack[...] = jnp.zeros_like(gpack)
    x_copy.wait()
    ct_copy.wait()
    await_bytes(vec.at[0], vsem.at[0])
    await_bytes(vec.at[1], vsem.at[1])
    lanes = lax.broadcasted_iota(jnp.int32, (ROWS, ROWS), 1)
    places = lax.broadcasted_iota(jnp.int32, (ROWS, ROWS), 0)

    def start(k):
        unit, _ = standardize(x_ref[span(k)].astype(F32))
        n1[0, span(k)] = (unit * vec[0, 0:1] + vec[0, 2:3]).astype(BF16)
        hrow[0, k] = x_ref[mine(k)].astype(F32)
        segment = docs_ref[pl.ds(xh * chunks + k, 1)].astype(F32)
        segment = jnp.broadcast_to(segment, (ROWS, ROWS))
        visible = jnp.logical_and(lanes <= places, segment == segment.T)
        mask_ref[span(k)] = jnp.where(visible, 1.0, 0.0)

    each(chunks, start)

    relay(0, 0)
    relay(1, 0)

    @pl.when(c == 0)
    def _():
        weight_left(0)
        send_weight(2)

    need(0, 0)
    need(1, 0)

    @pl.when(c == 0)
    def _():
        send_weight(3)

    def attention(layer, k):
        ph = layer * 2

        @pl.when(layer == 1)
        def _():
            gather_finish(0, n1, 1, k)

        packed = mm(n1[layer, span(k)], wqkv[layer]) + vec[layer, 6:7, 0:384]
        packed = packed.astype(BF16)
        qkv[layer, span(k)] = packed
        queries, keys, values = packed[:, 0:128], packed[:, 128:256], packed[:, 256:384]
        visible = mask_ref[span(k)] > 0
        parts = []
        for head, query in enumerate(heads(queries)):
            scores = jnp.where(visible, mm_nt(query, keys) * SCALE, -1e30)
            weights_ = jnp.exp(scores - jnp.max(scores, -1, keepdims=True))
            p = weights_ / jnp.sum(weights_, -1, keepdims=True)
            prob[layer, k, head] = p
            parts.append(mm(p.astype(BF16), values))
        mixture = jnp.where(left_half, parts[0], parts[1]).astype(BF16)
        mix[layer, span(k)] = mixture
        part[ph, span(k)] = mm(mixture, wout[layer]).astype(BF16)
        reduce_start(ph, k)

    def second_norm(layer, k):
        rows = hrow[layer, k] + reduce_finish(layer * 2, k) + vec[layer, 3:4]
        mrow[layer, k] = rows
        unit, _ = standardize(rows)
        n2[layer, mine(k)] = (unit * vec[layer, 1:2] + vec[layer, 4:5]).astype(BF16)
        gather_start(1, n2, layer, k)

    def feed(layer, k):
        ph = layer * 2 + 1
        gather_finish(1, n2, layer, k)
        u = mm(n2[layer, span(k)], w1[layer]) + vec[layer, 7:8, 0:512]
        up[layer, span(k)] = u
        g = 0.5 * u * (1.0 + jnp.tanh(GELU_C * (u + GELU_A * (u * u * u))))
        g = g.astype(BF16)
        act[layer, span(k)] = g
        part[ph, span(k)] = mm(g, w2[layer]).astype(BF16)
        reduce_start(ph, k)

    def finish(layer, k):
        rows = mrow[layer, k] + reduce_finish(layer * 2 + 1, k) + vec[layer, 5:6]

        @pl.when(layer == 0)
        def _():
            entering = rows.astype(BF16).astype(F32)
            hrow[1, k] = entering
            unit, _ = standardize(entering)
            n1[1, mine(k)] = (unit * vec[1, 0:1] + vec[1, 2:3]).astype(BF16)
            gather_start(0, n1, 1, k)

        emit(0, layer, k, rows)

    def feed_back(layer, k):
        ph = 6 - layer * 2

        @pl.when(layer == 0)
        def _():
            gather_finish(3, dyr, 0, k)

        grad = mm_nt(dyr[layer, span(k)], w2[layer])
        u = up[layer, span(k)]
        bend = jnp.tanh(GELU_C * (u + GELU_A * (u * u * u)))
        slope = 0.5 * (1.0 + bend) + (0.5 * u) * (1.0 - bend * bend) * (
            GELU_C * (1.0 + (3.0 * GELU_A) * (u * u))
        )
        du = (grad * slope).astype(BF16)
        dup[span(k)] = du
        part[ph, span(k)] = mm_nt(du, w1[layer]).astype(BF16)
        reduce_start(ph, k)
        gpack[layer, 6:7, 384:896] += jnp.sum(du.astype(F32), 0, keepdims=True)

    def middle(layer, k):
        grad = dyr[layer, mine(k)].astype(F32)
        slope, gain_grad, shift_grad = norm_back(
            mrow[layer, k], vec[layer, 1:2], reduce_finish(6 - layer * 2, k)
        )
        dm = grad + slope
        mrow[layer, k] = dm
        low = dm.astype(BF16)
        dmr[layer, mine(k)] = low
        gather_start(2, dmr, layer, k)
        gpack[layer, 1:2] += gain_grad
        gpack[layer, 3:4] += jnp.sum(low.astype(F32), 0, keepdims=True)
        gpack[layer, 4:5] += shift_grad
        gpack[layer, 5:6] += jnp.sum(grad, 0, keepdims=True)

    def attention_back(layer, k):
        ph = 7 - layer * 2
        gather_finish(2, dmr, layer, k)
        da = mm_nt(dmr[layer, span(k)], wout[layer]).astype(BF16)
        packed = qkv[layer, span(k)]
        queries, keys, values = packed[:, 0:128], packed[:, 128:256], packed[:, 256:384]
        dqs, dks, dvs = [], [], []
        for head, grad in enumerate(heads(da)):
            p = prob[layer, k, head]
            dvs.append(mm_tn(p.astype(BF16), da))
            dp = mm_nt(grad, values)
            ds = p * (dp - jnp.sum(p * dp, -1, keepdims=True))
            ds = ds.astype(BF16)
            dqs.append(mm(ds, keys))
            dks.append(mm_tn(ds, queries))
        grads = jnp.concatenate(
            [
                jnp.where(left_half, dqs[0], dqs[1]) * SCALE,
                jnp.where(left_half, dks[0], dks[1]) * SCALE,
                jnp.where(left_half, dvs[0], dvs[1]),
            ],
            1,
        ).astype(BF16)
        dqkv[span(k)] = grads
        part[ph, span(k)] = mm_nt(grads, wqkv[layer]).astype(BF16)
        reduce_start(ph, k)
        gpack[layer, 6:7, 0:384] += jnp.sum(grads.astype(F32), 0, keepdims=True)

    def last(layer, k):
        slope, gain_grad, shift_grad = norm_back(
            hrow[layer, k], vec[layer, 0:1], reduce_finish(7 - layer * 2, k)
        )
        rows = mrow[layer, k] + slope

        @pl.when(layer == 1)
        def _():
            dyr[0, mine(k)] = rows.astype(BF16)
            gather_start(3, dyr, 0, k)

        emit(1, layer, k, rows)
        gpack[layer, 0:1] += gain_grad
        gpack[layer, 2:3] += shift_grad

    pieces = 2 * nz
    wide = D // pieces

    def grad_down(layer, b):
        cols = pl.ds(pl.multiple_of(b * 128, 128), 128)
        block = mm_tn(act[layer, :, cols], dyr[layer]).astype(BF16)
        for q in range(pieces):
            gbufs[0][layer, q, cols] = block[:, q * wide : (q + 1) * wide]

    up_wide = max(256 // wide, 1)
    up_steps = pieces // up_wide

    def grad_up(layer, b):
        size = wide * up_wide
        cols = pl.ds(pl.multiple_of(b * size, size), size)
        block = mm_tn(n2[layer, :, cols], dup[...]).astype(BF16)
        for q in range(up_wide):
            gbufs[1][layer, b * up_wide + q] = block[q * wide : (q + 1) * wide]

    def grad_out(layer):
        block = mm_tn(mix[layer], dmr[layer]).astype(BF16)
        for q in range(pieces):
            gbufs[4][layer, q] = block[:, q * wide : (q + 1) * wide]

    def grad_qkv(layer, b):
        size = wide * up_wide
        cols = pl.ds(pl.multiple_of(b * size, size), size)
        block = mm_tn(n1[layer, :, cols], dqkv[...]).astype(BF16)
        for q in range(up_wide):
            rows = slice(q * wide, (q + 1) * wide)
            gbufs[2][layer, b * up_wide + q] = block[rows, 0:256]
            gbufs[3][layer, b * up_wide + q] = block[rows, 256:384]

    def small_start(layer):
        for j in range(T):
            sstage[layer, j] = gpack[layer, :, j * 128 : (j + 1) * 128]
            sbias[layer, j : j + 1] = gpack[layer, 6:7, j * 128 : (j + 1) * 128]

        def send(src, dst, to, self_):
            @pl.when(self_)
            def _():
                pltpu.make_async_copy(src, dst, ssem.at[0]).start()

            @pl.when(jnp.logical_not(self_))
            def _():
                remote(src, dst, ssend.at[layer], ssem.at[0], (layer, to, d))

        for j in range(T):
            to = lax.rem(t + j, T)
            src, dst = sstage.at[layer, to], sgot.at[c * T + t]
            if j:
                remote(src, dst, ssend.at[layer], ssem.at[0], (layer, to, d))
            else:
                send(src, dst, to, c == layer)
        send(
            sbias.at[layer],
            sgot.at[2 * T + xh],
            c * Y + y,
            jnp.logical_and(c == layer, native),
        )

    def small_middle():
        await_bytes(sgot, ssem.at[0])
        total = sgot[0]
        for j in range(1, 2 * T):
            total = total + sgot[j]
        ssum[0] = total
        ssum[1] = sgot[2 * T] + sgot[2 * T + 1]
        for j in range(1, 2 * nz):
            to = lax.rem(d + j, 2 * nz)
            remote(ssum, sall.at[j - 1], ssend.at[2], ssem.at[1], (c, t, to))

    def small_finish():
        await_bytes(sall, ssem.at[1])
        total = ssum[...]
        for j in range(2 * nz - 1):
            total = total + sall[j]
        return total

    def collect_attention(layer):
        z_first_middle(2, layer)

        @pl.when(c == layer)
        def _():
            x_first_middle(3)
            x_first_middle(4)
            small_middle()

    def collect_feed(layer):
        z_first_middle(0, layer)

        @pl.when(c == layer)
        def _():
            x_first_middle(1)

    def on(condition, body, *args):
        @pl.when(condition)
        def _():
            body(*args)

    def stage_body(stage):
        odd = lax.rem(stage, 2)
        ahead = stage < 4
        layer = jnp.where(ahead, stage // 2, 3 - stage // 2)
        front_even = jnp.logical_and(ahead, odd == 0)
        front_odd = jnp.logical_and(ahead, odd == 1)
        back_even = jnp.logical_and(stage >= 4, odd == 0)
        back_odd = jnp.logical_and(stage >= 4, odd == 1)

        @pl.when(stage == 1)
        def _():
            need(2, 0)
            need(3, 0)

        @pl.when(stage == 2)
        def _():
            need(0, 1)
            need(1, 1)

        @pl.when(stage == 3)
        def _():
            need(2, 1)
            need(3, 1)

        def step(s):
            @pl.when(s < chunks)
            def _():
                on(front_odd, gather_middle, 1, n2, layer, s)
                on(stage == 2, gather_middle, 0, n1, 1, s)
                on(back_odd, gather_middle, 2, dmr, layer, s)
                on(stage == 6, gather_middle, 3, dyr, 0, s)

            @pl.when(jnp.logical_and(s >= 1, s < chunks + 1))
            def _():
                on(front_even, attention, layer, s - 1)
                on(front_odd, feed, layer, s - 1)
                on(back_even, feed_back, layer, s - 1)
                on(back_odd, attention_back, layer, s - 1)

            @pl.when(s >= 2)
            def _():
                reduce_middle(stage, s - 2)

            @pl.when(s == 2)
            def _():
                on(stage == 0, relay, 2, 0)
                on(stage == 2, relay, 2, 1)

        each(chunks + 2, step)

        @pl.when(stage == 0)
        def _():
            relay(3, 0)

            @pl.when(c == 1)
            def _():
                send_weight(0)
                send_weight(1)

        @pl.when(stage == 1)
        def _():
            relay(0, 1)
            relay(1, 1)

            @pl.when(c == 1)
            def _():
                send_weight(3)

        @pl.when(stage == 2)
        def _():
            relay(3, 1)

        @pl.when(stage == 4)
        def _():
            each(chunks, lambda k: finish(1, k))

        @pl.when(back_even)
        def _():
            each(4, lambda b: grad_down(layer, b))
            z_first_start(0, layer)

        @pl.when(back_odd)
        def _():
            grad_out(layer)
            x_first_start(4, layer)
            each(up_steps, lambda b: grad_qkv(layer, b))
            z_first_start(2, layer)
            x_first_start(3, layer)

        def settle(k):
            on(front_even, second_norm, layer, k)
            on(stage == 1, finish, 0, k)
            on(back_even, middle, layer, k)
            on(back_odd, last, layer, k)

        on(stage != 3, each, chunks, settle)

        @pl.when(jnp.logical_and(stage == 0, c == 1))
        def _():
            send_weight(2)

        @pl.when(back_even)
        def _():
            each(up_steps, lambda b: grad_up(layer, b))
            x_first_start(1, layer)

        on(back_odd, small_start, layer)
        on(stage == 5, collect_feed, 1)
        on(stage == 6, collect_attention, 1)

    each(8, stage_body)
    collect_feed(0)
    collect_attention(0)

    places_ = layout(nz)

    def put(name, value, start=0):
        rows = value.shape[0]
        first = places_[name] + start * rows
        for j in range(value.shape[1] // 128):
            grads_ref[first + j * rows : first + (j + 1) * rows] = value[:, j * 128 : (j + 1) * 128]

    put("down", z_first_finish(0))
    put("up", x_first_finish(1))
    put("qkv", z_first_finish(2))
    put("qkv", x_first_finish(3), 2)
    put("out", x_first_finish(4))
    small = small_finish()
    put("small", small[0])
    put("bias", small[1])
    for kind in range(2):
        await_bytes(obuf.at[kind], osem.at[kind])
    rows_ref[...] = obuf[...]

    for i in range(4):
        both = weights[i][1]

        @pl.when(jnp.logical_not(native))
        def _():
            await_bytes(both.at[0], whome.at[i])
            for layer in range(2):
                await_bytes(whole_half(i), wrelay.at[i, layer])

        if i:
            weight_left(i)

    @pl.when(c == 1)
    def _():
        weight_left(0)

    @pl.when(jnp.logical_not(native))
    def _():
        await_bytes(vec.at[0], vsend.at[0])

    await_bytes(vec.at[0], vsend.at[0])
    for ph in range(8):
        await_bytes(cbuf.at[ph], csend.at[ph])
        await_bytes(rs.at[ph], rsend.at[ph])
    for which, layer in ((0, 1), (1, 0), (1, 1), (2, 0), (2, 1), (3, 0)):
        await_bytes(rs.at[0], gsend.at[which, layer])
        await_bytes(cbuf.at[0], hsend.at[which, layer])
    for layer in range(2):
        for kind in range(2):

            @pl.when(c == layer)
            def _():
                view = ostage.at[kind, layer, :, pl.ds(0, T - 1)]
                await_bytes(view, osend.at[kind, layer])

            @pl.when(c != layer)
            def _():
                await_bytes(ostage.at[kind, layer], osend.at[kind, layer])

        self_ = jnp.logical_and(c == layer, native)
        for m in range(5):
            if nz > 1 and m in (0, 2):
                await_bytes(zrs[m].at[layer], zsend.at[m, layer])
            await_bytes(xrs[m].at[0], xsend.at[m, layer])

            @pl.when(jnp.logical_not(self_))
            def _():
                await_bytes(xrs[m].at[0], xsend.at[m, layer])

        await_bytes(sgot.at[pl.ds(0, T - 1)], ssend.at[layer])

        @pl.when(c != layer)
        def _():
            await_bytes(sgot.at[0], ssend.at[layer])

        @pl.when(jnp.logical_not(self_))
        def _():
            await_bytes(sgot.at[0], ssend.at[layer])

    if nz > 1:
        for m in (1, 3, 4):
            await_bytes(zrs[m], zsend.at[m, 0])
    await_bytes(sall, ssend.at[2])


def layout(nz):
    wide = D // (2 * nz)
    sizes = (
        ("qkv", 3 * wide),
        ("up", 4 * wide),
        ("down", 4 * wide),
        ("out", wide),
        ("small", 8),
        ("bias", 8),
    )
    places, first = {}, 0
    for name, size in sizes:
        places[name] = first
        first += size
    places["end"] = first
    return places


def core(chunks, nz, x, ct, docs, wqkv, wout, w1, w2, qb, b1, gains, shifts):
    n = chunks * ROWS
    vm = pl.BlockSpec(memory_space=pltpu.VMEM)
    hbm = pl.BlockSpec(memory_space=pl.ANY)
    pieces = 2 * nz
    wide = D // pieces
    out_shape = (
        jax.ShapeDtypeStruct((2, 2 * n, 128), BF16),
        jax.ShapeDtypeStruct((layout(nz)["end"], 128), F32),
    )
    dma = pltpu.SemaphoreType.DMA
    shape = ((512, wide), (wide, 512), (wide, 256), (wide, 128), (128, wide))
    back = max(nz - 1, 1)
    gbufs = [pltpu.VMEM((2, pieces) + s, BF16) for s in shape]
    zrs, zsums, xrs = [], [], []
    for m, s in enumerate(shape):
        if m in (0, 2):
            zrs.append(pltpu.VMEM((2, back, 2) + s, BF16))
            zsums.append(pltpu.VMEM((2, 2) + s, BF16))
            xrs.append(pltpu.VMEM((4,) + s, BF16))
        else:
            zrs.append(pltpu.VMEM((back,) + s, BF16))
            zsums.append(pltpu.VMEM((nz,) + s, BF16))
            xrs.append(pltpu.VMEM((4, nz) + s, BF16))
    scratch = [
        pltpu.VMEM((n, D), BF16),
        pltpu.VMEM((n, ROWS), F32),
        pltpu.VMEM((8, D), F32),
        pltpu.VMEM((2, D, 384), BF16),
        pltpu.VMEM((2, 128, D), BF16),
        pltpu.VMEM((2, D, 512), BF16),
        pltpu.VMEM((2, 512, D), BF16),
        pltpu.VMEM((2, 8, D), F32),
        pltpu.VMEM((2, n, D), BF16),
        pltpu.VMEM((2, n, D), BF16),
        pltpu.VMEM((2, n, D), BF16),
        pltpu.VMEM((2, n, D), BF16),
        pltpu.VMEM((2, n, 384), BF16),
        pltpu.VMEM((2, n, 128), BF16),
        pltpu.VMEM((2, chunks, 2, ROWS, ROWS), F32),
        pltpu.VMEM((2, n, 512), F32),
        pltpu.VMEM((2, n, 512), BF16),
        pltpu.VMEM((n, 512), BF16),
        pltpu.VMEM((n, 384), BF16),
        pltpu.VMEM((2, chunks, OWN, D), F32),
        pltpu.VMEM((2, chunks, OWN, D), F32),
        pltpu.VMEM((8, n, D), BF16),
        pltpu.VMEM((8, chunks, ROWS // 2, D), BF16),
        pltpu.VMEM((8, chunks, ROWS // 2, D), BF16),
        pltpu.VMEM((8, chunks, Y - 1, OWN, D), BF16),
        pltpu.VMEM((2, 2, chunks, T, OWN, 128), BF16),
        pltpu.VMEM((2, 2 * n, 128), BF16),
        gbufs,
        zrs,
        zsums,
        xrs,
        pltpu.VMEM((2, 8, D), F32),
        pltpu.VMEM((2, T, 8, 128), F32),
        pltpu.VMEM((2, 8, 128), F32),
        pltpu.VMEM((2 * T + 2, 8, 128), F32),
        pltpu.VMEM((2, 8, 128), F32),
        pltpu.VMEM((pieces - 1, 2, 8, 128), F32),
        dma((2,)),
        dma((4, 2, 2, PARTS)),
        dma((4,)),
        dma((4,)),
        dma((4, 2)),
        dma((2,)),
        dma((1,)),
        dma((8, chunks)),
        dma((8,)),
        dma((8, chunks)),
        dma((8,)),
        dma((4, 2, chunks)),
        dma((4, 2)),
        dma((4, 2, chunks)),
        dma((4, 2)),
        dma((2,)),
        dma((2, 2)),
        dma((5, 2)),
        dma((5, 2)),
        dma((5,)),
        dma((5, 2)),
        dma((2,)),
        dma((3,)),
    ]
    return pl.pallas_call(
        functools.partial(kernel, chunks, nz),
        out_shape=out_shape,
        in_specs=[hbm, hbm, vm, hbm, hbm, hbm, hbm, vm, vm, vm, vm],
        out_specs=[vm] * 2,
        scratch_shapes=scratch,
        compiler_params=pltpu.CompilerParams(
            collective_id=0, has_side_effects=True, vmem_limit_bytes=62 * 2**20
        ),
        name="layers",
    )(x, ct, docs, wqkv, wout, w1, w2, qb, b1, gains, shifts)


def closing(
    m,
    rows,
    grads,
    sec_out,
    ing_out,
    gqkv_out,
    qb_out,
    gout_out,
    g1_out,
    b1_out,
    g2_out,
    gains_out,
    shifts_out,
):
    d = lax.axis_index("dp")
    sec_out[0] = rows[0].astype(F32)
    ing_out[0] = rows[1].astype(F32)
    places = layout(m // 2)
    width = D // m

    def get(name, height, j):
        first = places[name] + j * height
        return grads[first : first + height]

    for j in range(3):
        gqkv_out[0, :, j, :] = get("qkv", width, j)
    for j in range(4):
        g1_out[0, :, j * 128 : (j + 1) * 128] = get("up", width, j)
    for j in range(width // 128):
        gout_out[0, :, j * 128 : (j + 1) * 128] = get("out", 128, j)
        g2_out[0, :, j * 128 : (j + 1) * 128] = get("down", 512, j)
    share = 128 // m
    shift = lax.rem(128 - d * share, 128)
    rolled = pltpu.roll(get("small", 8, 0), shift, 1)
    gains_out[0] = rolled[0:2, 0:share]
    shifts_out[0] = rolled[2:6, 0:share]
    bias = get("bias", 8, 0)
    rolled = pltpu.roll(bias, shift, 1)
    for j in range(2):
        qb_out[0, j : j + 1] = rolled[2 * j : 2 * j + 1, 0:share]
    lines = lax.broadcasted_iota(jnp.int32, (8, 128), 0)

    def line(block, which):
        return jnp.sum(jnp.where(lines == which, block, 0.0), 0, keepdims=True)

    wide = 512 // m
    if wide >= 128:
        for j in range(wide // 128):
            b1_out[:, j * 128 : (j + 1) * 128] = line(bias, 3 + d * (wide // 128) + j)
    else:
        per = 128 // wide
        rolled = pltpu.roll(bias, lax.rem(128 - lax.rem(d, per) * wide, 128), 1)
        b1_out[...] = line(rolled, 3 + d // per)[:, 0:wide]


def shards(
    inputs,
    cotangent,
    doc_ids,
    qkv_weight,
    qkv_bias,
    out_weight,
    fc1_weight,
    fc1_bias,
    fc2_weight,
    norm_gains,
    shifts,
):
    m = lax.axis_size("dp")
    chunks = doc_ids.shape[0] // 2
    n = chunks * ROWS
    results = core(
        chunks,
        m // 2,
        inputs,
        cotangent,
        doc_ids,
        qkv_weight[0].reshape(D, 384),
        out_weight[0],
        fc1_weight[0],
        fc2_weight[0],
        qkv_bias,
        fc1_bias,
        norm_gains,
        shifts,
    )
    vm = pl.BlockSpec(memory_space=pltpu.VMEM)
    shapes = (
        (1, 2 * n, 128),
        (1, 2 * n, 128),
        (1, D // m, 3, 128),
        (1, 2, 128 // m),
        (1, 128, D // m),
        (1, D // m, 512),
        (1, 512 // m),
        (1, 512, D // m),
        (1, 2, 128 // m),
        (1, 4, 128 // m),
    )
    return pl.pallas_call(
        functools.partial(closing, m),
        out_shape=[jax.ShapeDtypeStruct(shape, F32) for shape in shapes],
        in_specs=[vm] * 2,
        out_specs=[vm] * 10,
        compiler_params=pltpu.CompilerParams(vmem_limit_bytes=48 * 2**20),
        name="closing",
    )(*results)


def solution(mesh):
    return jax.shard_map(
        shards,
        mesh=mesh,
        in_specs=(
            P("dp", None),
            P("dp", None),
            P("dp", None),
            P("pipe", None, None, "tensor"),
            P("pipe", None, "tensor"),
            P("pipe", "tensor", None),
            P("pipe", None, "tensor"),
            P("pipe", "tensor"),
            P("pipe", "tensor", None),
            P("pipe", None, None),
            P("pipe", None, None),
        ),
        out_specs=(
            P("pipe", "dp", "tensor"),
            P("pipe", "dp", "tensor"),
            P("pipe", "dp", None, "tensor"),
            P("pipe", None, ("tensor", "dp")),
            P("pipe", "tensor", "dp"),
            P("pipe", "dp", "tensor"),
            P("pipe", ("tensor", "dp")),
            P("pipe", "tensor", "dp"),
            P("pipe", None, ("tensor", "dp")),
            P("pipe", None, ("tensor", "dp")),
        ),
        check_vma=False,
    )
```

time: 168 us -> 151 us (0.90)
  Pallas kernels: 158 us -> 145 us
  local copies, waits for them, and re-layouts: 9.34 us -> 5.39 us
    pallas_call x1, Pallas kernels: 157 us -> 144 us  [core(): pl.pallas_call(functools.partial(kernel, chunks, nz), out_shape=out_shape...]
    unnamed x15 -> x5, local copies, waits for them, and re-layouts: 7.49 us -> 3.53 us
where the time goes in v4:
time: 151 us
  Pallas kernels  145 us (96%)
  local copies, waits for them, and re-layouts  5.39 us (4%)
    pallas_call x1, Pallas kernels, core(): pl.pallas_call(functools.partial(kernel, chunks, nz), out_shape=out_shape...  144 us
    unnamed x5, local copies, waits for them, and re-layouts  3.53 us

profile of v4, /device:TPU:0, one launch (start us, length us, event | category | flops | bytes accessed | tf_op | source)
XLA Modules:
  0.0 151.2 jit_solution(4096448430695887600)
XLA Ops:
  0.6 1.4 copy.23
  2.1 1.2 copy.24.wqkv_in
  3.2 144.0 %layers.1 = (bf16[2,768,128]{2,1,0:T(8,128)(2,1)}, f32[1552,128]{1,0:T(8,128)}) custom-call(bf16[768,1024]{1,0:T(8,128)(2,1)} %x_in.1, bf16[768,1024]{1,0:T(8,128)(2,1)} %ct_in.1, s32[6,128]{1,0:T(8,128)} %docs_ref.1, bf16[1024,384]{1,0:T(8,128)(2,1)} %copy.24.wqkv_in, bf16[128,1024]{1,0:T(8,128)(2,1)} %bitcast.7, bf16[1024,512]{1,0:T(8,128)(2,1)} %bitcast.5, ...), custom_call_target="tpu_custom_call" | custom-call | tf_op jit(solution)/shard_map/layers/pallas_call | solution.py:992
  147.2 0.0 copy-start
  147.2 1.1 copy-done
  148.4 0.0 copy-start.1
  148.4 1.0 copy-done.1
  149.4 1.1 closing.1
  150.5 0.7 copy.25
Async XLA Ops:
  147.2 1.1 copy-start
  148.4 1.0 copy-start.1

commit v5 on v4

--- a/solution.py
+++ b/solution.py
@@ -48,7 +48,7 @@
     slope = root * (
         e - jnp.mean(e, -1, keepdims=True) - unit * jnp.mean(e * unit, -1, keepdims=True)
     )
-    return slope, jnp.sum(grad * unit, 0, keepdims=True), jnp.sum(grad, 0, keepdims=True)
+    return slope, grad * unit
 
 
 def kernel(
@@ -88,6 +88,7 @@
     dqkv,
     hrow,
     mrow,
+    ledger,
     part,
     cbuf,
     psum,
@@ -190,24 +191,30 @@
         size = weights[i][1].shape[1] // (2 * PARTS)
         return pl.ds(pl.multiple_of((which * PARTS + q) * size, size), size)
 
+    def views(i, h, q):
+        own, both = weights[i]
+        piece = half(i, h, q)
+        if i:
+            return [(own.at[piece], both.at[c, piece])]
+        return [
+            (own.at[j, piece], both.at[c, piece, pl.ds(j * 128, 128)]) for j in range(3)
+        ]
+
     def send_weight(i):
-        own, both = weights[i]
         for q in range(PARTS):
-            piece = half(i, xl, q)
-            remote(
-                own.at[piece], both.at[c, piece], wsend.at[i], wsem.at[i, c, xl, q], partner
-            )
+            for src, dst in views(i, xl, q):
+                remote(src, dst, wsend.at[i], wsem.at[i, c, xl, q], partner)
         for h in range(2):
             for q in range(PARTS):
-                src, dst = own.at[half(i, h, q)], both.at[c, half(i, h, q)]
-
-                @pl.when(native)
-                def _():
-                    pltpu.make_async_copy(src, dst, wsem.at[i, c, h, q]).start()
-
-                @pl.when(jnp.logical_not(native))
-                def _():
-                    remote(src, dst, whome.at[i], wsem.at[i, c, h, q], home)
+                for src, dst in views(i, h, q):
+
+                    @pl.when(native)
+                    def _():
+                        pltpu.make_async_copy(src, dst, wsem.at[i, c, h, q]).start()
+
+                    @pl.when(jnp.logical_not(native))
+                    def _():
+                        remote(src, dst, whome.at[i], wsem.at[i, c, h, q], home)
 
     def whole_half(i):
         return weights[i][1].at[0, pl.ds(0, weights[i][1].shape[1] // 2)]
@@ -218,12 +225,12 @@
     def await_half(i, layer, h, q):
         await_bytes(weights[i][1].at[layer, half(i, h, q)], wsem.at[i, layer, h, q])
 
-    def relay(i, layer):
+    def relay(i, layer, parts=tuple(range(PARTS))):
         both = weights[i][1]
 
         @pl.when(jnp.logical_not(native))
         def _():
-            for q in range(PARTS):
+            for q in parts:
                 await_half(i, layer, 1 - xl, q)
                 piece = both.at[layer, half(i, 1 - xl, q)]
                 remote(
@@ -392,6 +399,7 @@
             total = total + zrs[m][j].astype(F32)
         return total
 
+    ones = jnp.ones((8, chunks * ROWS), BF16)
     left_half = lax.broadcasted_iota(jnp.int32, (ROWS, 128), 1) < HD
 
     def heads(value):
@@ -419,40 +427,41 @@
     def _():
         send_weight(0)
         send_weight(1)
+        send_weight(2)
+        send_weight(3)
 
     gpack[...] = jnp.zeros_like(gpack)
+    lanes = lax.broadcasted_iota(jnp.int32, (ROWS, ROWS), 1)
+    places = lax.broadcasted_iota(jnp.int32, (ROWS, ROWS), 0)
+
+    def visibility(k):
+        segment = docs_ref[pl.ds(xh * chunks + k, 1)].astype(F32)
+        segment = jnp.broadcast_to(segment, (ROWS, ROWS))
+        visible = jnp.logical_and(lanes <= places, segment == segment.T)
+        mask_ref[span(k)] = jnp.where(visible, 1.0, 0.0)
+
+    each(chunks, visibility)
     x_copy.wait()
     ct_copy.wait()
-    await_bytes(vec.at[0], vsem.at[0])
-    await_bytes(vec.at[1], vsem.at[1])
-    lanes = lax.broadcasted_iota(jnp.int32, (ROWS, ROWS), 1)
-    places = lax.broadcasted_iota(jnp.int32, (ROWS, ROWS), 0)
 
     def start(k):
         unit, _ = standardize(x_ref[span(k)].astype(F32))
         n1[0, span(k)] = (unit * vec[0, 0:1] + vec[0, 2:3]).astype(BF16)
         hrow[0, k] = x_ref[mine(k)].astype(F32)
-        segment = docs_ref[pl.ds(xh * chunks + k, 1)].astype(F32)
-        segment = jnp.broadcast_to(segment, (ROWS, ROWS))
-        visible = jnp.logical_and(lanes <= places, segment == segment.T)
-        mask_ref[span(k)] = jnp.where(visible, 1.0, 0.0)
-
+
+    await_bytes(vec.at[0], vsem.at[0])
+    await_bytes(vec.at[1], vsem.at[1])
+    relay(0, 0, (0,))
     each(chunks, start)
-
-    relay(0, 0)
+    relay(0, 0, (1,))
     relay(1, 0)
 
     @pl.when(c == 0)
     def _():
         weight_left(0)
-        send_weight(2)
 
     need(0, 0)
     need(1, 0)
-
-    @pl.when(c == 0)
-    def _():
-        send_weight(3)
 
     def attention(layer, k):
         ph = layer * 2
@@ -470,7 +479,7 @@
         for head, query in enumerate(heads(queries)):
             scores = jnp.where(visible, mm_nt(query, keys) * SCALE, -1e30)
             weights_ = jnp.exp(scores - jnp.max(scores, -1, keepdims=True))
-            p = weights_ / jnp.sum(weights_, -1, keepdims=True)
+            p = weights_ * (1.0 / jnp.sum(weights_, -1, keepdims=True))
             prob[layer, k, head] = p
             parts.append(mm(p.astype(BF16), values))
         mixture = jnp.where(left_half, parts[0], parts[1]).astype(BF16)
@@ -507,7 +516,7 @@
             n1[1, mine(k)] = (unit * vec[1, 0:1] + vec[1, 2:3]).astype(BF16)
             gather_start(0, n1, 1, k)
 
-        emit(0, layer, k, rows)
+        ledger[0, k] = rows
 
     def feed_back(layer, k):
         ph = 6 - layer * 2
@@ -526,22 +535,20 @@
         dup[span(k)] = du
         part[ph, span(k)] = mm_nt(du, w1[layer]).astype(BF16)
         reduce_start(ph, k)
-        gpack[layer, 6:7, 384:896] += jnp.sum(du.astype(F32), 0, keepdims=True)
 
     def middle(layer, k):
         grad = dyr[layer, mine(k)].astype(F32)
-        slope, gain_grad, shift_grad = norm_back(
-            mrow[layer, k], vec[layer, 1:2], reduce_finish(6 - layer * 2, k)
-        )
+        inner = reduce_finish(6 - layer * 2, k)
+        slope, product = norm_back(mrow[layer, k], vec[layer, 1:2], inner)
         dm = grad + slope
         mrow[layer, k] = dm
         low = dm.astype(BF16)
         dmr[layer, mine(k)] = low
         gather_start(2, dmr, layer, k)
-        gpack[layer, 1:2] += gain_grad
-        gpack[layer, 3:4] += jnp.sum(low.astype(F32), 0, keepdims=True)
-        gpack[layer, 4:5] += shift_grad
-        gpack[layer, 5:6] += jnp.sum(grad, 0, keepdims=True)
+        ledger[0, k] = product
+        ledger[1, k] = inner
+        ledger[2, k] = low.astype(F32)
+        ledger[3, k] = grad
 
     def attention_back(layer, k):
         ph = 7 - layer * 2
@@ -569,12 +576,16 @@
         dqkv[span(k)] = grads
         part[ph, span(k)] = mm_nt(grads, wqkv[layer]).astype(BF16)
         reduce_start(ph, k)
-        gpack[layer, 6:7, 0:384] += jnp.sum(grads.astype(F32), 0, keepdims=True)
+
+    def column_sum(layer, row, which):
+        total = jnp.sum(ledger[which, 0], 0, keepdims=True)
+        for k in range(1, chunks):
+            total = total + jnp.sum(ledger[which, k], 0, keepdims=True)
+        gpack[layer, row : row + 1] = total
 
     def last(layer, k):
-        slope, gain_grad, shift_grad = norm_back(
-            hrow[layer, k], vec[layer, 0:1], reduce_finish(7 - layer * 2, k)
-        )
+        inner = reduce_finish(7 - layer * 2, k)
+        slope, product = norm_back(hrow[layer, k], vec[layer, 0:1], inner)
         rows = mrow[layer, k] + slope
 
         @pl.when(layer == 1)
@@ -582,9 +593,9 @@
             dyr[0, mine(k)] = rows.astype(BF16)
             gather_start(3, dyr, 0, k)
 
-        emit(1, layer, k, rows)
-        gpack[layer, 0:1] += gain_grad
-        gpack[layer, 2:3] += shift_grad
+        ledger[0, k] = product
+        ledger[1, k] = inner
+        ledger[2, k] = rows
 
     pieces = 2 * nz
     wide = D // pieces
@@ -674,13 +685,6 @@
             x_first_middle(4)
             small_middle()
 
-    def collect_feed(layer):
-        z_first_middle(0, layer)
-
-        @pl.when(c == layer)
-        def _():
-            x_first_middle(1)
-
     def on(condition, body, *args):
         @pl.when(condition)
         def _():
@@ -729,38 +733,32 @@
             def _():
                 reduce_middle(stage, s - 2)
 
-            @pl.when(s == 2)
-            def _():
-                on(stage == 0, relay, 2, 0)
-                on(stage == 2, relay, 2, 1)
+            @pl.when(jnp.logical_and(stage == 0, s == 1))
+            def _():
+                relay(2, 0)
+            @pl.when(jnp.logical_and(stage == 0, s == 3))
+            def _():
+                relay(3, 0)
 
         each(chunks + 2, step)
+        @pl.when(stage == 1)
+        def _():
+            relay(0, 1)
+        @pl.when(stage == 1)
+        def _():
+            relay(1, 1)
 
         @pl.when(stage == 0)
         def _():
-            relay(3, 0)
-
             @pl.when(c == 1)
             def _():
-                send_weight(0)
-                send_weight(1)
-
-        @pl.when(stage == 1)
-        def _():
-            relay(0, 1)
-            relay(1, 1)
-
-            @pl.when(c == 1)
-            def _():
-                send_weight(3)
-
-        @pl.when(stage == 2)
-        def _():
-            relay(3, 1)
+                for i in range(4):
+                    send_weight(i)
 
         @pl.when(stage == 4)
         def _():
             each(chunks, lambda k: finish(1, k))
+            each(chunks, lambda k: emit(0, 1, k, ledger[0, k]))
 
         @pl.when(back_even)
         def _():
@@ -774,6 +772,7 @@
             each(up_steps, lambda b: grad_qkv(layer, b))
             z_first_start(2, layer)
             x_first_start(3, layer)
+            gpack[layer, 6:7, 0:384] = mm(ones, dqkv[...])[0:1]
 
         def settle(k):
             on(front_even, second_norm, layer, k)
@@ -782,22 +781,42 @@
             on(back_odd, last, layer, k)
 
         on(stage != 3, each, chunks, settle)
-
-        @pl.when(jnp.logical_and(stage == 0, c == 1))
-        def _():
-            send_weight(2)
+        @pl.when(stage == 1)
+        def _():
+            relay(2, 1)
+        @pl.when(stage == 1)
+        def _():
+            relay(3, 1)
+
 
         @pl.when(back_even)
         def _():
             each(up_steps, lambda b: grad_up(layer, b))
             x_first_start(1, layer)
-
-        on(back_odd, small_start, layer)
-        on(stage == 5, collect_feed, 1)
+            column_sum(layer, 1, 0)
+            column_sum(layer, 4, 1)
+            column_sum(layer, 3, 2)
+            column_sum(layer, 5, 3)
+            gpack[layer, 6:7, 384:896] = mm(ones, dup[...])[0:1]
+
+        @pl.when(stage == 1)
+        def _():
+            each(chunks, lambda k: emit(0, 0, k, ledger[0, k]))
+
+        @pl.when(back_odd)
+        def _():
+            column_sum(layer, 0, 0)
+            column_sum(layer, 2, 1)
+            small_start(layer)
+            each(chunks, lambda k: emit(1, layer, k, ledger[2, k]))
+
+        on(stage == 5, z_first_middle, 0, layer)
+        on(jnp.logical_and(stage == 5, c == 1), x_first_middle, 1)
         on(stage == 6, collect_attention, 1)
 
     each(8, stage_body)
-    collect_feed(0)
+    z_first_middle(0, 0)
+    on(c == 0, x_first_middle, 1)
     collect_attention(0)
 
     places_ = layout(nz)
@@ -810,12 +829,12 @@
 
     put("down", z_first_finish(0))
     put("up", x_first_finish(1))
-    put("qkv", z_first_finish(2))
-    put("qkv", x_first_finish(3), 2)
-    put("out", x_first_finish(4))
     small = small_finish()
     put("small", small[0])
     put("bias", small[1])
+    put("qkv", x_first_finish(3), 2)
+    put("out", x_first_finish(4))
+    put("qkv", z_first_finish(2))
     for kind in range(2):
         await_bytes(obuf.at[kind], osem.at[kind])
     rows_ref[...] = obuf[...]
@@ -949,6 +968,7 @@
         pltpu.VMEM((n, 384), BF16),
         pltpu.VMEM((2, chunks, OWN, D), F32),
         pltpu.VMEM((2, chunks, OWN, D), F32),
+        pltpu.VMEM((4, chunks, OWN, D), F32),
         pltpu.VMEM((8, n, D), BF16),
         pltpu.VMEM((8, chunks, ROWS // 2, D), BF16),
         pltpu.VMEM((8, chunks, ROWS // 2, D), BF16),
@@ -1004,8 +1024,8 @@
 
 def closing(
     m,
-    rows,
-    grads,
+    rows_in,
+    grads_in,
     sec_out,
     ing_out,
     gqkv_out,
@@ -1016,10 +1036,19 @@
     g2_out,
     gains_out,
     shifts_out,
+    rows,
+    grads,
+    sems,
 ):
     d = lax.axis_index("dp")
+    rows_copy = pltpu.make_async_copy(rows_in, rows, sems.at[0])
+    grads_copy = pltpu.make_async_copy(grads_in, grads, sems.at[1])
+    rows_copy.start()
+    grads_copy.start()
+    rows_copy.wait()
     sec_out[0] = rows[0].astype(F32)
     ing_out[0] = rows[1].astype(F32)
+    grads_copy.wait()
     places = layout(m // 2)
     width = D // m
 
@@ -1028,7 +1057,7 @@
         return grads[first : first + height]
 
     for j in range(3):
-        gqkv_out[0, :, j, :] = get("qkv", width, j)
+        gqkv_out[0, j] = get("qkv", width, j)
     for j in range(4):
         g1_out[0, :, j * 128 : (j + 1) * 128] = get("up", width, j)
     for j in range(width // 128):
@@ -1080,7 +1109,7 @@
         inputs,
         cotangent,
         doc_ids,
-        qkv_weight[0].reshape(D, 384),
+        qkv_weight[0].transpose(1, 0, 2),
         out_weight[0],
         fc1_weight[0],
         fc2_weight[0],
@@ -1093,7 +1122,7 @@
     shapes = (
         (1, 2 * n, 128),
         (1, 2 * n, 128),
-        (1, D // m, 3, 128),
+        (1, 3, D // m, 128),
         (1, 2, 128 // m),
         (1, 128, D // m),
         (1, D // m, 512),
@@ -1102,14 +1131,20 @@
         (1, 2, 128 // m),
         (1, 4, 128 // m),
     )
-    return pl.pallas_call(
+    outs = pl.pallas_call(
         functools.partial(closing, m),
         out_shape=[jax.ShapeDtypeStruct(shape, F32) for shape in shapes],
-        in_specs=[vm] * 2,
+        in_specs=[pl.BlockSpec(memory_space=pl.ANY)] * 2,
         out_specs=[vm] * 10,
-        compiler_params=pltpu.CompilerParams(vmem_limit_bytes=48 * 2**20),
+        scratch_shapes=[
+            pltpu.VMEM(results[0].shape, BF16),
+            pltpu.VMEM(results[1].shape, F32),
+            pltpu.SemaphoreType.DMA((2,)),
+        ],
+        compiler_params=pltpu.CompilerParams(vmem_limit_bytes=62 * 2**20),
         name="closing",
     )(*results)
+    return (*outs[:2], outs[2].transpose(0, 2, 1, 3), *outs[3:])
 
 
 def solution(mesh):

time: 151 us -> 140 us (0.927)
  local copies, waits for them, and re-layouts: 5.39 us -> 0 us
  Pallas kernels: 145 us -> 140 us
    pallas_call x1, Pallas kernels: 144 us -> 137 us  [core(): pl.pallas_call(functools.partial(kernel, chunks, nz), out_shape=out_shape...]
    unnamed x5 -> x0, local copies, waits for them, and re-layouts: 3.53 us -> none
where the time goes in v5:
time: 140 us
  Pallas kernels  140 us (100%)
    pallas_call x1, Pallas kernels, core(): pl.pallas_call(functools.partial(kernel, chunks, nz), out_shape=out_shape...  137 us

profile of v5, /device:TPU:0, one launch (start us, length us, event | category | flops | bytes accessed | tf_op | source)
XLA Modules:
  0.0 140.2 jit_solution(13445445575622256884)
XLA Ops:
  0.6 137.1 %layers.1 = (bf16[2,768,128]{2,1,0:T(8,128)(2,1)}, f32[1552,128]{1,0:T(8,128)}) custom-call(bf16[768,1024]{1,0:T(8,128)(2,1)} %x_in.1, bf16[768,1024]{1,0:T(8,128)(2,1)} %ct_in.1, s32[6,128]{1,0:T(8,128)} %docs_ref.1, bf16[3,1024,128]{2,1,0:T(8,128)(2,1)} %bitcast.9, bf16[128,1024]{1,0:T(8,128)(2,1)} %bitcast.10, bf16[1024,512]{1,0:T(8,128)(2,1)} %bitcast.7, ...), custom_call_target="tpu_custom_call" | custom-call | tf_op jit(solution)/shard_map/layers/pallas_call | solution.py:1012
  137.8 2.4 %closing.1 = (f32[1,768,128]{2,1,0:T(8,128)}, f32[1,768,128]{2,1,0:T(8,128)}, f32[1,3,128,128]{3,2,1,0:T(8,128)}, f32[1,2,16]{2,1,0:T(2,128)}, f32[1,128,128]{2,...) custom-call(bf16[2,768,128]{2,1,0:T(8,128)(2,1)} %get-tuple-element., ...), custom_call_target="tpu_custom_call" | custom-call | tf_op jit(solution)/shard_map/closing/pallas_call | solution.py:1134

commit v6 on v5

--- a/solution.py
+++ b/solution.py
@@ -268,7 +268,7 @@
     def reduce_middle(ph, k):
         await_bytes(cbuf.at[ph, k], csem.at[ph, k])
         psum[ph, k] = (part[ph, side(k, c)].astype(F32) + cbuf[ph, k].astype(F32)).astype(BF16)
-        for j in range(1, Y):
+        for j in (2, 1, 3):
             rows = pl.ds(pl.multiple_of(lax.rem(y + j, Y) * OWN, OWN), OWN)
             remote(
                 psum.at[ph, k, rows], rs.at[ph, k, j - 1], rsend.at[ph], rsem.at[ph, k], y_peer(j)
@@ -283,7 +283,7 @@
         return total
 
     def gather_start(which, buf, layer, k):
-        for j in range(1, Y):
+        for j in (2, 1, 3):
             view = buf.at[layer, mine(k)]
             remote(view, view, gsend.at[which, layer], gsem.at[which, layer, k], y_peer(j))
 
@@ -404,7 +404,12 @@
 
     def heads(value):
         zero = jnp.zeros_like(value)
-        return jnp.where(left_half, value, zero), jnp.where(left_half, zero, value)
+        return jnp.concatenate(
+            [jnp.where(left_half, value, zero), jnp.where(left_half, zero, value)], 0
+        )
+
+    def beside(value):
+        return jnp.concatenate([value[0:ROWS], value[ROWS:]], 1)
 
     def each(count, body):
         def step(i, carry):
@@ -475,14 +480,13 @@
         qkv[layer, span(k)] = packed
         queries, keys, values = packed[:, 0:128], packed[:, 128:256], packed[:, 256:384]
         visible = mask_ref[span(k)] > 0
-        parts = []
-        for head, query in enumerate(heads(queries)):
-            scores = jnp.where(visible, mm_nt(query, keys) * SCALE, -1e30)
-            weights_ = jnp.exp(scores - jnp.max(scores, -1, keepdims=True))
-            p = weights_ * (1.0 / jnp.sum(weights_, -1, keepdims=True))
-            prob[layer, k, head] = p
-            parts.append(mm(p.astype(BF16), values))
-        mixture = jnp.where(left_half, parts[0], parts[1]).astype(BF16)
+        visible = jnp.concatenate([visible, visible], 0)
+        scores = mm_nt(heads(queries * SCALE), keys)
+        scores = jnp.where(visible, scores, -1e30)
+        weights_ = jnp.exp(scores - jnp.max(scores, -1, keepdims=True))
+        p = weights_ * (1.0 / jnp.sum(weights_, -1, keepdims=True))
+        prob[layer, k] = p
+        mixture = mm(beside(p.astype(BF16)), heads(values)).astype(BF16)
         mix[layer, span(k)] = mixture
         part[ph, span(k)] = mm(mixture, wout[layer]).astype(BF16)
         reduce_start(ph, k)
@@ -556,23 +560,14 @@
         da = mm_nt(dmr[layer, span(k)], wout[layer]).astype(BF16)
         packed = qkv[layer, span(k)]
         queries, keys, values = packed[:, 0:128], packed[:, 128:256], packed[:, 256:384]
-        dqs, dks, dvs = [], [], []
-        for head, grad in enumerate(heads(da)):
-            p = prob[layer, k, head]
-            dvs.append(mm_tn(p.astype(BF16), da))
-            dp = mm_nt(grad, values)
-            ds = p * (dp - jnp.sum(p * dp, -1, keepdims=True))
-            ds = ds.astype(BF16)
-            dqs.append(mm(ds, keys))
-            dks.append(mm_tn(ds, queries))
-        grads = jnp.concatenate(
-            [
-                jnp.where(left_half, dqs[0], dqs[1]) * SCALE,
-                jnp.where(left_half, dks[0], dks[1]) * SCALE,
-                jnp.where(left_half, dvs[0], dvs[1]),
-            ],
-            1,
-        ).astype(BF16)
+        p = prob[layer, k]
+        outer = heads(da)
+        dv = mm_tn(p.astype(BF16), outer)
+        dp = mm_nt(outer, values)
+        ds = (p * (dp - jnp.sum(p * dp, -1, keepdims=True))).astype(BF16)
+        dq = mm(beside(ds), heads(keys)) * SCALE
+        dk = mm_tn(ds, heads(queries)) * SCALE
+        grads = jnp.concatenate([dq, dk, dv], 1).astype(BF16)
         dqkv[span(k)] = grads
         part[ph, span(k)] = mm_nt(grads, wqkv[layer]).astype(BF16)
         reduce_start(ph, k)
@@ -765,6 +760,11 @@
             each(4, lambda b: grad_down(layer, b))
             z_first_start(0, layer)
 
+            @pl.when(layer == 0)
+            def _():
+                each(up_steps, lambda b: grad_up(layer, b))
+                x_first_start(1, layer)
+
         @pl.when(back_odd)
         def _():
             grad_out(layer)
@@ -791,8 +791,11 @@
 
         @pl.when(back_even)
         def _():
-            each(up_steps, lambda b: grad_up(layer, b))
-            x_first_start(1, layer)
+            @pl.when(layer == 1)
+            def _():
+                each(up_steps, lambda b: grad_up(layer, b))
+                x_first_start(1, layer)
+
             column_sum(layer, 1, 0)
             column_sum(layer, 4, 1)
             column_sum(layer, 3, 2)
@@ -961,7 +964,7 @@
         pltpu.VMEM((2, n, D), BF16),
         pltpu.VMEM((2, n, 384), BF16),
         pltpu.VMEM((2, n, 128), BF16),
-        pltpu.VMEM((2, chunks, 2, ROWS, ROWS), F32),
+        pltpu.VMEM((2, chunks, 2 * ROWS, ROWS), F32),
         pltpu.VMEM((2, n, 512), F32),
         pltpu.VMEM((2, n, 512), BF16),
         pltpu.VMEM((n, 512), BF16),

time: 140 us -> 136 us (0.971)
  Pallas kernels: 140 us -> 135 us
    pallas_call x1, Pallas kernels: 137 us -> 132 us  [core(): pl.pallas_call(functools.partial(kernel, chunks, nz), out_shape=out_shape...]
where the time goes in v6:
time: 136 us; the launch traced here: 135 us
  Pallas kernels  135 us (99%)
    pallas_call x1, Pallas kernels, core(): pl.pallas_call(functools.partial(kernel, chunks, nz), out_shape=out_shape...  132 us

profile of v6, /device:TPU:0, one launch (start us, length us, event | category | flops | bytes accessed | tf_op | source)
XLA Modules:
  0.0 135.4 jit_solution(14597589015255002845)
XLA Ops:
  0.6 132.3 %layers.1 = (bf16[2,768,128]{2,1,0:T(8,128)(2,1)}, f32[1552,128]{1,0:T(8,128)}) custom-call(bf16[768,1024]{1,0:T(8,128)(2,1)} %x_in.1, bf16[768,1024]{1,0:T(8,128)(2,1)} %ct_in.1, s32[6,128]{1,0:T(8,128)} %docs_ref.1, bf16[3,1024,128]{2,1,0:T(8,128)(2,1)} %bitcast.9, bf16[128,1024]{1,0:T(8,128)(2,1)} %bitcast.10, bf16[1024,512]{1,0:T(8,128)(2,1)} %bitcast.7, ...), custom_call_target="tpu_custom_call" | custom-call | tf_op jit(solution)/shard_map/layers/pallas_call | solution.py:1015
  133.0 2.4 %closing.1 = (f32[1,768,128]{2,1,0:T(8,128)}, f32[1,768,128]{2,1,0:T(8,128)}, f32[1,3,128,128]{3,2,1,0:T(8,128)}, f32[1,2,16]{2,1,0:T(2,128)}, f32[1,128,128]{2,...) custom-call(bf16[2,768,128]{2,1,0:T(8,128)(2,1)} %get-tuple-element., ...), custom_call_target="tpu_custom_call" | custom-call | tf_op jit(solution)/shard_map/closing/pallas_call | solution.py:1137

commit v7 on v6

--- a/solution.py
+++ b/solution.py
@@ -734,11 +734,11 @@
             @pl.when(jnp.logical_and(stage == 0, s == 3))
             def _():
                 relay(3, 0)
+            @pl.when(jnp.logical_and(stage == 1, s == 3))
+            def _():
+                relay(0, 1)
 
         each(chunks + 2, step)
-        @pl.when(stage == 1)
-        def _():
-            relay(0, 1)
         @pl.when(stage == 1)
         def _():
             relay(1, 1)

time: 136 us -> 135 us (level)
  no operation moved by 1% of the time
where the time goes in v7:
time: 135 us
  Pallas kernels  134 us (99%)
    pallas_call x1, Pallas kernels, core(): pl.pallas_call(functools.partial(kernel, chunks, nz), out_shape=out_shape...  132 us

profile of v7, /device:TPU:0, one launch (start us, length us, event | category | flops | bytes accessed | tf_op | source)
XLA Modules:
  0.0 134.9 jit_solution(16873354412935620349)
XLA Ops:
  0.6 131.8 %layers.1 = (bf16[2,768,128]{2,1,0:T(8,128)(2,1)}, f32[1552,128]{1,0:T(8,128)}) custom-call(bf16[768,1024]{1,0:T(8,128)(2,1)} %x_in.1, bf16[768,1024]{1,0:T(8,128)(2,1)} %ct_in.1, s32[6,128]{1,0:T(8,128)} %docs_ref.1, bf16[3,1024,128]{2,1,0:T(8,128)(2,1)} %bitcast.9, bf16[128,1024]{1,0:T(8,128)(2,1)} %bitcast.10, bf16[1024,512]{1,0:T(8,128)(2,1)} %bitcast.7, ...), custom_call_target="tpu_custom_call" | custom-call | tf_op jit(solution)/shard_map/layers/pallas_call | solution.py:1015
  132.5 2.4 %closing.1 = (f32[1,768,128]{2,1,0:T(8,128)}, f32[1,768,128]{2,1,0:T(8,128)}, f32[1,3,128,128]{3,2,1,0:T(8,128)}, f32[1,2,16]{2,1,0:T(2,128)}, f32[1,128,128]{2,...) custom-call(bf16[2,768,128]{2,1,0:T(8,128)(2,1)} %get-tuple-element., ...), custom_call_target="tpu_custom_call" | custom-call | tf_op jit(solution)/shard_map/closing/pallas_call | solution.py:1137
